TPU v7x, 32 devices: a whole 2x2x4 slice. The times are simulated.
32 devices in a mesh: sweep: 2 (over x), env: 4 (over y, core), sec: 4 (over z).
Axes of the slice: x: 2, y: 2, z: 4, core: 2. Of those that a mesh axis runs over, the one named last changes fastest.
Arguments:
- corner: bfloat16 [1536, 768], P(('sweep', 'env')), parts along dimension 0, as said below
- edges: bfloat16 [72, 768, 768], P(('sweep', 'sec'), 'env'), parts along dimension 0, as said below
- projectors: bfloat16 [72, 768, 768], P(('sweep', 'sec'), 'env'), parts along dimension 0, as said below
- tile_counts: int32 [72], P(('sweep', 'sec')), parts along dimension 0, may hold values from 1 to 6, as said below
- cotangent: float32 [1536, 768], P(('sweep', 'env'), 'sec'), parts along dimension 0, may hold values from -6 to 6
Outputs:
- corner_new: float32 [1536, 768], P(('sweep', 'env'), 'sec'), parts along dimension 0
- corner_grad: float32 [1536, 768], P(('sweep', 'env'), 'sec'), parts along dimension 0
- edge_grad: float32 [72, 768, 768], P(('sweep', 'sec'), 'env'), parts along dimension 0
- proj_grad: float32 [72, 768, 768], P(('sweep', 'sec'), 'env'), parts along dimension 0
There are 2 independent parts, one for each index of `sweep`. A program takes and returns all parts, laid end to end along the dimension named above; each array names one. Nothing has to cross between parts.
Inputs may be any that keep to these rules, and one draw needn't show every extreme that they name: `tile_counts`: each entry counts live tiles of 128 environment columns of one sector slice; in every draw some slice has all 6 tiles live. `corner`: Real-valued entries. `edges`: Real-valued entries. `projectors`: Real-valued entries.
All inputs are finite; a program needn't handle non-finite values.
Results may differ from a plain program's by a relative error of at most 0.018.
Values may be sent and summed in bfloat16 or wider, within the bound.
No kernel may reach another device: no remote copies, remote signals or barrier semaphores. Data moves between devices by JAX's collectives and lax.ppermute only.
A program may use at most 128 MiB of HBM per device.

v0:
```python
import jax
import jax.numpy as jnp
from jax import lax
from jax.sharding import PartitionSpec as P

CHI = 768
TILE = 128


def per_device(corner, edges, projectors, tile_counts, cotangent):
    slices = edges.shape[0]
    width = corner.shape[1]
    full_edges = lax.all_gather(edges, "env", axis=1, tiled=True)
    columns = lax.broadcasted_iota(jnp.int32, (slices, 1, width), 2)
    keep = columns < (tile_counts * TILE)[:, None, None]
    enlarged = jnp.einsum("ab,kbc->kac", corner, full_edges, preferred_element_type=jnp.float32)
    enlarged = jnp.where(keep, enlarged, 0.0).astype(jnp.bfloat16)
    partial_sum = jnp.einsum(
        "kaz,kac->zc", projectors, enlarged, preferred_element_type=jnp.float32
    )
    by_sector = lax.psum_scatter(
        partial_sum.astype(jnp.bfloat16), "sec", scatter_dimension=1, tiled=True
    )
    absorbed = lax.psum_scatter(by_sector, "env", scatter_dimension=0, tiled=True).astype(
        jnp.float32
    )
    norm_sq = lax.psum(jnp.sum(absorbed * absorbed), ("env", "sec"))
    scale = CHI / jnp.sqrt(norm_sq)
    corner_new = scale * absorbed
    intersection = lax.psum(jnp.sum(cotangent * corner_new), ("env", "sec"))
    absorbed_grad = (scale * (cotangent - corner_new * intersection / (CHI * CHI))).astype(
        jnp.bfloat16
    )
    grad_cols = lax.all_gather(absorbed_grad, "sec", axis=1, tiled=True)
    grad_full = lax.all_gather(grad_cols, "env", axis=0, tiled=True)
    enlarged_grad = jnp.einsum(
        "kaz,zc->kac", projectors, grad_full, preferred_element_type=jnp.float32
    )
    enlarged_grad = jnp.where(keep, enlarged_grad, 0.0).astype(jnp.bfloat16)
    proj_grad = jnp.einsum("kac,zc->kaz", enlarged, grad_full, preferred_element_type=jnp.float32)
    corner_part = jnp.einsum(
        "kac,kbc->ab", enlarged_grad, full_edges, preferred_element_type=jnp.float32
    )
    corner_grad = lax.psum_scatter(
        corner_part.astype(jnp.bfloat16), "sec", scatter_dimension=1, tiled=True
    ).astype(jnp.float32)
    edge_part = jnp.einsum("ab,kac->kbc", corner, enlarged_grad, preferred_element_type=jnp.float32)
    edge_grad = lax.psum_scatter(
        edge_part.astype(jnp.bfloat16), "env", scatter_dimension=1, tiled=True
    ).astype(jnp.float32)
    return (corner_new, corner_grad, edge_grad, proj_grad)


def solution(mesh):
    placed = (
        P(("sweep", "env"), None),
        P(("sweep", "sec"), "env", None),
        P(("sweep", "sec"), "env", None),
        P(("sweep", "sec")),
        P(("sweep", "env"), "sec"),
    )
    return jax.shard_map(
        per_device,
        mesh=mesh,
        in_specs=placed,
        out_specs=(
            P(("sweep", "env"), "sec"),
            P(("sweep", "env"), "sec"),
            P(("sweep", "sec"), "env", None),
            P(("sweep", "sec"), "env", None),
        ),
        check_vma=False,
    )
```

profile of v0, /device:TPU:0, one launch (start us, length us, event | category | flops | bytes accessed | tf_op | source)
XLA Modules:
  0.0 416.5 jit_solution(9792952277197280987)
XLA Ops:
  8.1 75.2 %all-gather.3.cloned.1.call-done = bf16[9,768,768]{2,1,0:T(8,128)(2,1)} async-done(((bf16[9,192,768]{2,1,0:T(8,128)(2,1)}), bf16[9,768,768]{2,1,0:T(8,128)(2,1)}) %all-gather.3.cloned.1.call-update) | async-done | bytes 10616848 | tf_op jit(solution)/shard_map/all_gather | solution.py:13
  83.3 6.3 %fusion.1 = bf16[9,192,768]{2,1,0:T(8,128)(2,1)S(1)} fusion(pred[9,768]{1,0:T(8,128)(4,1)S(1)} %iota_compare_fusion, bf16[9,768,768]{2,1,0:T(8,128)(2,1)} %all-gather.3.cloned.1.call-done, bf16[192,768]{1,0:T(8,128)(2,1)S(1)} %copy-done.3), kind=kOutput, calls=%fused_computation.4 | convolution fusion | flops 2041085952 | bytes 13572864 | tf_op jit(solution)/shard_map/ab,kbc->kac/dot_general | solution.py:16
  89.6 1.5 copy-done.7
  91.1 3.4 fusion.2
  94.5 29.3 %reduce-scatter.11.cloned.1.call-done = bf16[768,192]{0,1:T(8,128)(2,1)} async-done(((bf16[768,768]{0,1:T(8,128)(2,1)}), bf16[768,192]{0,1:T(8,128)(2,1)}) %reduce-scatter.11.cloned.1.call-update) | async-done | bytes 294928 | tf_op jit(solution)/shard_map/reduce_scatter | solution.py:21
  123.8 1.9 copy.20
  125.8 20.7 %reduce-scatter.13.cloned.1.call-done = bf16[192,192]{1,0:T(8,128)(2,1)} async-done(((bf16[768,192]{1,0:T(8,128)(2,1)}), bf16[192,192]{1,0:T(8,128)(2,1)}) %reduce-scatter.13.cloned.1.call-update) | async-done | bytes 73744
  146.4 1.0 copy.21
  148.2 33.1 %psum.14 = f32[]{:T(128)} all-reduce(f32[]{:T(128)} %fusion.9), channel_id=1, replica_groups=mesh['sweep'=2,'env'=4,'sec'=4] {'env','sec'}, use_global_device_ids=true, to_apply=%region_3.4 | all-reduce | flops 1 | bytes 8 | tf_op jit(solution)/shard_map/psum | solution.py:27
  182.7 30.3 %psum.15 = f32[]{:T(128)} all-reduce(f32[]{:T(128)} %multiply_reduce_fusion), channel_id=1, replica_groups=mesh['sweep'=2,'env'=4,'sec'=4] {'env','sec'}, use_global_device_ids=true, to_apply=%region_5.6 | all-reduce | flops 1 | bytes 8 | tf_op jit(solution)/shard_map/psum | solution.py:30
  213.7 15.1 %all_gather.10 = bf16[192,768]{0,1:T(8,128)(2,1)S(1)} all-gather(bf16[192,192]{0,1:T(8,128)(2,1)S(1)} %get-tuple-element.12), channel_id=1, replica_groups=mesh['sweep'=2,'env'=4,'sec'=4] {'sec'}, dimensions={1}, use_global_device_ids=true | all-gather | bytes 368640 | tf_op jit(solution)/shard_map/all_gather | solution.py:34
  229.7 16.7 %all-gather.5.cloned.1.call-done = bf16[768,768]{1,0:T(8,128)(2,1)} async-done(((bf16[192,768]{1,0:T(8,128)(2,1)}), bf16[768,768]{1,0:T(8,128)(2,1)}) %all-gather.5.cloned.1.call-update) | async-done | bytes 1179664 | tf_op jit(solution)/shard_map/all_gather | solution.py:35
  246.4 3.5 fusion
  250.0 1.5 copy-done.2
  251.4 7.6 %fusion.3 = bf16[192,768]{1,0:T(8,128)(2,1)S(1)} fusion(bf16[9,192,768]{2,1,0:T(8,128)(2,1)S(1)} %fusion, bf16[9,768,768]{2,1,0:T(8,128)(2,1)} %all-gather.3.cloned.1.call-done), kind=kOutput, calls=%fused_computation.8 | convolution fusion | flops 2038579200 | bytes 13565952 | tf_op jit(solution)/shard_map/kac,kbc->ab/dot_general | solution.py:41
  260.2 8.7 %convert_bitcast_fusion = bf16[9,768,768]{1,2,0:T(8,128)(2,1)} fusion(bf16[9,192,768]{2,1,0:T(8,128)(2,1)} %copy-done.2, bf16[192,768]{1,0:T(8,128)(2,1)S(1)} %copy-done.3), kind=kOutput, calls=%fused_computation | convolution fusion | flops 2043740160 | bytes 13565952 | tf_op jit(solution)/shard_map/ab,kac->kbc/dot_general | solution.py:47
  268.9 22.3 %copy.24 = bf16[9,768,768]{2,0,1:T(8,128)(2,1)} copy(bf16[9,768,768]{1,2,0:T(8,128)(2,1)} %convert_bitcast_fusion) | data formatting | bytes 21233664
  291.3 13.6 %copy.26 = bf16[96,8,9,768]{3,1,2,0:T(8,128)(2,1)} copy(bf16[96,8,9,768]{3,2,1,0:T(8,128)(2,1)} %bitcast.44) | data formatting | bytes 21233664
  306.2 6.4 %fusion.4 = f32[9,192,768]{2,1,0:T(8,128)} fusion(bf16[9,192,768]{2,1,0:T(8,128)(2,1)} %copy-done.7, bf16[768,768]{1,0:T(8,128)(2,1)S(1)} %copy-done.5), kind=kOutput, calls=%fused_computation.9 | convolution fusion | flops 2038431744 | bytes 9142272 | tf_op jit(solution)/shard_map/kac,zc->kaz/dot_general | solution.py:40
  312.6 1.0 copy.23
  314.3 76.9 %reduce-scatter.17.cloned.1.call-done = bf16[192,6912]{1,0:T(8,128)(2,1)} async-done(((bf16[768,6912]{1,0:T(8,128)(2,1)}), bf16[192,6912]{1,0:T(8,128)(2,1)}) %reduce-scatter.17.cloned.1.call-update) | async-done | bytes 2654224
  391.2 5.9 %reshape.35 = bf16[192,9,768]{2,1,0:T(8,128)(2,1)} reshape(bf16[192,6912]{1,0:T(8,128)(2,1)} %reduce-scatter.17.cloned.1.call-done) | data formatting | bytes 5308416
  397.1 6.8 %copy.25 = bf16[9,192,768]{1,2,0:T(8,128)(2,1)} copy(bf16[9,192,768]{2,0,1:T(8,128)(2,1)} %bitcast.46) | data formatting | bytes 5308416
  403.8 5.8 %copy.19 = f32[9,192,768]{2,1,0:T(8,128)} copy(bf16[9,192,768]{1,2,0:T(8,128)(2,1)} %copy.25) | data formatting | bytes 7962624
  (37 shorter events, 7.2 us)
Async XLA Ops:
  7.2 83.9 %copy-start = (bf16[9,192,768]{2,1,0:T(8,128)(2,1)S(1)}, bf16[9,192,768]{2,1,0:T(8,128)(2,1)}, u32[]{:S(2)}) copy-start(bf16[9,192,768]{2,1,0:T(8,128)(2,1)} %param.7) | copy-start | bytes 7962628
  7.2 0.8 copy-start.6
  7.2 76.1 %copy-start.3 = (bf16[192,768]{1,0:T(8,128)(2,1)S(1)}, bf16[192,768]{1,0:T(8,128)(2,1)}, u32[]{:S(2)}) copy-start(bf16[192,768]{1,0:T(8,128)(2,1)} %param.5) | copy-start | bytes 884740
  7.2 76.1 %all-gather.3.cloned.1.call-start = ((), (), s32[]{:S(2)}) async-start(), calls=%async_computation.4 | async-start | bytes 13271040 | tf_op jit(solution)/shard_map/all_gather | solution.py:13
  7.9 115.9 %reduce-scatter.11.cloned.1.call-start = ((), (), s32[]{:S(2)}) async-start(), calls=%async_computation.5 | async-start | bytes 1474560 | tf_op jit(solution)/shard_map/reduce_scatter | solution.py:21
  89.5 1.5 copy-start.7
  94.5 53.6 %copy-start.4 = (f32[192,192]{1,0:T(8,128)S(1)}, f32[192,192]{1,0:T(8,128)}, u32[]{:S(2)}) copy-start(f32[192,192]{1,0:T(8,128)} %param.9) | copy-start | bytes 442372
  94.5 52.0 %reduce-scatter.13.cloned.1.call-start = ((), (), s32[]{:S(2)}) async-start(), calls=%async_computation.7 | async-start | bytes 491520
  125.7 120.7 %all-gather.5.cloned.1.call-start = ((), (), s32[]{:S(2)}) async-start(), calls=%async_computation.6 | async-start | bytes 1474560 | tf_op jit(solution)/shard_map/all_gather | solution.py:35
  229.7 82.9 %reduce-scatter.15.cloned.1.call-start = ((), (), s32[]{:S(2)}) async-start(), calls=%async_computation.8 | async-start | bytes 491520
  249.9 1.5 copy-start.2
  260.0 131.2 %reduce-scatter.17.cloned.1.call-start = ((), (), s32[]{:S(2)}) async-start(), calls=%async_computation.9 | async-start | bytes 13271040
  304.9 1.3 copy-start.5
  397.1 12.6 %copy-start.1 = (bf16[9,192,768]{2,1,0:T(8,128)(2,1)S(1)}, bf16[9,192,768]{2,1,0:T(8,128)(2,1)}, u32[]{:S(2)}) copy-start(bf16[9,192,768]{2,1,0:T(8,128)(2,1)} %param.7) | copy-start | bytes 7962628
Sparse Core Ops, SparseCore 0:
  9.6 73.6 all-gather.2
  94.6 29.1 reduce-scatter.10
  126.9 19.5 reduce-scatter.12
  229.8 16.5 all-gather.4
  260.1 20.5 reduce-scatter.14
  305.0 86.1 reduce-scatter.16
where the time goes:
time: 418 us; the launch traced here: 416 us
  waiting for transfers between devices  219 us (52%)
  blocking collectives  78.5 us (19%)
  local copies, waits for them, and re-layouts  64.5 us (15%)
  matrix products  35.9 us (9%)
  between operations  14.9 us (4%)
    unnamed x9, waiting for transfers between devices  98.3 us
    all_gather x1, waiting for transfers between devices, per_device(): full_edges = lax.all_gather(edges, 'env', axis=1, tiled=True)  75.2 us
    unnamed x27, local copies, waits for them, and re-layouts  63.6 us
    psum x1, blocking collectives, per_device(): norm_sq = lax.psum(jnp.sum(absorbed * absorbed), ('env', 'sec'))  33.1 us
    psum x1, blocking collectives, per_device(): intersection = lax.psum(jnp.sum(cotangent * corner_new), ('env', 'sec'))  30.3 us
    reduce_scatter x1, waiting for transfers between devices, per_device(): lax.psum_scatter(partial_sum.astype(jnp.bfloat16), 'sec', scatter_dimensi...  29.3 us
    all_gather x1, waiting for transfers between devices, per_device(): grad_full = lax.all_gather(grad_cols, 'env', axis=0, tiled=True)  16.7 us
    all_gather x1, blocking collectives, per_device(): grad_cols = lax.all_gather(absorbed_grad, 'sec', axis=1, tiled=True)  15.1 us
  transfers between devices with their start and end apart: 6, of which 5 were waited for; matrix products, arithmetic and copies ran while one was open for 13% of the time, Pallas kernels for 0%

commit v1 on v0

v1 whole, which is shorter than its diff:
```python
import functools

import jax
import jax.numpy as jnp
from jax import lax
from jax.experimental import pallas as pl
from jax.experimental.pallas import tpu as pltpu
from jax.sharding import PartitionSpec as P

TILE = 128
F32, BF16 = jnp.float32, jnp.bfloat16
VMEM_LIMIT = 40 * 1024 * 1024


def swap(value, axis, offset):
    size = lax.axis_size(axis)
    return lax.ppermute(value, axis, [(i, i ^ offset) for i in range(size)])


def gather_blocks(own):
    blocks = [own]
    for m in range(1, lax.axis_size("env")):
        blocks.append(swap(blocks[m - 1], "env", 1) if m % 2 else swap(own, "env", m))
    return blocks


def after(value, *earlier):
    return lax.optimization_barrier((value, *earlier))[0]


def dot(a, b, dims=((1,), (0,))):
    return lax.dot_general(a, b, (dims, ((), ())), preferred_element_type=F32)


def call(kernel, name, grid, in_specs, out_specs, out_shape, scratch, flops, nbytes, prefetch, args):
    return pl.pallas_call(
        kernel,
        grid_spec=pltpu.PrefetchScalarGridSpec(
            num_scalar_prefetch=prefetch,
            grid=grid,
            in_specs=in_specs,
            out_specs=out_specs,
            scratch_shapes=scratch,
        ),
        out_shape=out_shape,
        name=name,
        compiler_params=pltpu.CompilerParams(vmem_limit_bytes=VMEM_LIMIT),
        cost_estimate=pl.CostEstimate(flops=flops, bytes_accessed=nbytes, transcendentals=0),
    )(*args)


def keep_columns(shape, first, count):
    return lax.broadcasted_iota(jnp.int32, shape, 1) + first < count * TILE


def whole(shape):
    return pl.BlockSpec(shape, lambda k, *s: (0,) * len(shape))


def per_slice(shape, index=0):
    return pl.BlockSpec((1, *shape), lambda k, *s: (k, 0, index))


def absorb_kernel(n, rows, first, me, counts, *refs):
    c_ref, e_refs, p_ref = refs[0], refs[1 : n + 1], refs[n + 1]
    enl_ref, keep_ref, send_ref, acc = refs[n + 2 :]
    k = pl.program_id(0)

    @pl.when(k == 0)
    def _():
        acc[...] = jnp.zeros_like(acc)

    x = dot(c_ref[0], e_refs[0][0])
    for m in range(1, n):
        x = x + dot(c_ref[m], e_refs[m][0])
    x = jnp.where(keep_columns(x.shape, first, counts[k]), x, 0.0).astype(BF16)
    enl_ref[0] = x
    acc[...] += dot(p_ref[0], x, ((0,), (0,)))

    @pl.when(k == pl.num_programs(0) - 1)
    def _():
        for j in range(n // 2):
            mine = pl.multiple_of((me[0] ^ (2 * j)) * rows, rows)
            other = pl.multiple_of((me[0] ^ (2 * j + 1)) * rows, rows)
            keep_ref[j] = acc[pl.ds(mine, rows), :]
            send_ref[j] = acc[pl.ds(other, rows), :].astype(BF16)


def absorb(me, counts, c_parts, e_blocks, edges, projectors, first, cols):
    n, rows = c_parts.shape[:2]
    slices, _, width = projectors.shape
    return call(
        functools.partial(absorb_kernel, n, rows, first),
        "absorb",
        (slices,),
        [whole(c_parts.shape), per_slice((rows, cols), first // cols)]
        + [per_slice((rows, cols))] * (n - 1)
        + [per_slice((rows, width))],
        [per_slice((rows, cols)), whole((n // 2, rows, cols)), whole((n // 2, rows, cols))],
        [
            jax.ShapeDtypeStruct((slices, rows, cols), BF16),
            jax.ShapeDtypeStruct((n // 2, rows, cols), F32),
            jax.ShapeDtypeStruct((n // 2, rows, cols), BF16),
        ],
        [pltpu.VMEM((width, cols), F32)],
        4 * slices * rows * width * cols,
        2 * slices * width * (cols + rows),
        2,
        (me, counts, c_parts, edges, *e_blocks[1:], projectors),
    )


def mix_kernel(n, refs_c, *refs):
    p_refs, out = refs[:n], refs[n]
    x = dot(refs_c[0], p_refs[0][0], ((0,), (0,)))
    for m in range(1, n):
        x = x + dot(refs_c[m], p_refs[m][0], ((0,), (0,)))
    out[0] = x.astype(BF16)


def mix(c_cols, p_blocks):
    n, rows = c_cols.shape[:2]
    slices, _, width = p_blocks[0].shape
    return call(
        functools.partial(mix_kernel, n),
        "mix",
        (slices,),
        [whole(c_cols.shape)] + [per_slice((rows, width))] * n,
        per_slice((rows, width)),
        jax.ShapeDtypeStruct((slices, rows, width), BF16),
        [],
        2 * slices * rows * width * width,
        2 * slices * width * (width + rows),
        0,
        (c_cols, *p_blocks),
    )


def fill(n, rows, me, g_refs, g):
    @pl.when(pl.program_id(0) == 0)
    def _():
        for m in range(n):
            at = pl.multiple_of((me[0] ^ m) * rows, rows)
            g[pl.ds(at, rows), :] = g_refs[m][...]


def corner_kernel(n, rows, me, counts, *refs):
    g_refs, p_ref, e_refs = refs[:n], refs[n], refs[n + 1 : 2 * n + 1]
    out, g, acc = refs[2 * n + 1 :]
    k = pl.program_id(0)
    fill(n, rows, me, g_refs, g)

    @pl.when(k == 0)
    def _():
        acc[...] = jnp.zeros_like(acc)

    x = dot(p_ref[0], g[...])
    x = jnp.where(keep_columns(x.shape, 0, counts[k]), x, 0.0).astype(BF16)
    for m in range(n):
        acc[m] += dot(x, e_refs[m][0], ((1,), (1,)))

    @pl.when(k == pl.num_programs(0) - 1)
    def _():
        for m in range(n):
            out[me[0] ^ m] = acc[m].astype(BF16)


def corner_part(me, counts, g_blocks, projectors, e_blocks):
    n = len(g_blocks)
    slices, rows, width = projectors.shape
    return call(
        functools.partial(corner_kernel, n, rows),
        "corner_part",
        (slices,),
        [whole((rows, width))] * n + [per_slice((rows, width))] * (n + 1),
        whole((n, rows, rows)),
        jax.ShapeDtypeStruct((n, rows, rows), BF16),
        [pltpu.VMEM((width, width), BF16), pltpu.VMEM((n, rows, rows), F32)],
        4 * slices * rows * width * width,
        2 * slices * width * (width + rows),
        2,
        (me, counts, *g_blocks, projectors, *e_blocks),
    )


def grads_kernel(n, rows, parts, me, counts, *refs):
    g_refs, q_ref, enl_refs = refs[:n], refs[n], refs[n + 1 : n + 1 + len(parts)]
    edge, proj, g = refs[n + 1 + len(parts) :]
    fill(n, rows, me, g_refs, g)
    k = pl.program_id(0)
    x = dot(q_ref[0], g[...])
    edge[0] = jnp.where(keep_columns(x.shape, 0, counts[k]), x, 0.0)
    y = None
    for (first, cols), enl in zip(parts, enl_refs):
        z = dot(enl[0], g[:, first : first + cols], ((1,), (1,)))
        y = z if y is None else y + z
    proj[0] = y


def grads(me, counts, g_blocks, q, enlarged, parts):
    n = len(g_blocks)
    slices, rows, width = q.shape
    return call(
        functools.partial(grads_kernel, n, rows, parts),
        "grads",
        (slices,),
        [whole((rows, width))] * n
        + [per_slice((rows, width))]
        + [per_slice((rows, cols)) for _, cols in parts],
        [per_slice((rows, width))] * 2,
        [jax.ShapeDtypeStruct((slices, rows, width), F32)] * 2,
        [pltpu.VMEM((width, width), BF16)],
        4 * slices * rows * width * width,
        12 * slices * width * rows,
        2,
        (me, counts, *g_blocks, q, *enlarged),
    )


def per_device(corner, edges, projectors, tile_counts, cotangent):
    n, n_sec = lax.axis_size("env"), lax.axis_size("sec")
    e, s = lax.axis_index("env"), lax.axis_index("sec")
    slices, rows, width = edges.shape
    cols = cotangent.shape[1]
    me = jnp.reshape(e, (1,)).astype(jnp.int32)
    parts = ((0, width // 3 * 2), (width // 3 * 2, width // 3))

    e_parts, earlier = [], None
    for first, size in parts:
        piece = edges[:, :, first : first + size]
        if earlier is not None:
            piece = after(piece, earlier)
        e_parts.append(gather_blocks(piece))
        earlier = e_parts[-1][2]

    c_parts = [lax.dynamic_slice_in_dim(corner, (e ^ m) * rows, rows, 1) for m in range(n)]
    c_cols = jnp.stack([c_parts[0]] + [swap(c_parts[m], "env", m) for m in range(1, n)])
    c_parts = jnp.stack(c_parts)

    cot_blocks = [cotangent] + [swap(cotangent, "sec", m) for m in range(1, n_sec)]
    cot_rows = jnp.concatenate(
        [
            functools.reduce(
                lambda a, m: jnp.where((s ^ m) == q, cot_blocks[m], a), range(1, n_sec), cot_blocks[0]
            )
            for q in range(n_sec)
        ],
        axis=1,
    )

    enlarged, absorbed = [], []
    for (first, size), blocks in zip(parts, e_parts):
        enl, keep, send = absorb(me, tile_counts, c_parts, blocks, edges, projectors, first, size)
        enlarged.append(enl)
        total = keep + swap(send, "env", 1).astype(F32)
        moved = total.astype(BF16)
        total = total[0]
        for j in range(1, n // 2):
            total = total + swap(moved[j], "env", 2 * j).astype(F32)
        moved = total.astype(BF16)
        total = moved.astype(F32)
        for m in range(1, n_sec):
            total = total + swap(moved, "sec", m).astype(F32)
        absorbed.append(total)
    absorbed = jnp.concatenate(absorbed, axis=1)

    third = slices // 3
    mixed, earlier = [], e_parts[-1][2]
    for at in range(0, slices, third):
        piece = after(projectors[at : at + third], earlier)
        blocks = gather_blocks(piece)
        earlier = blocks[2]
        mixed.append(mix(c_cols, blocks))
    mixed = jnp.concatenate(mixed, axis=0)

    sums = jnp.stack([jnp.sum(absorbed * absorbed), jnp.sum(cot_rows * absorbed)])
    own = sums
    for m in range(2, n, 2):
        sums = sums + swap(own, "env", m)
    sums = sums + swap(sums, "env", 1)
    scale = width / jnp.sqrt(sums[0])
    intersection = scale * sums[1]
    corner_new = scale * absorbed
    grad_rows = (scale * (cot_rows - corner_new * intersection / (width * width))).astype(BF16)
    corner_new = lax.dynamic_slice_in_dim(corner_new, s * cols, cols, 1)
    g_blocks = gather_blocks(grad_rows)

    e_full = [edges] + [
        jnp.concatenate([blocks[m] for blocks in e_parts], axis=2) for m in range(1, n)
    ]
    part = corner_part(me, tile_counts, g_blocks, projectors, e_full)
    part = jnp.transpose(part, (1, 0, 2)).reshape(rows, width)
    corner_grad = lax.dynamic_slice_in_dim(part, s * cols, cols, 1).astype(F32)
    for m in range(1, n_sec):
        piece = lax.dynamic_slice_in_dim(part, (s ^ m) * cols, cols, 1)
        corner_grad = corner_grad + swap(piece, "sec", m).astype(F32)

    edge_grad, proj_grad = grads(me, tile_counts, g_blocks, mixed, enlarged, parts)
    return (corner_new, corner_grad, edge_grad, proj_grad)


def solution(mesh):
    placed = (
        P(("sweep", "env"), None),
        P(("sweep", "sec"), "env", None),
        P(("sweep", "sec"), "env", None),
        P(("sweep", "sec")),
        P(("sweep", "env"), "sec"),
    )
    return jax.shard_map(
        per_device,
        mesh=mesh,
        in_specs=placed,
        out_specs=(
            P(("sweep", "env"), "sec"),
            P(("sweep", "env"), "sec"),
            P(("sweep", "sec"), "env", None),
            P(("sweep", "sec"), "env", None),
        ),
        check_vma=False,
    )
```

time: 418 us -> 269 us (0.64)
  blocking collectives: 78.5 us -> 0 us
  waiting for transfers between devices: 219 us -> 141 us
  local copies, waits for them, and re-layouts: 64.5 us -> 13.9 us
  Pallas kernels: 0 us -> 49 us
  starting transfers between devices: 0.42 us -> 42.4 us
  matrix products: 35.9 us -> 0 us
  other arithmetic: 2.77 us -> 19.3 us
  between operations: 14.9 us -> 2.44 us
    ppermute x0 -> x39, waiting for transfers between devices: none -> 141 us  [swap(): return lax.ppermute(value, axis, [(i, i ^ offset) for i in range(size)])]
    unnamed x9 -> x0, waiting for transfers between devices: 98.3 us -> none
    all_gather x2 -> x0, waiting for transfers between devices: 91.9 us -> none  [the longest x1 75.2 us: per_device(): full_edges = lax.all_gather(edges, 'env', axis=1, tiled=True)]
    psum x2 -> x0, blocking collectives: 63.4 us -> none  [the longest x1 33.1 us: per_device(): norm_sq = lax.psum(jnp.sum(absorbed * absorbed), ('env', 'sec'))]
    unnamed x27 -> x46, local copies, waits for them, and re-layouts: 63.6 us -> 3.3 us
    pallas_call x0 -> x7, Pallas kernels: none -> 49 us  [call(): pl.pallas_call(kernel, grid_spec=pltpu.PrefetchScalarGridSpec(num_scalar_...]
    ppermute x0 -> x39, starting transfers between devices: none -> 42.4 us  [swap(): return lax.ppermute(value, axis, [(i, i ^ offset) for i in range(size)])]
    dot_general x6 -> x0, matrix products: 35.9 us -> none  [the longest x1 8.7 us: per_device(): jnp.einsum('ab,kac->kbc', corner, enlarged_grad, preferred_element_type=j...]
  transfers between devices with their start and end apart: 6 -> 39, of which waited for: 5 -> 16; matrix products, arithmetic and copies ran while one was open for 13% -> 10% of each run, Pallas kernels for 0% -> 13%
where the time goes in v1:
time: 269 us; the launch traced here: 268 us
  waiting for transfers between devices  141 us (52%)
  Pallas kernels  49 us (18%)
  starting transfers between devices  42.4 us (16%)
  other arithmetic  19.3 us (7%)
  local copies, waits for them, and re-layouts  13.9 us (5%)
    ppermute x39, waiting for transfers between devices, swap(): return lax.ppermute(value, axis, [(i, i ^ offset) for i in range(size)])  141 us
    pallas_call x7, Pallas kernels, call(): pl.pallas_call(kernel, grid_spec=pltpu.PrefetchScalarGridSpec(num_scalar_...  49 us
    ppermute x39, starting transfers between devices, swap(): return lax.ppermute(value, axis, [(i, i ^ offset) for i in range(size)])  42.4 us
    concatenate x3, other arithmetic, per_device(): jnp.concatenate([blocks[m] for blocks in e_parts], axis=2)  7.43 us
  transfers between devices with their start and end apart: 39, of which 16 were waited for; matrix products, arithmetic and copies ran while one was open for 10% of the time, Pallas kernels for 13%

profile of v1, /device:TPU:0, one launch (start us, length us, event | category | flops | bytes accessed | tf_op | source)
XLA Modules:
  0.0 268.1 jit_solution(2414353790037659729)
XLA Ops:
  3.6 3.0 %collective-permute-start.1 = (bf16[9,192,512]{2,1,0:T(8,128)(2,1)}, bf16[9,192,512]{2,1,0:T(8,128)(2,1)}, u32[]{:S(2)}, u32[]{:S(2)}) collective-permute-start(bf16[9,192,512]{2,1,0:T(8,128)(2,1)} %slice.33), channel_id=1, source_target_pairs={{0,8},{4,12},{8,0},{12,4},{1,9},{5,13},{9,1},{13,5},{2,10},{6,14},... | collective-permute-start | bytes 5308424 | tf_op jit(solution)/shard_map/ppermute | solution.py:17
  7.5 37.9 %collective-permute-done.1.refs_3_ = bf16[9,192,512]{2,1,0:T(8,128)(2,1)} collective-permute-done((bf16[9,192,512]{2,1,0:T(8,128)(2,1)}, bf16[9,192,512]{2,1,0:T(8,128)(2,1)}, u32[]{:S(2)}, u32[]{:S(2)}) %collective-permute-start.1) | collective-permute-done | bytes 1769504 | tf_op jit(solution)/shard_map/ppermute | solution.py:17
  51.5 17.1 %collective-permute-done.29 = bf16[192,192]{1,0:T(8,128)(2,1)} collective-permute-done((bf16[192,192]{1,0:T(8,128)(2,1)S(1)}, bf16[192,192]{1,0:T(8,128)(2,1)}, u32[]{:S(2)}, u32[]{:S(2)}) %collective-permute-start.29) | collective-permute-done | bytes 73760 | tf_op jit(solution)/shard_map/ppermute | solution.py:17
  71.2 3.1 %collective-permute-start.16 = (f32[192,192]{1,0:T(8,128)}, f32[192,192]{1,0:T(8,128)S(1)}, u32[]{:S(2)}, u32[]{:S(2)}) collective-permute-start(f32[192,192]{1,0:T(8,128)} %param.9), channel_id=1, source_target_pairs={{0,3},{1,2},{2,1},{3,0},{4,7},{5,6},{6,5},{7,4},{8,11},{9,10},{10,... | collective-permute-start | bytes 442376 | tf_op jit(solution)/shard_map/ppermute | solution.py:17
  74.4 11.6 %collective-permute-done.17 = f32[192,192]{1,0:T(8,128)S(1)} collective-permute-done((f32[192,192]{1,0:T(8,128)}, f32[192,192]{1,0:T(8,128)S(1)}, u32[]{:S(2)}, u32[]{:S(2)}) %collective-permute-start.17) | collective-permute-done | bytes 147488 | tf_op jit(solution)/shard_map/ppermute | solution.py:17
  86.5 4.4 %collective-permute-start.18 = (f32[192,192]{1,0:T(8,128)}, f32[192,192]{1,0:T(8,128)}, u32[]{:S(2)}, u32[]{:S(2)}) collective-permute-start(f32[192,192]{1,0:T(8,128)} %param.9), channel_id=1, source_target_pairs={{0,1},{1,0},{2,3},{3,2},{4,5},{5,4},{6,7},{7,6},{8,9},{9,8},{10,11... | collective-permute-start | bytes 442376 | tf_op jit(solution)/shard_map/ppermute | solution.py:17
  90.9 3.2 %fusion.11 = (bf16[3,192,768]{2,1,0:T(8,128)(2,1)}, bf16[3,192,768]{2,1,0:T(8,128)(2,1)}, bf16[3,192,768]{2,1,0:T(8,128)(2,1)}) fusion(bf16[9,192,768]{2,1,0:T(8,128)(2,1)} %refs_4_.1), kind=kLoop, calls=%fused_computation.44 | loop fusion | bytes 5308416 | tf_op jit(solution)/shard_map/slice | solution.py:270
  99.7 9.1 %absorb.3 = (bf16[9,192,256]{2,1,0:T(8,128)(2,1)S(1)}, f32[2,192,256]{2,1,0:T(8,128)S(1)}, bf16[2,192,256]{2,1,0:T(8,128)(2,1)S(1)}) custom-call(s32[1]{0:T(128)} %bitcast.me, s32[9]{0:T(128)S(1)} %copy-done.3, bf16[4,192,192]{2,1,0:T(8,128)(2,1)S(1)} %get-tuple-element.47.refs_0_, bf16[9,192,768]{2,1,0:T(8,128)(2,1)S(1)} %copy-done, ...), custom_call_target="tpu_custom_call" | custom-call | flops 1358954496 | bytes 6193152 | tf_op jit(solution)/shard_map/absorb/pallas_call | solution.py:36
  110.3 10.0 %absorb.2 = (bf16[9,192,512]{2,1,0:T(8,128)(2,1)S(1)}, f32[2,192,512]{2,1,0:T(8,128)S(1)}, bf16[2,192,512]{2,1,0:T(8,128)(2,1)S(1)}) custom-call(s32[1]{0:T(128)} %bitcast.me, s32[9]{0:T(128)S(1)} %copy-done.3, bf16[4,192,192]{2,1,0:T(8,128)(2,1)S(1)} %get-tuple-element.47.refs_0_, bf16[9,192,768]{2,1,0:T(8,128)(2,1)S(1)} %copy-done, ...), custom_call_target="tpu_custom_call" | custom-call | flops 2717908992 | bytes 9732096 | tf_op jit(solution)/shard_map/absorb/pallas_call | solution.py:36
  124.3 21.0 %collective-permute-done.12 = bf16[192,256]{1,0:T(8,128)(2,1)S(1)} collective-permute-done((bf16[192,256]{1,0:T(8,128)(2,1)S(1)}, bf16[192,256]{1,0:T(8,128)(2,1)S(1)}, u32[]{:S(2)}, u32[]{:S(2)}) %collective-permute-start.12) | collective-permute-done | bytes 98336 | tf_op jit(solution)/shard_map/ppermute | solution.py:17
  145.3 3.2 %collective-permute-start.15 = (bf16[192,256]{1,0:T(8,128)(2,1)S(1)}, bf16[192,256]{1,0:T(8,128)(2,1)S(1)}, u32[]{:S(2)}, u32[]{:S(2)}) collective-permute-start(bf16[192,256]{1,0:T(8,128)(2,1)S(1)} %fusion.9), channel_id=1, source_target_pairs={{0,3},{1,2},{2,1},{3,0},{4,7},{5,6},{6,5},{7,4},{8,11},{9,10},{10,... | collective-permute-start | bytes 294920 | tf_op jit(solution)/shard_map/ppermute | solution.py:17
  152.5 3.3 %collective-permute-start.7 = (bf16[192,512]{1,0:T(8,128)(2,1)S(1)}, bf16[192,512]{1,0:T(8,128)(2,1)S(1)}, u32[]{:S(2)}, u32[]{:S(2)}) collective-permute-start(bf16[192,512]{1,0:T(8,128)(2,1)S(1)} %fusion.5), channel_id=1, source_target_pairs={{0,3},{1,2},{2,1},{3,0},{4,7},{5,6},{6,5},{7,4},{8,11},{9,10},{10,... | collective-permute-start | bytes 589832 | tf_op jit(solution)/shard_map/ppermute | solution.py:17
  155.8 6.2 %collective-permute-done.14 = bf16[192,256]{1,0:T(8,128)(2,1)S(1)} collective-permute-done((bf16[192,256]{1,0:T(8,128)(2,1)S(1)}, bf16[192,256]{1,0:T(8,128)(2,1)S(1)}, u32[]{:S(2)}, u32[]{:S(2)}) %collective-permute-start.14) | collective-permute-done | bytes 98336 | tf_op jit(solution)/shard_map/ppermute | solution.py:17
  162.0 3.5 %collective-permute-start.5 = (bf16[192,512]{1,0:T(8,128)(2,1)S(1)}, bf16[192,512]{1,0:T(8,128)(2,1)S(1)}, u32[]{:S(2)}, u32[]{:S(2)}) collective-permute-start(bf16[192,512]{1,0:T(8,128)(2,1)S(1)} %fusion.5), channel_id=1, source_target_pairs={{0,1},{1,0},{2,3},{3,2},{4,5},{5,4},{6,7},{7,6},{8,9},{9,8},{10,11... | collective-permute-start | bytes 589832 | tf_op jit(solution)/shard_map/ppermute | solution.py:17
  165.5 8.6 %collective-permute-done.6 = bf16[192,512]{1,0:T(8,128)(2,1)S(1)} collective-permute-done((bf16[192,512]{1,0:T(8,128)(2,1)S(1)}, bf16[192,512]{1,0:T(8,128)(2,1)S(1)}, u32[]{:S(2)}, u32[]{:S(2)}) %collective-permute-start.6) | collective-permute-done | bytes 196640 | tf_op jit(solution)/shard_map/ppermute | solution.py:17
  193.1 19.6 %collective-permute-done.22.refs_2_ = bf16[192,768]{1,0:T(8,128)(2,1)} collective-permute-done((bf16[192,768]{1,0:T(8,128)(2,1)S(1)}, bf16[192,768]{1,0:T(8,128)(2,1)}, u32[]{:S(2)}, u32[]{:S(2)}) %collective-permute-start.22) | collective-permute-done | bytes 294944 | tf_op jit(solution)/shard_map/ppermute | solution.py:17
  214.6 3.6 %pad_maximum_fusion.2.refs_8_ = bf16[9,192,768]{2,1,0:T(8,128)(2,1)} fusion(bf16[9,192,256]{2,1,0:T(8,128)(2,1)} %collective-permute-done.10.refs_4_, bf16[9,192,512]{2,1,0:T(8,128)(2,1)} %collective-permute-done.2.refs_4_), kind=kLoop, calls=%fused_computation.2 | loop fusion | flops 5308416 | bytes 5308416 | tf_op jit(solution)/shard_map/concatenate | solution.py:289
  219.3 9.4 %corner_part.1 = bf16[4,192,192]{2,1,0:T(8,128)(2,1)S(1)} custom-call(s32[1]{0:T(128)} %bitcast.me, s32[9]{0:T(128)S(1)} %copy-done.3, bf16[192,768]{1,0:T(8,128)(2,1)S(1)} %get-tuple-element.37.refs_0_, bf16[192,768]{1,0:T(8,128)(2,1)S(1)} %collective-permute-done.21.refs_1_, bf16[192,768]{1,0:T(8,128)(2,1)} %collective-permute-done.22.refs_2_, ...), custom_call_target="tpu_custom_call" | custom-call | flops 4076863488 | bytes 13271040 | tf_op jit(solution)/shard_map/corner_part/pallas_call | solution.py:36
  229.7 5.1 %collective-permute-done.24 = bf16[192,192]{1,0:T(8,128)(2,1)S(1)} collective-permute-done((bf16[192,192]{1,0:T(8,128)(2,1)S(1)}, bf16[192,192]{1,0:T(8,128)(2,1)S(1)}, u32[]{:S(2)}, u32[]{:S(2)}) %collective-permute-start.24) | collective-permute-done | bytes 73760 | tf_op jit(solution)/shard_map/ppermute | solution.py:17
  237.4 3.8 %collective-permute-done.26 = bf16[192,192]{1,0:T(8,128)(2,1)S(1)} collective-permute-done((bf16[192,192]{1,0:T(8,128)(2,1)S(1)}, bf16[192,192]{1,0:T(8,128)(2,1)S(1)}, u32[]{:S(2)}, u32[]{:S(2)}) %collective-permute-start.26) | collective-permute-done | bytes 73760 | tf_op jit(solution)/shard_map/ppermute | solution.py:17
  243.8 3.5 %mix.3 = bf16[3,192,768]{2,1,0:T(8,128)(2,1)S(1)} custom-call(bf16[4,192,192]{2,1,0:T(8,128)(2,1)S(1)} %get-tuple-element.46.refs_c, bf16[3,192,768]{2,1,0:T(8,128)(2,1)} %get-tuple-element.21.refs_0_, bf16[3,192,768]{2,1,0:T(8,128)(2,1)} %collective-permute-done.30.refs_1_, bf16[3,192,768]{2,1,0:T(8,128)(2,1)} %collective-permute-done.31.refs_2_, ...), custom_call_target="tpu_custom_call" | custom-call | flops 679477248 | bytes 4423680 | tf_op jit(solution)/shard_map/mix/pallas_call | solution.py:36
  249.2 3.5 %mix.4 = bf16[3,192,768]{2,1,0:T(8,128)(2,1)S(1)} custom-call(bf16[4,192,192]{2,1,0:T(8,128)(2,1)S(1)} %get-tuple-element.46.refs_c, bf16[3,192,768]{2,1,0:T(8,128)(2,1)} %get-tuple-element.22.refs_0_, bf16[3,192,768]{2,1,0:T(8,128)(2,1)} %collective-permute-done.33.refs_1_, bf16[3,192,768]{2,1,0:T(8,128)(2,1)} %collective-permute-done.34.refs_2_, ...), custom_call_target="tpu_custom_call" | custom-call | flops 679477248 | bytes 4423680 | tf_op jit(solution)/shard_map/mix/pallas_call | solution.py:36
  252.7 3.5 %mix.5 = bf16[3,192,768]{2,1,0:T(8,128)(2,1)S(1)} custom-call(bf16[4,192,192]{2,1,0:T(8,128)(2,1)S(1)} %get-tuple-element.46.refs_c, bf16[3,192,768]{2,1,0:T(8,128)(2,1)} %get-tuple-element.23.refs_0_, bf16[3,192,768]{2,1,0:T(8,128)(2,1)} %collective-permute-done.36.refs_1_, bf16[3,192,768]{2,1,0:T(8,128)(2,1)} %collective-permute-done.37.refs_2_, ...), custom_call_target="tpu_custom_call" | custom-call | flops 679477248 | bytes 4423680 | tf_op jit(solution)/shard_map/mix/pallas_call | solution.py:36
  258.1 10.0 %grads.1 = (f32[9,192,768]{2,1,0:T(8,128)}, f32[9,192,768]{2,1,0:T(8,128)}) custom-call(s32[1]{0:T(128)} %bitcast.me, s32[9]{0:T(128)S(1)} %copy-done.3, bf16[192,768]{1,0:T(8,128)(2,1)S(1)} %get-tuple-element.37.refs_0_, bf16[192,768]{1,0:T(8,128)(2,1)S(1)} %copy-done.9, bf16[192,768]{1,0:T(8,128)(2,1)} %collective-permute-done.22.refs_2_, ...), custom_call_target="tpu_custom_call" | custom-call | flops 4076863488 | bytes 15925248 | tf_op jit(solution)/shard_map/grads/pallas_call | solution.py:36
  (136 shorter events, 58.4 us)
Async XLA Ops:
  3.6 41.9 %collective-permute-start.1 = (bf16[9,192,512]{2,1,0:T(8,128)(2,1)}, bf16[9,192,512]{2,1,0:T(8,128)(2,1)}, u32[]{:S(2)}, u32[]{:S(2)}) collective-permute-start(bf16[9,192,512]{2,1,0:T(8,128)(2,1)} %slice.33), channel_id=1, source_target_pairs={{0,8},{4,12},{8,0},{12,4},{1,9},{5,13},{9,1},{13,5},{2,10},{6,14},... | collective-permute-start | bytes 5308424 | tf_op jit(solution)/shard_map/ppermute | solution.py:17
  45.5 40.6 %collective-permute-start.9 = (bf16[9,192,256]{2,1,0:T(8,128)(2,1)}, bf16[9,192,256]{2,1,0:T(8,128)(2,1)}, u32[]{:S(2)}, u32[]{:S(2)}) collective-permute-start(bf16[9,192,256]{2,1,0:T(8,128)(2,1)} %slice.36), channel_id=1, source_target_pairs={{0,8},{4,12},{8,0},{12,4},{1,9},{5,13},{9,1},{13,5},{2,10},{6,14},... | collective-permute-start | bytes 2654216 | tf_op jit(solution)/shard_map/ppermute | solution.py:17
  47.2 63.1 %collective-permute-start = (bf16[9,192,512]{2,1,0:T(8,128)(2,1)}, bf16[9,192,512]{2,1,0:T(8,128)(2,1)}, u32[]{:S(2)}, u32[]{:S(2)}) collective-permute-start(bf16[9,192,512]{2,1,0:T(8,128)(2,1)} %slice.33), channel_id=1, source_target_pairs={{0,4},{4,0},{8,12},{12,8},{1,5},{5,1},{9,13},{13,9},{2,6},{6,2},{1... | collective-permute-start | bytes 5308424 | tf_op jit(solution)/shard_map/ppermute | solution.py:17
  47.2 63.1 %collective-permute-start.2 = (bf16[9,192,512]{2,1,0:T(8,128)(2,1)}, bf16[9,192,512]{2,1,0:T(8,128)(2,1)}, u32[]{:S(2)}, u32[]{:S(2)}) collective-permute-start(bf16[9,192,512]{2,1,0:T(8,128)(2,1)} %collective-permute-done.1.refs_3_), channel_id=1, source_target_pairs={{0,4},{4,0},{8,12},{12,8},{1,5},{5,1},{9,13},{13,9},{2,6},{6,2},{1... | collective-permute-start | bytes 5308424 | tf_op jit(solution)/shard_map/ppermute | solution.py:17
  48.0 20.6 %collective-permute-start.29 = (bf16[192,192]{1,0:T(8,128)(2,1)S(1)}, bf16[192,192]{1,0:T(8,128)(2,1)}, u32[]{:S(2)}, u32[]{:S(2)}) collective-permute-start(bf16[192,192]{1,0:T(8,128)(2,1)S(1)} %get-tuple-element.44), channel_id=1, source_target_pairs={{0,12},{4,8},{8,4},{12,0},{1,13},{5,9},{9,5},{13,1},{2,14},{6,10},... | collective-permute-start | bytes 221192 | tf_op jit(solution)/shard_map/ppermute | solution.py:17
  51.2 20.0 %collective-permute-start.28 = (bf16[192,192]{1,0:T(8,128)(2,1)S(1)}, bf16[192,192]{1,0:T(8,128)(2,1)}, u32[]{:S(2)}, u32[]{:S(2)}) collective-permute-start(bf16[192,192]{1,0:T(8,128)(2,1)S(1)} %get-tuple-element.45), channel_id=1, source_target_pairs={{0,8},{4,12},{8,0},{12,4},{1,9},{5,13},{9,1},{13,5},{2,10},{6,14},... | collective-permute-start | bytes 221192 | tf_op jit(solution)/shard_map/ppermute | solution.py:17
  68.6 17.3 %collective-permute-start.17 = (f32[192,192]{1,0:T(8,128)}, f32[192,192]{1,0:T(8,128)S(1)}, u32[]{:S(2)}, u32[]{:S(2)}) collective-permute-start(f32[192,192]{1,0:T(8,128)} %param.9), channel_id=1, source_target_pairs={{0,2},{1,3},{2,0},{3,1},{4,6},{5,7},{6,4},{7,5},{8,10},{9,11},{10,... | collective-permute-start | bytes 442376 | tf_op jit(solution)/shard_map/ppermute | solution.py:17
  71.2 15.2 %collective-permute-start.16 = (f32[192,192]{1,0:T(8,128)}, f32[192,192]{1,0:T(8,128)S(1)}, u32[]{:S(2)}, u32[]{:S(2)}) collective-permute-start(f32[192,192]{1,0:T(8,128)} %param.9), channel_id=1, source_target_pairs={{0,3},{1,2},{2,1},{3,0},{4,7},{5,6},{6,5},{7,4},{8,11},{9,10},{10,... | collective-permute-start | bytes 442376 | tf_op jit(solution)/shard_map/ppermute | solution.py:17
  85.9 13.7 %collective-permute-start.8 = (bf16[9,192,256]{2,1,0:T(8,128)(2,1)}, bf16[9,192,256]{2,1,0:T(8,128)(2,1)}, u32[]{:S(2)}, u32[]{:S(2)}) collective-permute-start(bf16[9,192,256]{2,1,0:T(8,128)(2,1)} %slice.36), channel_id=1, source_target_pairs={{0,4},{4,0},{8,12},{12,8},{1,5},{5,1},{9,13},{13,9},{2,6},{6,2},{1... | collective-permute-start | bytes 2654216 | tf_op jit(solution)/shard_map/ppermute | solution.py:17
  86.1 13.6 %collective-permute-start.10 = (bf16[9,192,256]{2,1,0:T(8,128)(2,1)}, bf16[9,192,256]{2,1,0:T(8,128)(2,1)}, u32[]{:S(2)}, u32[]{:S(2)}) collective-permute-start(bf16[9,192,256]{2,1,0:T(8,128)(2,1)} %collective-permute-done.9.refs_3_), channel_id=1, source_target_pairs={{0,4},{4,0},{8,12},{12,8},{1,5},{5,1},{9,13},{13,9},{2,6},{6,2},{1... | collective-permute-start | bytes 2654216 | tf_op jit(solution)/shard_map/ppermute | solution.py:17
  96.4 24.1 %collective-permute-start.31 = (bf16[3,192,768]{2,1,0:T(8,128)(2,1)}, bf16[3,192,768]{2,1,0:T(8,128)(2,1)}, u32[]{:S(2)}, u32[]{:S(2)}) collective-permute-start(bf16[3,192,768]{2,1,0:T(8,128)(2,1)} %get-tuple-element.21.refs_0_), channel_id=1, source_target_pairs={{0,8},{4,12},{8,0},{12,4},{1,9},{5,13},{9,1},{13,5},{2,10},{6,14},... | collective-permute-start | bytes 2654216 | tf_op jit(solution)/shard_map/ppermute | solution.py:17
  99.6 118.6 %collective-permute-start.30 = (bf16[3,192,768]{2,1,0:T(8,128)(2,1)}, bf16[3,192,768]{2,1,0:T(8,128)(2,1)}, u32[]{:S(2)}, u32[]{:S(2)}) collective-permute-start(bf16[3,192,768]{2,1,0:T(8,128)(2,1)} %get-tuple-element.21.refs_0_), channel_id=1, source_target_pairs={{0,4},{4,0},{8,12},{12,8},{1,5},{5,1},{9,13},{13,9},{2,6},{6,2},{1... | collective-permute-start | bytes 2654216 | tf_op jit(solution)/shard_map/ppermute | solution.py:17
  120.4 63.8 %collective-permute-start.34 = (bf16[3,192,768]{2,1,0:T(8,128)(2,1)}, bf16[3,192,768]{2,1,0:T(8,128)(2,1)}, u32[]{:S(2)}, u32[]{:S(2)}) collective-permute-start(bf16[3,192,768]{2,1,0:T(8,128)(2,1)} %get-tuple-element.22.refs_0_), channel_id=1, source_target_pairs={{0,8},{4,12},{8,0},{12,4},{1,9},{5,13},{9,1},{13,5},{2,10},{6,14},... | collective-permute-start | bytes 2654216 | tf_op jit(solution)/shard_map/ppermute | solution.py:17
  122.0 23.3 %collective-permute-start.12 = (bf16[192,256]{1,0:T(8,128)(2,1)S(1)}, bf16[192,256]{1,0:T(8,128)(2,1)S(1)}, u32[]{:S(2)}, u32[]{:S(2)}) collective-permute-start(bf16[192,256]{1,0:T(8,128)(2,1)S(1)} %fusion.10), channel_id=1, source_target_pairs={{0,8},{4,12},{8,0},{12,4},{1,9},{5,13},{9,1},{13,5},{2,10},{6,14},... | collective-permute-start | bytes 294920 | tf_op jit(solution)/shard_map/ppermute | solution.py:17
  122.8 26.2 %collective-permute-start.4 = (bf16[192,512]{1,0:T(8,128)(2,1)S(1)}, bf16[192,512]{1,0:T(8,128)(2,1)S(1)}, u32[]{:S(2)}, u32[]{:S(2)}) collective-permute-start(bf16[192,512]{1,0:T(8,128)(2,1)S(1)} %fusion.7), channel_id=1, source_target_pairs={{0,8},{4,12},{8,0},{12,4},{1,9},{5,13},{9,1},{13,5},{2,10},{6,14},... | collective-permute-start | bytes 589832 | tf_op jit(solution)/shard_map/ppermute | solution.py:17
  148.5 13.5 %collective-permute-start.14 = (bf16[192,256]{1,0:T(8,128)(2,1)S(1)}, bf16[192,256]{1,0:T(8,128)(2,1)S(1)}, u32[]{:S(2)}, u32[]{:S(2)}) collective-permute-start(bf16[192,256]{1,0:T(8,128)(2,1)S(1)} %fusion.9), channel_id=1, source_target_pairs={{0,2},{1,3},{2,0},{3,1},{4,6},{5,7},{6,4},{7,5},{8,10},{9,11},{10,... | collective-permute-start | bytes 294920 | tf_op jit(solution)/shard_map/ppermute | solution.py:17
  184.2 35.0 %collective-permute-start.37 = (bf16[3,192,768]{2,1,0:T(8,128)(2,1)}, bf16[3,192,768]{2,1,0:T(8,128)(2,1)}, u32[]{:S(2)}, u32[]{:S(2)}) collective-permute-start(bf16[3,192,768]{2,1,0:T(8,128)(2,1)} %get-tuple-element.23.refs_0_), channel_id=1, source_target_pairs={{0,8},{4,12},{8,0},{12,4},{1,9},{5,13},{9,1},{13,5},{2,10},{6,14},... | collective-permute-start | bytes 2654216 | tf_op jit(solution)/shard_map/ppermute | solution.py:17
  190.0 22.6 %collective-permute-start.22 = (bf16[192,768]{1,0:T(8,128)(2,1)S(1)}, bf16[192,768]{1,0:T(8,128)(2,1)}, u32[]{:S(2)}, u32[]{:S(2)}) collective-permute-start(bf16[192,768]{1,0:T(8,128)(2,1)S(1)} %get-tuple-element.37.refs_0_), channel_id=1, source_target_pairs={{0,8},{4,12},{8,0},{12,4},{1,9},{5,13},{9,1},{13,5},{2,10},{6,14},... | collective-permute-start | bytes 884744 | tf_op jit(solution)/shard_map/ppermute | solution.py:17
  190.5 39.0 %collective-permute-start.32 = (bf16[3,192,768]{2,1,0:T(8,128)(2,1)}, bf16[3,192,768]{2,1,0:T(8,128)(2,1)}, u32[]{:S(2)}, u32[]{:S(2)}) collective-permute-start(bf16[3,192,768]{2,1,0:T(8,128)(2,1)} %collective-permute-done.31.refs_2_), channel_id=1, source_target_pairs={{0,4},{4,0},{8,12},{12,8},{1,5},{5,1},{9,13},{13,9},{2,6},{6,2},{1... | collective-permute-start | bytes 2654216 | tf_op jit(solution)/shard_map/ppermute | solution.py:17
  192.5 26.2 %collective-permute-start.21 = (bf16[192,768]{1,0:T(8,128)(2,1)S(1)}, bf16[192,768]{1,0:T(8,128)(2,1)S(1)}, u32[]{:S(2)}, u32[]{:S(2)}) collective-permute-start(bf16[192,768]{1,0:T(8,128)(2,1)S(1)} %get-tuple-element.37.refs_0_), channel_id=1, source_target_pairs={{0,4},{4,0},{8,12},{12,8},{1,5},{5,1},{9,13},{13,9},{2,6},{6,2},{1... | collective-permute-start | bytes 884744 | tf_op jit(solution)/shard_map/ppermute | solution.py:17
  218.2 31.1 %collective-permute-start.33 = (bf16[3,192,768]{2,1,0:T(8,128)(2,1)}, bf16[3,192,768]{2,1,0:T(8,128)(2,1)}, u32[]{:S(2)}, u32[]{:S(2)}) collective-permute-start(bf16[3,192,768]{2,1,0:T(8,128)(2,1)} %get-tuple-element.22.refs_0_), channel_id=1, source_target_pairs={{0,4},{4,0},{8,12},{12,8},{1,5},{5,1},{9,13},{13,9},{2,6},{6,2},{1... | collective-permute-start | bytes 2654216 | tf_op jit(solution)/shard_map/ppermute | solution.py:17
  218.7 34.1 %collective-permute-start.36 = (bf16[3,192,768]{2,1,0:T(8,128)(2,1)}, bf16[3,192,768]{2,1,0:T(8,128)(2,1)}, u32[]{:S(2)}, u32[]{:S(2)}) collective-permute-start(bf16[3,192,768]{2,1,0:T(8,128)(2,1)} %get-tuple-element.23.refs_0_), channel_id=1, source_target_pairs={{0,4},{4,0},{8,12},{12,8},{1,5},{5,1},{9,13},{13,9},{2,6},{6,2},{1... | collective-permute-start | bytes 2654216 | tf_op jit(solution)/shard_map/ppermute | solution.py:17
  218.8 30.5 %collective-permute-start.35 = (bf16[3,192,768]{2,1,0:T(8,128)(2,1)}, bf16[3,192,768]{2,1,0:T(8,128)(2,1)}, u32[]{:S(2)}, u32[]{:S(2)}) collective-permute-start(bf16[3,192,768]{2,1,0:T(8,128)(2,1)} %collective-permute-done.34.refs_2_), channel_id=1, source_target_pairs={{0,4},{4,0},{8,12},{12,8},{1,5},{5,1},{9,13},{13,9},{2,6},{6,2},{1... | collective-permute-start | bytes 2654216 | tf_op jit(solution)/shard_map/ppermute | solution.py:17
  219.2 33.5 %collective-permute-start.38 = (bf16[3,192,768]{2,1,0:T(8,128)(2,1)}, bf16[3,192,768]{2,1,0:T(8,128)(2,1)}, u32[]{:S(2)}, u32[]{:S(2)}) collective-permute-start(bf16[3,192,768]{2,1,0:T(8,128)(2,1)} %collective-permute-done.37.refs_2_), channel_id=1, source_target_pairs={{0,4},{4,0},{8,12},{12,8},{1,5},{5,1},{9,13},{13,9},{2,6},{6,2},{1... | collective-permute-start | bytes 2654216 | tf_op jit(solution)/shard_map/ppermute | solution.py:17
  (38 other events, 521.1 us)

commit v2 on v0

v2 whole, which is shorter than its diff:
```python
import functools

import jax
import jax.numpy as jnp
from jax import lax
from jax.experimental import pallas as pl
from jax.experimental.pallas import tpu as pltpu
from jax.sharding import PartitionSpec as P

TILE = 128
F32, BF16 = jnp.float32, jnp.bfloat16
VMEM_LIMIT = 40 * 1024 * 1024


def swap(value, axis, offset):
    size = lax.axis_size(axis)
    return lax.ppermute(value, axis, [(i, i ^ offset) for i in range(size)])


def after(value, *earlier):
    return lax.optimization_barrier((value, *earlier))[0]


def dot(a, b, dims=((1,), (0,))):
    return lax.dot_general(a, b, (dims, ((), ())), preferred_element_type=F32)


def call(kernel, name, grid, in_specs, out_specs, out_shape, scratch, flops, nbytes, prefetch, args):
    return pl.pallas_call(
        kernel,
        grid_spec=pltpu.PrefetchScalarGridSpec(
            num_scalar_prefetch=prefetch,
            grid=grid,
            in_specs=in_specs,
            out_specs=out_specs,
            scratch_shapes=scratch,
        ),
        out_shape=out_shape,
        name=name,
        compiler_params=pltpu.CompilerParams(vmem_limit_bytes=VMEM_LIMIT),
        cost_estimate=pl.CostEstimate(flops=1000, bytes_accessed=1000, transcendentals=0),
    )(*args)


def keep_columns(shape, first, count):
    return lax.broadcasted_iota(jnp.int32, shape, 1) + first < count * TILE


def whole(shape):
    return pl.BlockSpec(shape, lambda k, *s: (0,) * len(shape))


def group(size, shape, column=0, first=0):
    return pl.BlockSpec((size, *shape), lambda k, *s: (k + first, 0, column))


def sizes(mesh_rows, width):
    n, n_sec = lax.axis_size("env"), lax.axis_size("sec")
    return n, n_sec, n // 2, width // (n * n_sec)


def place(me, m_core, m_sec, m_y, n_sec, n_y, piece):
    core, y = me[0] & 1, me[0] >> 1
    at = (((core ^ m_core) * n_sec + (me[1] ^ m_sec)) * n_y + (y ^ m_y)) * piece
    return pl.multiple_of(at, piece)


def fetch(per, ref, buffer, rows, sems):
    copies = []
    for k in range(ref.shape[0] // per):
        at = pl.ds(k * per, per)
        copies.append(pltpu.make_async_copy(ref.at[at], buffer.at[at, rows], sems.at[k]))
        copies[-1].start()
    return copies


def absorb_kernel(n, n_sec, piece, per, me, counts, c_ref, *refs):
    e_refs, p_ref = refs[:n], refs[n]
    enl_ref, keep_ref, send_ref, held, p_held, enl, acc, sems, out_sems = refs[n + 1 :]
    n_y = n // 2
    slices, rows, width = p_ref.shape
    copies = [
        fetch(per, e_refs[m], held, pl.ds(m * rows, rows), sems.at[m]) for m in range(n)
    ]
    p_copies = fetch(per, p_ref, p_held, pl.ds(0, rows), sems.at[n])
    stores = []
    for k in range(slices // per):
        for m in range(n):
            copies[m][k].wait()
        for i in range(k * per, k * per + per):
            x = dot(c_ref[...], held[i])
            enl[i] = jnp.where(keep_columns(x.shape, 0, counts[i]), x, 0.0).astype(BF16)
        at = pl.ds(k * per, per)
        stores.append(pltpu.make_async_copy(enl.at[at], enl_ref.at[at], out_sems.at[k]))
        stores[-1].start()
    for copy in p_copies:
        copy.wait()
    half = width // 2
    for first in (0, half):
        acc[first : first + half, :] = dot(
            p_held[:, :, first : first + half].reshape(slices * rows, half),
            enl[...].reshape(slices * rows, width),
            ((0,), (0,)),
        )
    if piece % 16:
        keep_ref[...] = acc[...]
        send_ref[...] = acc[...].astype(BF16)
    else:
        for m_sec in range(n_sec):
            for m_y in range(n_y):
                at = (m_sec * n_y + m_y) * piece
                for m_core, ref in ((0, keep_ref), (1, send_ref)):
                    part = acc[pl.ds(place(me, m_core, m_sec, m_y, n_sec, n_y, piece), piece), :]
                    ref[at : at + piece] = part.astype(ref.dtype)
    for store in stores:
        store.wait()


SCALARS = pl.BlockSpec(memory_space=pltpu.SMEM)
ARRAY = pl.BlockSpec(memory_space=pltpu.VMEM)
FAR = pl.BlockSpec(memory_space=pl.ANY)


def at_once(kernel, name, out_shape, out_specs, scratch, scalars, near, far):
    return pl.pallas_call(
        kernel,
        in_specs=[SCALARS] * len(scalars) + [ARRAY] * len(near) + [FAR] * len(far),
        out_specs=out_specs,
        out_shape=out_shape,
        scratch_shapes=scratch,
        name=name,
        compiler_params=pltpu.CompilerParams(vmem_limit_bytes=VMEM_LIMIT),
        cost_estimate=pl.CostEstimate(flops=1000, bytes_accessed=1000, transcendentals=0),
    )(*scalars, *near, *far)


def absorb(me, counts, c_parts, e_blocks, projectors):
    slices, rows, width = projectors.shape
    n, n_sec, n_y, piece = sizes(rows, width)
    per = 3 if slices % 3 == 0 else 1
    half = (width if piece % 16 else width // 2, width)
    held = (slices, rows, width)
    enlarged, keep, send = at_once(
        functools.partial(absorb_kernel, n, n_sec, piece, per),
        "absorb",
        [
            jax.ShapeDtypeStruct(held, BF16),
            jax.ShapeDtypeStruct(half, F32),
            jax.ShapeDtypeStruct(half, BF16),
        ],
        [FAR, ARRAY, ARRAY],
        [
            pltpu.VMEM((slices, width, width), BF16),
            pltpu.VMEM(held, BF16),
            pltpu.VMEM(held, BF16),
            pltpu.VMEM((width, width), F32),
            pltpu.SemaphoreType.DMA((n + 1, slices // per)),
            pltpu.SemaphoreType.DMA((slices // per,)),
        ],
        (me, counts),
        (c_parts,),
        (*e_blocks, projectors),
    )
    if piece % 16:
        keep = relative(keep, me, n_sec, n_y)[0]
        send = relative(send, me, n_sec, n_y)[1]
    shape = (n_sec, n_y * piece, width)
    return enlarged, keep.reshape(shape), send.reshape(shape)


def relative(value, me, n_sec, n_y):
    rows, cols = value.shape
    value = value.reshape(2, n_sec, n_y, rows // (2 * n_sec * n_y), cols)
    value = jnp.take(value, jnp.arange(2) ^ (me[0] & 1), axis=0)
    value = jnp.take(value, jnp.arange(n_sec) ^ me[1], axis=1)
    return jnp.take(value, jnp.arange(n_y) ^ (me[0] >> 1), axis=2).reshape(2, rows // 2, cols)


class Order:
    def __init__(self):
        self.last = None

    def __call__(self, step, *args):
        if self.last is not None:
            args = lax.optimization_barrier((*args, self.last))[:-1]
        out = step(*args)
        self.last = jax.tree.leaves(out)[0]
        return out


def add_core(keep, arrived):
    total = keep + arrived.astype(F32)
    return total.astype(BF16), total[0]


def add_sec(total, *arrived):
    for block in arrived:
        total = total + block.astype(F32)
    total = total.reshape(lax.axis_size("env") // 2, -1, total.shape[-1])
    return total.astype(BF16), total[0]


def add_chips(total, *arrived):
    for block in arrived:
        total = total + block.astype(F32)
    return total.astype(BF16)


def join(*blocks):
    return jnp.concatenate(blocks, axis=0)


def to_sec(blocks):
    return [swap(blocks[m], "sec", m) for m in range(1, lax.axis_size("sec"))]


def to_chips(blocks):
    return [swap(blocks[m], "env", 2 * m) for m in range(1, lax.axis_size("env") // 2)]


def all_chips(block):
    return [block] + to_chips([block] * (lax.axis_size("env") // 2))


def all_sec(block):
    return [block] + to_sec([block] * lax.axis_size("sec"))


def gradient_kernel(n, n_sec, piece, rows, me, *refs):
    cot_refs, blocks = refs[:n], refs[n : n + 2 * n_sec]
    g_ref, own_ref, full, cot_ref = refs[n + 2 * n_sec :]
    width = full.shape[0]
    n_y = n // 2
    for m in range(n):
        to = pl.multiple_of((me[0] ^ m) * rows, rows)
        cot_ref[pl.ds(to, rows), :] = cot_refs[m][0]
    for m_core in range(2):
        for m_sec in range(n_sec):
            block = blocks[m_core * n_sec + m_sec]
            if piece % 16:
                at = (m_core * n_sec + m_sec) * n_y * piece
                full[at : at + n_y * piece] = block[...]
                continue
            for m_y in range(n_y):
                to = place(me, m_core, m_sec, m_y, n_sec, n_y, piece)
                full[pl.ds(to, piece), :] = block[m_y * piece : (m_y + 1) * piece]
    step = 16
    zero = jnp.zeros((step, width), F32)

    def add(i, sums):
        at = pl.ds(pl.multiple_of(i * step, step), step)
        x, c = full[at, :].astype(F32), cot_ref[at, :].astype(F32)
        return sums[0] + x * x, sums[1] + c * x

    norm_sq, cross = lax.fori_loop(0, width // step, add, (zero, zero), unroll=2)
    norm_sq = jnp.sum(norm_sq, keepdims=True)
    cross = jnp.sum(cross, keepdims=True)
    scale = width / jnp.sqrt(norm_sq)
    ratio = scale * cross * scale / (width * width)

    def write(i, _):
        at = pl.ds(pl.multiple_of(i * step, step), step)
        x, c = full[at, :].astype(F32), cot_ref[at, :].astype(F32)
        g_ref[at, :] = (scale * (c - x * ratio)).astype(BF16)
        return _

    lax.fori_loop(0, width // step, write, 0, unroll=2)
    own = full[pl.ds(pl.multiple_of(me[0] * rows, rows), rows), :]
    own_ref[...] = own.astype(F32) * scale


def gradient(me, rows, cots, at, halves):
    width = cots[0].shape[2]
    n, n_sec, n_y, piece = sizes(rows, width)
    return call(
        functools.partial(gradient_kernel, n, n_sec, piece, rows),
        "gradient",
        (1,),
        [pl.BlockSpec((1, rows, width), lambda k, *s: (at, 0, 0))] * n
        + [whole(h.shape) for h in halves],
        [whole((width, width)), whole((rows, width))],
        [jax.ShapeDtypeStruct((width, width), BF16), jax.ShapeDtypeStruct((rows, width), F32)],
        [pltpu.VMEM((width, width), BF16)] * 2,
        8 * width * width,
        10 * width * width,
        1,
        (me, *cots, *halves),
    )


def corner_kernel(n, n_sec, per, me, counts, g_ref, p_ref, *refs):
    e_refs, (out, held, p_held, grad, acc, sems) = refs[:n], refs[n:]
    slices, rows, width = p_ref.shape
    cols = width // n_sec
    p_copies = fetch(per, p_ref, p_held, pl.ds(0, rows), sems.at[n])
    copies = [
        fetch(per, e_refs[m], held, pl.ds(m * rows, rows), sems.at[m]) for m in range(n)
    ]
    for k in range(slices // per):
        p_copies[k].wait()
        x = dot(p_held[k * per : k * per + per].reshape(per * rows, width), g_ref[...])
        for i in range(per):
            part = x[i * rows : (i + 1) * rows]
            keep = keep_columns(part.shape, 0, counts[k * per + i])
            grad[k * per + i] = jnp.where(keep, part, 0.0).astype(BF16)
    for m in range(n):
        for copy in copies[m]:
            copy.wait()
        x = None
        for k in range(slices):
            y = dot(held[k, m * rows : (m + 1) * rows], grad[k], ((1,), (1,)))
            x = y if x is None else x + y
        acc[pl.ds(pl.multiple_of((me[0] ^ m) * rows, rows), rows), :] = x
    for m in range(n_sec):
        at = pl.multiple_of((me[1] ^ m) * cols, cols)
        out[m] = acc[pl.ds(at, cols), :].astype(BF16)


def corner_part(me, counts, g, projectors, e_blocks):
    slices, rows, width = projectors.shape
    n, n_sec = lax.axis_size("env"), lax.axis_size("sec")
    held = (slices, rows, width)
    per = 3 if slices % 3 == 0 else 1
    return at_once(
        functools.partial(corner_kernel, n, n_sec, per),
        "corner_part",
        jax.ShapeDtypeStruct((n_sec, width // n_sec, rows), BF16),
        ARRAY,
        [
            pltpu.VMEM((slices, width, width), BF16),
            pltpu.VMEM(held, BF16),
            pltpu.VMEM(held, BF16),
            pltpu.VMEM((width, rows), F32),
            pltpu.SemaphoreType.DMA((n + 1, slices // per)),
        ],
        (me, counts),
        (g,),
        (projectors, *e_blocks),
    )


def early_kernel(per, counts, g_ref, enl_ref, q_ref, proj, edge):
    k = pl.program_id(0)
    for i in range(per):
        proj[i] = dot(enl_ref[i], g_ref[...], ((1,), (1,)))
    x = dot(q_ref[0], g_ref[...])
    edge[0] = jnp.where(keep_columns(x.shape, 0, counts[k]), x, 0.0)


def early_gradients(counts, g, enlarged, q):
    slices, rows, width = enlarged.shape
    steps = q.shape[0]
    per = slices // steps
    out = jax.ShapeDtypeStruct((slices, rows, width), F32)
    return call(
        functools.partial(early_kernel, per),
        "early_gradients",
        (steps,),
        [whole((width, width)), group(per, (rows, width)), group(1, (rows, width))],
        [group(per, (rows, width)), group(1, (rows, width))],
        [out, out],
        [],
        2 * slices * rows * width * width,
        6 * slices * width * rows,
        1,
        (counts, g, enlarged, q),
    )


def turn(n, c_refs, turned):
    @pl.when(pl.program_id(0) == 0)
    def _():
        for m in range(n):
            turned[m] = c_refs[m].T


def mixed(n, turned, p_refs, i):
    q = dot(turned[0], p_refs[0][i])
    for m in range(1, n):
        q = q + dot(turned[m], p_refs[m][i])
    return q.astype(BF16)


def mix_kernel(n, per, c_ref, *refs):
    p_refs, out, turned = refs[:n], refs[n], refs[n + 1]
    turn(n, c_ref, turned)
    for i in range(per):
        out[i] = mixed(n, turned, p_refs, i)


def mix(c_cols, p_blocks, slices):
    n, rows = c_cols.shape[:2]
    width = p_blocks[0].shape[2]
    return call(
        functools.partial(mix_kernel, n, slices),
        "mix",
        (1,),
        [whole(c_cols.shape)] + [group(slices, (rows, width))] * n,
        group(slices, (rows, width)),
        jax.ShapeDtypeStruct((slices, rows, width), BF16),
        [pltpu.VMEM(c_cols.shape, BF16)],
        2 * slices * rows * width * width,
        2 * slices * width * (width + rows),
        0,
        (c_cols, *p_blocks),
    )


def late_edge_kernel(n, first, per, counts, g_ref, c_ref, *refs):
    p_refs, out, turned = refs[:n], refs[-2], refs[-1]
    k = pl.program_id(0)
    turn(n, c_ref, turned)
    for i in range(per):
        x = dot(mixed(n, turned, p_refs, i), g_ref[...])
        keep = keep_columns(x.shape, 0, counts[first + k * per + i])
        out[i] = jnp.where(keep, x, 0.0)


def late_edge_gradient(result, shape, counts, g, c_cols, p_blocks, first):
    n, rows = c_cols.shape[:2]
    slices, _, width = p_blocks[0].shape
    per = 3 if slices % 3 == 0 else 1
    return into(
        functools.partial(late_edge_kernel, n, first, per),
        "late_edge_gradient",
        result,
        shape,
        first,
        slices,
        [whole((width, width)), whole(c_cols.shape)] + [group(per, (rows, width))] * n,
        [pltpu.VMEM(c_cols.shape, BF16)],
        (counts, g, c_cols, *p_blocks),
        per,
    )


def into(kernel, name, result, shape, first, slices, in_specs, scratch, args, per):
    aliases = {}
    if result is not None:
        aliases = {len(args): 0}
        in_specs = in_specs + [pl.BlockSpec(memory_space=pl.ANY)]
        args = (*args, result)
    return pl.pallas_call(
        kernel,
        grid_spec=pltpu.PrefetchScalarGridSpec(
            num_scalar_prefetch=1,
            grid=(slices // per,),
            in_specs=in_specs,
            out_specs=group(per, shape[1:], 0, first // per),
            scratch_shapes=scratch,
        ),
        out_shape=jax.ShapeDtypeStruct(shape, F32),
        input_output_aliases=aliases,
        name=name,
        compiler_params=pltpu.CompilerParams(vmem_limit_bytes=VMEM_LIMIT),
        cost_estimate=pl.CostEstimate(flops=1000, bytes_accessed=1000, transcendentals=0),
    )(*args)


def cotangent_order(*blocks):
    n_sec, s = lax.axis_size("sec"), lax.axis_index("sec")
    ordered = []
    for q in range(n_sec):
        block = blocks[0]
        for m in range(1, n_sec):
            block = jnp.where((s ^ m) == q, blocks[m], block)
        ordered.append(block)
    return jnp.concatenate(ordered, axis=1)


def per_device(corner, edges, projectors, tile_counts, cotangent):
    n, n_sec = lax.axis_size("env"), lax.axis_size("sec")
    e, s = lax.axis_index("env"), lax.axis_index("sec")
    slices, rows, width = edges.shape
    cols = cotangent.shape[1]
    piece = width // (n * n_sec)
    me = jnp.stack([e, s]).astype(jnp.int32)
    core, y = e & 1, e >> 1

    def from_chips(value):
        return to_chips([value] * (n // 2))

    def both_cores(arrived):
        return [b for block in arrived for b in (block, swap(block, "env", 1))]

    def barrier(value, *earlier):
        return lax.optimization_barrier((value, earlier))[0]

    far = from_chips(edges)
    cot = cotangent.astype(BF16)
    cot = cotangent_order(cot, *to_sec([cot] * n_sec))
    third = slices // 3
    pieces = [
        jnp.concatenate([projectors[:third], corner[None], cot[None]], axis=0),
        projectors[third:],
    ]
    p_blocks = [[p, swap(p, "env", 1)] for p in pieces]
    c_parts = jnp.concatenate(
        [lax.dynamic_slice_in_dim(corner, (e ^ m) * rows, rows, 1) for m in range(n)], axis=1
    )
    e_near = swap(edges, "env", 1)
    far = barrier(far, p_blocks, c_parts, e_near)
    p_far = [from_chips(barrier(pieces[0], far))]
    e_blocks = [edges, e_near, *both_cores(far)]

    order = Order()

    enlarged, keep, send = order(
        lambda *f: absorb(me, tile_counts, c_parts, f, projectors), *e_blocks)
    moved, total = order(add_core, keep, swap(send, "env", 1))
    sec = to_sec(moved)
    total = barrier(total, p_far[0])
    moved, total = order(add_sec, total, *sec)
    own = order(add_chips, total, *to_chips(moved))
    some = order(join, *all_chips(own))
    half = all_sec(some)
    p_far += [from_chips(barrier(p, some)) for p in pieces[1:]]
    p_blocks[0] += both_cores(barrier(p_far[0], some))
    cots = p_blocks[0]
    c_cols = jnp.stack(
        [lax.dynamic_slice_in_dim(p[third], e * rows, rows, 1) for p in p_blocks[0]]
    )
    q = order(lambda c: mix(c, p_blocks[0], third), c_cols)
    half = barrier(half, order.last)
    halves = half + [swap(h, "env", 1) for h in half]
    if piece % 16:
        halves = list(
            relative(jnp.concatenate(halves), me, n_sec, n // 2).reshape(2 * n_sec, -1, width))
    g, corner_new = order(lambda *h: gradient(me, rows, cots, third + 1, h), *halves)
    corner_new = lax.dynamic_slice_in_dim(corner_new, s * cols, cols, 1)

    part = order(lambda g: corner_part(me, tile_counts, g, projectors, e_blocks), g)
    moved = to_sec(part)
    proj_grad, edge_grad = order(
        lambda g: early_gradients(tile_counts, g, enlarged, q), g)
    corner_grad = order(
        lambda *b: sum((x.astype(F32) for x in b[1:]), b[0].astype(F32)).T, part[0], *moved)
    p_blocks[1] += both_cores(barrier(p_far[1], corner_grad))
    edge_grad = order(
        lambda r, *p: late_edge_gradient(
            r, (slices, rows, width), tile_counts, g, c_cols, p, third), edge_grad, *p_blocks[1])
    return (corner_new, corner_grad, edge_grad, proj_grad)


def solution(mesh):
    placed = (
        P(("sweep", "env"), None),
        P(("sweep", "sec"), "env", None),
        P(("sweep", "sec"), "env", None),
        P(("sweep", "sec")),
        P(("sweep", "env"), "sec"),
    )
    return jax.shard_map(
        per_device,
        mesh=mesh,
        in_specs=placed,
        out_specs=(
            P(("sweep", "env"), "sec"),
            P(("sweep", "env"), "sec"),
            P(("sweep", "sec"), "env", None),
            P(("sweep", "sec"), "env", None),
        ),
        check_vma=False,
    )
```

time: 418 us -> 167 us (0.40)
  waiting for transfers between devices: 219 us -> 82.3 us
  blocking collectives: 78.5 us -> 0 us
  local copies, waits for them, and re-layouts: 64.5 us -> 11.1 us
  Pallas kernels: 0 us -> 40.9 us
  matrix products: 35.9 us -> 0 us
  starting transfers between devices: 0.42 us -> 29.1 us
  between operations: 14.9 us -> 0.93 us
    unnamed x9 -> x0, waiting for transfers between devices: 98.3 us -> none
    all_gather x2 -> x0, waiting for transfers between devices: 91.9 us -> none  [the longest x1 75.2 us: per_device(): full_edges = lax.all_gather(edges, 'env', axis=1, tiled=True)]
    ppermute x0 -> x28, waiting for transfers between devices: none -> 82.3 us  [swap(): return lax.ppermute(value, axis, [(i, i ^ offset) for i in range(size)])]
    psum x2 -> x0, blocking collectives: 63.4 us -> none  [the longest x1 33.1 us: per_device(): norm_sq = lax.psum(jnp.sum(absorbed * absorbed), ('env', 'sec'))]
    unnamed x27 -> x18, local copies, waits for them, and re-layouts: 63.6 us -> 4.88 us
    pallas_call x0 -> x6, Pallas kernels: none -> 40.9 us  [the longest x2 20.3 us: at_once(): pl.pallas_call(kernel, in_specs=[SCALARS] * len(scalars) + [ARRAY] * len(...]
    dot_general x6 -> x0, matrix products: 35.9 us -> none  [the longest x1 8.7 us: per_device(): jnp.einsum('ab,kac->kbc', corner, enlarged_grad, preferred_element_type=j...]
    reduce_scatter x1 -> x0, waiting for transfers between devices: 29.3 us -> none  [per_device(): lax.psum_scatter(partial_sum.astype(jnp.bfloat16), 'sec', scatter_dimensi...]
  transfers between devices with their start and end apart: 6 -> 28, of which waited for: 5 -> 17; matrix products, arithmetic and copies ran while one was open for 13% -> 5% of each run, Pallas kernels for 0% -> 19%
where the time goes in v2:
time: 167 us; the launch traced here: 166 us
  waiting for transfers between devices  82.3 us (49%)
  Pallas kernels  40.9 us (24%)
  starting transfers between devices  29.1 us (17%)
  local copies, waits for them, and re-layouts  11.1 us (7%)
  other arithmetic  1.88 us (1%)
    ppermute x28, waiting for transfers between devices, swap(): return lax.ppermute(value, axis, [(i, i ^ offset) for i in range(size)])  82.3 us
    ppermute x28, starting transfers between devices, swap(): return lax.ppermute(value, axis, [(i, i ^ offset) for i in range(size)])  29.1 us
    pallas_call x2, Pallas kernels, at_once(): pl.pallas_call(kernel, in_specs=[SCALARS] * len(scalars) + [ARRAY] * len(...  20.3 us
    pallas_call x3, Pallas kernels, call(): pl.pallas_call(kernel, grid_spec=pltpu.PrefetchScalarGridSpec(num_scalar_...  12.1 us
    pallas_call x1, Pallas kernels, into(): pl.pallas_call(kernel, grid_spec=pltpu.PrefetchScalarGridSpec(num_scalar_...  8.51 us
    unnamed x18, local copies, waits for them, and re-layouts  4.88 us
  transfers between devices with their start and end apart: 28, of which 17 were waited for; matrix products, arithmetic and copies ran while one was open for 5% of the time, Pallas kernels for 19%

profile of v2, /device:TPU:0, one launch (start us, length us, event | category | flops | bytes accessed | tf_op | source)
XLA Modules:
  0.0 166.2 jit_solution(11749159245210392283)
XLA Ops:
  1.1 2.6 %collective-permute-start.4 = (bf16[9,192,768]{2,1,0:T(8,128)(2,1)}, bf16[9,192,768]{2,1,0:T(8,128)(2,1)}, u32[]{:S(2)}, u32[]{:S(2)}) collective-permute-start(bf16[9,192,768]{2,1,0:T(8,128)(2,1)} %refs_0_.3), channel_id=1, source_target_pairs={{0,8},{4,12},{8,0},{12,4},{1,9},{5,13},{9,1},{13,5},{2,10},{6,14},... | collective-permute-start | bytes 7962632 | tf_op jit(solution)/shard_map/ppermute | solution.py:17
  6.3 2.6 %collective-permute-start.1 = (bf16[192,192]{1,0:T(8,128)(2,1)S(1)}, bf16[192,192]{1,0:T(8,128)(2,1)S(1)}, u32[]{:S(2)}, u32[]{:S(2)}) collective-permute-start(bf16[192,192]{1,0:T(8,128)(2,1)S(1)} %convert_element_type.40), channel_id=1, source_target_pairs={{0,2},{1,3},{2,0},{3,1},{4,6},{5,7},{6,4},{7,5},{8,10},{9,11},{10,... | collective-permute-start | bytes 221192 | tf_op jit(solution)/shard_map/ppermute | solution.py:17
  9.1 2.9 %slice.48.refs_0_ = bf16[6,192,768]{2,1,0:T(8,128)(2,1)} slice(bf16[9,192,768]{2,1,0:T(8,128)(2,1)} %p_ref.1), slice={[3:9], [0:192], [0:768]} | slice | bytes 3538944 | tf_op jit(solution)/shard_map/slice | solution.py:495
  12.1 4.9 %collective-permute-done.1 = bf16[192,192]{1,0:T(8,128)(2,1)S(1)} collective-permute-done((bf16[192,192]{1,0:T(8,128)(2,1)S(1)}, bf16[192,192]{1,0:T(8,128)(2,1)S(1)}, u32[]{:S(2)}, u32[]{:S(2)}) %collective-permute-start.1) | collective-permute-done | bytes 73760 | tf_op jit(solution)/shard_map/ppermute | solution.py:17
  17.8 3.0 %collective-permute-done.3.refs_1_ = bf16[5,192,768]{2,1,0:T(8,128)(2,1)} collective-permute-done((bf16[5,192,768]{2,1,0:T(8,128)(2,1)S(1)}, bf16[5,192,768]{2,1,0:T(8,128)(2,1)}, u32[]{:S(2)}, u32[]{:S(2)}) %collective-permute-start.3) | collective-permute-done | bytes 1474592 | tf_op jit(solution)/shard_map/ppermute | solution.py:17
  20.9 41.4 %collective-permute-done.4.refs_2_ = bf16[9,192,768]{2,1,0:T(8,128)(2,1)} collective-permute-done((bf16[9,192,768]{2,1,0:T(8,128)(2,1)}, bf16[9,192,768]{2,1,0:T(8,128)(2,1)}, u32[]{:S(2)}, u32[]{:S(2)}) %collective-permute-start.4) | collective-permute-done | bytes 2654240 | tf_op jit(solution)/shard_map/ppermute | solution.py:17
  64.1 3.3 %collective-permute-done.8.refs_3_ = bf16[9,192,768]{2,1,0:T(8,128)(2,1)S(1)} collective-permute-done((bf16[9,192,768]{2,1,0:T(8,128)(2,1)}, bf16[9,192,768]{2,1,0:T(8,128)(2,1)S(1)}, u32[]{:S(2)}, u32[]{:S(2)}) %collective-permute-start.8) | collective-permute-done | bytes 2654240 | tf_op jit(solution)/shard_map/ppermute | solution.py:17
  70.6 9.6 %absorb.1 = (bf16[9,192,768]{2,1,0:T(8,128)(2,1)S(1)}, f32[384,768]{1,0:T(8,128)S(1)}, bf16[384,768]{1,0:T(8,128)(2,1)S(1)}) custom-call(s32[2]{0:T(128)S(1)} %pad_add_fusion.me, s32[9]{0:T(128)S(1)} %copy-done.4, bf16[192,768]{1,0:T(8,128)(2,1)S(1)} %pad_maximum_fusion.2.c_ref, bf16[9,192,768]{2,1,0:T(8,128)(2,1)S(1)} %copy-done.1, ...), custom_call_target="tpu_custom_call" | custom-call | flops 1000 | bytes 1000 | tf_op jit(solution)/shard_map/absorb/pallas_call | solution.py:125
  80.5 1.9 %collective-permute-done.9 = bf16[4,96,768]{2,1,0:T(8,128)(2,1)S(1)} collective-permute-done((bf16[4,96,768]{2,1,0:T(8,128)(2,1)S(1)}, bf16[4,96,768]{2,1,0:T(8,128)(2,1)S(1)}, u32[]{:S(2)}, u32[]{:S(2)}) %collective-permute-start.9) | collective-permute-done | bytes 589856 | tf_op jit(solution)/shard_map/ppermute | solution.py:17
  82.5 3.9 %collective-permute-start.12 = (bf16[96,768]{1,0:T(8,128)(2,1)S(1)}, bf16[96,768]{1,0:T(8,128)(2,1)S(1)}, u32[]{:S(2)}, u32[]{:S(2)}) collective-permute-start(bf16[96,768]{1,0:T(8,128)(2,1)S(1)} %get-tuple-element.104), channel_id=1, source_target_pairs={{0,3},{1,2},{2,1},{3,0},{4,7},{5,6},{6,5},{7,4},{8,11},{9,10},{10,... | collective-permute-start | bytes 442376 | tf_op jit(solution)/shard_map/ppermute | solution.py:17
  87.1 9.9 %collective-permute-done.7.refs_2_ = bf16[5,192,768]{2,1,0:T(8,128)(2,1)S(1)} collective-permute-done((bf16[5,192,768]{2,1,0:T(8,128)(2,1)S(1)}, bf16[5,192,768]{2,1,0:T(8,128)(2,1)S(1)}, u32[]{:S(2)}, u32[]{:S(2)}) %collective-permute-start.7) | collective-permute-done | bytes 1474592 | tf_op jit(solution)/shard_map/ppermute | solution.py:17
  96.9 2.3 %collective-permute-done.11 = bf16[96,768]{1,0:T(8,128)(2,1)S(1)} collective-permute-done((bf16[96,768]{1,0:T(8,128)(2,1)S(1)}, bf16[96,768]{1,0:T(8,128)(2,1)S(1)}, u32[]{:S(2)}, u32[]{:S(2)}) %collective-permute-start.11) | collective-permute-done | bytes 147488 | tf_op jit(solution)/shard_map/ppermute | solution.py:17
  100.9 2.8 %collective-permute-done.13 = bf16[48,768]{1,0:T(8,128)(2,1)S(1)} collective-permute-done((bf16[48,768]{1,0:T(8,128)(2,1)S(1)}, bf16[48,768]{1,0:T(8,128)(2,1)S(1)}, u32[]{:S(2)}, u32[]{:S(2)}) %collective-permute-start.13) | collective-permute-done | bytes 73760 | tf_op jit(solution)/shard_map/ppermute | solution.py:17
  105.3 2.8 %collective-permute-done.14 = bf16[48,768]{1,0:T(8,128)(2,1)S(1)} collective-permute-done((bf16[48,768]{1,0:T(8,128)(2,1)S(1)}, bf16[48,768]{1,0:T(8,128)(2,1)S(1)}, u32[]{:S(2)}, u32[]{:S(2)}) %collective-permute-start.14) | collective-permute-done | bytes 73760 | tf_op jit(solution)/shard_map/ppermute | solution.py:17
  110.9 2.5 %collective-permute-start.18 = (bf16[96,768]{1,0:T(8,128)(2,1)S(1)}, bf16[96,768]{1,0:T(8,128)(2,1)S(1)}, u32[]{:S(2)}, u32[]{:S(2)}) collective-permute-start(bf16[96,768]{1,0:T(8,128)(2,1)S(1)} %constant_dynamic-update-slice_fusion.refs_4_), channel_id=1, source_target_pairs={{0,3},{1,2},{2,1},{3,0},{4,7},{5,6},{6,5},{7,4},{8,11},{9,10},{10,... | collective-permute-start | bytes 442376 | tf_op jit(solution)/shard_map/ppermute | solution.py:17
  113.5 1.9 %collective-permute-start.16 = (bf16[96,768]{1,0:T(8,128)(2,1)S(1)}, bf16[96,768]{1,0:T(8,128)(2,1)S(1)}, u32[]{:S(2)}, u32[]{:S(2)}) collective-permute-start(bf16[96,768]{1,0:T(8,128)(2,1)S(1)} %constant_dynamic-update-slice_fusion.refs_4_), channel_id=1, source_target_pairs={{0,1},{1,0},{2,3},{3,2},{4,5},{5,4},{6,7},{7,6},{8,9},{9,8},{10,11... | collective-permute-start | bytes 442376 | tf_op jit(solution)/shard_map/ppermute | solution.py:17
  115.7 2.3 %mix.1.q_ref = bf16[3,192,768]{2,1,0:T(8,128)(2,1)S(1)} custom-call(bf16[4,192,192]{2,1,0:T(8,128)(2,1)S(1)} %pad_maximum_fusion.1.c_ref, bf16[5,192,768]{2,1,0:T(8,128)(2,1)S(1)} %pad_maximum_fusion.refs_0_, bf16[5,192,768]{2,1,0:T(8,128)(2,1)} %collective-permute-done.3.refs_1_, bf16[5,192,768]{2,1,0:T(8,128)(2,1)S(1)} %collective-permute-done.7.refs_2_, ...), custom_call_target="tpu_custom_call" | custom-call | flops 1000 | bytes 1000 | tf_op jit(solution)/shard_map/mix/pallas_call | solution.py:29
  119.6 5.9 %collective-permute-done.17.refs_6_ = bf16[96,768]{1,0:T(8,128)(2,1)S(1)} collective-permute-done((bf16[96,768]{1,0:T(8,128)(2,1)S(1)}, bf16[96,768]{1,0:T(8,128)(2,1)S(1)}, u32[]{:S(2)}, u32[]{:S(2)}) %collective-permute-start.17) | collective-permute-done | bytes 147488 | tf_op jit(solution)/shard_map/ppermute | solution.py:17
  127.6 3.3 %gradient.1 = (bf16[768,768]{1,0:T(8,128)(2,1)S(1)}, f32[192,768]{1,0:T(8,128)S(1)}) custom-call(s32[2]{0:T(128)S(1)} %pad_add_fusion.me, bf16[5,192,768]{2,1,0:T(8,128)(2,1)S(1)} %pad_maximum_fusion.refs_0_, bf16[5,192,768]{2,1,0:T(8,128)(2,1)} %collective-permute-done.3.refs_1_, bf16[5,192,768]{2,1,0:T(8,128)(2,1)S(1)} %collective-permute-done.7.refs_2_, ...), custom_call_target="tpu_custom_call" | custom-call | flops 1000 | bytes 1000 | tf_op jit(solution)/shard_map/gradient/pallas_call | solution.py:29
  131.7 10.8 %corner_part.1 = bf16[4,192,192]{2,1,0:T(8,128)(2,1)S(1)} custom-call(s32[2]{0:T(128)S(1)} %pad_add_fusion.me, s32[9]{0:T(128)S(1)} %copy-done.4, bf16[768,768]{1,0:T(8,128)(2,1)S(1)} %get-tuple-element.84.g_ref, bf16[9,192,768]{2,1,0:T(8,128)(2,1)S(1)} %copy-done, bf16[9,192,768]{2,1,0:T(8,128)(2,1)S(1)} %copy-done.2, ...), custom_call_target="tpu_custom_call" | custom-call | flops 1000 | bytes 1000 | tf_op jit(solution)/shard_map/corner_part/pallas_call | solution.py:125
  142.5 2.4 %collective-permute-start.25 = (bf16[192,192]{1,0:T(8,128)(2,1)S(1)}, bf16[192,192]{1,0:T(8,128)(2,1)S(1)}, u32[]{:S(2)}, u32[]{:S(2)}) collective-permute-start(bf16[192,192]{1,0:T(8,128)(2,1)S(1)} %get-tuple-element.107), channel_id=1, source_target_pairs={{0,3},{1,2},{2,1},{3,0},{4,7},{5,6},{6,5},{7,4},{8,11},{9,10},{10,... | collective-permute-start | bytes 221192 | tf_op jit(solution)/shard_map/ppermute | solution.py:17
  145.0 2.0 %collective-permute-start.23 = (bf16[192,192]{1,0:T(8,128)(2,1)S(1)}, bf16[192,192]{1,0:T(8,128)(2,1)S(1)}, u32[]{:S(2)}, u32[]{:S(2)}) collective-permute-start(bf16[192,192]{1,0:T(8,128)(2,1)S(1)} %get-tuple-element.109), channel_id=1, source_target_pairs={{0,1},{1,0},{2,3},{3,2},{4,5},{5,4},{6,7},{7,6},{8,9},{9,8},{10,11... | collective-permute-start | bytes 221192 | tf_op jit(solution)/shard_map/ppermute | solution.py:17
  147.0 6.4 %early_gradients.1 = (f32[9,192,768]{2,1,0:T(8,128)}, f32[9,192,768]{2,1,0:T(8,128)}) custom-call(s32[9]{0:T(128)S(1)} %copy-done.4, bf16[768,768]{1,0:T(8,128)(2,1)S(1)} %get-tuple-element.84.g_ref, bf16[9,192,768]{2,1,0:T(8,128)(2,1)S(1)} %get-tuple-element.55.enl_ref, bf16[3,192,768]{2,1,0:T(8,128)(2,1)S(1)} %mix.1.q_ref), custom_call_target="tpu_custom_call" | custom-call | flops 1000 | bytes 1000 | tf_op jit(solution)/shard_map/early_gradients/pallas_call | solution.py:29
  157.7 8.5 %late_edge_gradient.1 = f32[9,192,768]{2,1,0:T(8,128)} custom-call(s32[9]{0:T(128)S(1)} %copy-done.4, bf16[768,768]{1,0:T(8,128)(2,1)S(1)} %get-tuple-element.84.g_ref, bf16[4,192,192]{2,1,0:T(8,128)(2,1)S(1)} %pad_maximum_fusion.1.c_ref, bf16[6,192,768]{2,1,0:T(8,128)(2,1)} %slice.48.refs_0_, ...), custom_call_target="tpu_custom_call", output_to_operand_aliasing={{}: (7, {})} | custom-call | flops 1000 | bytes 1000 | tf_op jit(solution)/shard_map/late_edge_gradient/pallas_call | solution.py:443
  (84 shorter events, 25.5 us)
Async XLA Ops:
  0.6 20.2 %collective-permute-start.6 = (bf16[9,192,768]{2,1,0:T(8,128)(2,1)}, bf16[9,192,768]{2,1,0:T(8,128)(2,1)}, u32[]{:S(2)}, u32[]{:S(2)}) collective-permute-start(bf16[9,192,768]{2,1,0:T(8,128)(2,1)} %refs_0_.3), channel_id=1, source_target_pairs={{0,4},{4,0},{8,12},{12,8},{1,5},{5,1},{9,13},{13,9},{2,6},{6,2},{1... | collective-permute-start | bytes 7962632 | tf_op jit(solution)/shard_map/ppermute | solution.py:17
  1.1 61.1 %collective-permute-start.4 = (bf16[9,192,768]{2,1,0:T(8,128)(2,1)}, bf16[9,192,768]{2,1,0:T(8,128)(2,1)}, u32[]{:S(2)}, u32[]{:S(2)}) collective-permute-start(bf16[9,192,768]{2,1,0:T(8,128)(2,1)} %refs_0_.3), channel_id=1, source_target_pairs={{0,8},{4,12},{8,0},{12,4},{1,9},{5,13},{9,1},{13,5},{2,10},{6,14},... | collective-permute-start | bytes 7962632 | tf_op jit(solution)/shard_map/ppermute | solution.py:17
  4.7 7.3 %collective-permute-start.2 = (bf16[192,192]{1,0:T(8,128)(2,1)S(1)}, bf16[192,192]{1,0:T(8,128)(2,1)S(1)}, u32[]{:S(2)}, u32[]{:S(2)}) collective-permute-start(bf16[192,192]{1,0:T(8,128)(2,1)S(1)} %convert_element_type.40), channel_id=1, source_target_pairs={{0,1},{1,0},{2,3},{3,2},{4,5},{5,4},{6,7},{7,6},{8,9},{9,8},{10,11... | collective-permute-start | bytes 221192 | tf_op jit(solution)/shard_map/ppermute | solution.py:17
  6.3 10.6 %collective-permute-start.1 = (bf16[192,192]{1,0:T(8,128)(2,1)S(1)}, bf16[192,192]{1,0:T(8,128)(2,1)S(1)}, u32[]{:S(2)}, u32[]{:S(2)}) collective-permute-start(bf16[192,192]{1,0:T(8,128)(2,1)S(1)} %convert_element_type.40), channel_id=1, source_target_pairs={{0,2},{1,3},{2,0},{3,1},{4,6},{5,7},{6,4},{7,5},{8,10},{9,11},{10,... | collective-permute-start | bytes 221192 | tf_op jit(solution)/shard_map/ppermute | solution.py:17
  8.9 8.1 %collective-permute-start = (bf16[192,192]{1,0:T(8,128)(2,1)S(1)}, bf16[192,192]{1,0:T(8,128)(2,1)S(1)}, u32[]{:S(2)}, u32[]{:S(2)}) collective-permute-start(bf16[192,192]{1,0:T(8,128)(2,1)S(1)} %convert_element_type.40), channel_id=1, source_target_pairs={{0,3},{1,2},{2,1},{3,0},{4,7},{5,6},{6,5},{7,4},{8,11},{9,10},{10,... | collective-permute-start | bytes 221192 | tf_op jit(solution)/shard_map/ppermute | solution.py:17
  12.0 8.9 %collective-permute-start.5 = (bf16[6,192,768]{2,1,0:T(8,128)(2,1)}, bf16[6,192,768]{2,1,0:T(8,128)(2,1)}, u32[]{:S(2)}, u32[]{:S(2)}) collective-permute-start(bf16[6,192,768]{2,1,0:T(8,128)(2,1)} %slice.48.refs_0_), channel_id=1, source_target_pairs={{0,4},{4,0},{8,12},{12,8},{1,5},{5,1},{9,13},{13,9},{2,6},{6,2},{1... | collective-permute-start | bytes 5308424 | tf_op jit(solution)/shard_map/ppermute | solution.py:17
  17.4 3.5 %collective-permute-start.3 = (bf16[5,192,768]{2,1,0:T(8,128)(2,1)S(1)}, bf16[5,192,768]{2,1,0:T(8,128)(2,1)}, u32[]{:S(2)}, u32[]{:S(2)}) collective-permute-start(bf16[5,192,768]{2,1,0:T(8,128)(2,1)S(1)} %pad_maximum_fusion.refs_0_), channel_id=1, source_target_pairs={{0,4},{4,0},{8,12},{12,8},{1,5},{5,1},{9,13},{13,9},{2,6},{6,2},{1... | collective-permute-start | bytes 4423688 | tf_op jit(solution)/shard_map/ppermute | solution.py:17
  62.2 5.2 %collective-permute-start.8 = (bf16[9,192,768]{2,1,0:T(8,128)(2,1)}, bf16[9,192,768]{2,1,0:T(8,128)(2,1)S(1)}, u32[]{:S(2)}, u32[]{:S(2)}) collective-permute-start(bf16[9,192,768]{2,1,0:T(8,128)(2,1)} %collective-permute-done.4.refs_2_), channel_id=1, source_target_pairs={{0,4},{4,0},{8,12},{12,8},{1,5},{5,1},{9,13},{13,9},{2,6},{6,2},{1... | collective-permute-start | bytes 7962632 | tf_op jit(solution)/shard_map/ppermute | solution.py:17
  62.2 34.7 %collective-permute-start.7 = (bf16[5,192,768]{2,1,0:T(8,128)(2,1)S(1)}, bf16[5,192,768]{2,1,0:T(8,128)(2,1)S(1)}, u32[]{:S(2)}, u32[]{:S(2)}) collective-permute-start(bf16[5,192,768]{2,1,0:T(8,128)(2,1)S(1)} %pad_maximum_fusion.refs_0_), channel_id=1, source_target_pairs={{0,8},{4,12},{8,0},{12,4},{1,9},{5,13},{9,1},{13,5},{2,10},{6,14},... | collective-permute-start | bytes 4423688 | tf_op jit(solution)/shard_map/ppermute | solution.py:17
  80.2 2.1 %collective-permute-start.9 = (bf16[4,96,768]{2,1,0:T(8,128)(2,1)S(1)}, bf16[4,96,768]{2,1,0:T(8,128)(2,1)S(1)}, u32[]{:S(2)}, u32[]{:S(2)}) collective-permute-start(bf16[4,96,768]{2,1,0:T(8,128)(2,1)S(1)} %bitcast.27), channel_id=1, source_target_pairs={{0,4},{4,0},{8,12},{12,8},{1,5},{5,1},{9,13},{13,9},{2,6},{6,2},{1... | collective-permute-start | bytes 1769480 | tf_op jit(solution)/shard_map/ppermute | solution.py:17
  82.5 14.4 %collective-permute-start.12 = (bf16[96,768]{1,0:T(8,128)(2,1)S(1)}, bf16[96,768]{1,0:T(8,128)(2,1)S(1)}, u32[]{:S(2)}, u32[]{:S(2)}) collective-permute-start(bf16[96,768]{1,0:T(8,128)(2,1)S(1)} %get-tuple-element.104), channel_id=1, source_target_pairs={{0,3},{1,2},{2,1},{3,0},{4,7},{5,6},{6,5},{7,4},{8,11},{9,10},{10,... | collective-permute-start | bytes 442376 | tf_op jit(solution)/shard_map/ppermute | solution.py:17
  86.4 12.8 %collective-permute-start.11 = (bf16[96,768]{1,0:T(8,128)(2,1)S(1)}, bf16[96,768]{1,0:T(8,128)(2,1)S(1)}, u32[]{:S(2)}, u32[]{:S(2)}) collective-permute-start(bf16[96,768]{1,0:T(8,128)(2,1)S(1)} %get-tuple-element.105), channel_id=1, source_target_pairs={{0,2},{1,3},{2,0},{3,1},{4,6},{5,7},{6,4},{7,5},{8,10},{9,11},{10,... | collective-permute-start | bytes 442376 | tf_op jit(solution)/shard_map/ppermute | solution.py:17
  86.4 12.8 %collective-permute-start.10 = (bf16[96,768]{1,0:T(8,128)(2,1)S(1)}, bf16[96,768]{1,0:T(8,128)(2,1)S(1)}, u32[]{:S(2)}, u32[]{:S(2)}) collective-permute-start(bf16[96,768]{1,0:T(8,128)(2,1)S(1)} %get-tuple-element.106), channel_id=1, source_target_pairs={{0,1},{1,0},{2,3},{3,2},{4,5},{5,4},{6,7},{7,6},{8,9},{9,8},{10,11... | collective-permute-start | bytes 442376 | tf_op jit(solution)/shard_map/ppermute | solution.py:17
  99.3 4.4 %collective-permute-start.13 = (bf16[48,768]{1,0:T(8,128)(2,1)S(1)}, bf16[48,768]{1,0:T(8,128)(2,1)S(1)}, u32[]{:S(2)}, u32[]{:S(2)}) collective-permute-start(bf16[48,768]{1,0:T(8,128)(2,1)S(1)} %slice.83), channel_id=1, source_target_pairs={{0,8},{4,12},{8,0},{12,4},{1,9},{5,13},{9,1},{13,5},{2,10},{6,14},... | collective-permute-start | bytes 221192 | tf_op jit(solution)/shard_map/ppermute | solution.py:17
  103.7 4.4 %collective-permute-start.14 = (bf16[48,768]{1,0:T(8,128)(2,1)S(1)}, bf16[48,768]{1,0:T(8,128)(2,1)S(1)}, u32[]{:S(2)}, u32[]{:S(2)}) collective-permute-start(bf16[48,768]{1,0:T(8,128)(2,1)S(1)} %add_convert_fusion), channel_id=1, source_target_pairs={{0,8},{4,12},{8,0},{12,4},{1,9},{5,13},{9,1},{13,5},{2,10},{6,14},... | collective-permute-start | bytes 221192 | tf_op jit(solution)/shard_map/ppermute | solution.py:17
  108.2 7.3 %collective-permute-start.15 = (bf16[5,192,768]{2,1,0:T(8,128)(2,1)S(1)}, bf16[5,192,768]{2,1,0:T(8,128)(2,1)S(1)}, u32[]{:S(2)}, u32[]{:S(2)}) collective-permute-start(bf16[5,192,768]{2,1,0:T(8,128)(2,1)S(1)} %collective-permute-done.7.refs_2_), channel_id=1, source_target_pairs={{0,4},{4,0},{8,12},{12,8},{1,5},{5,1},{9,13},{13,9},{2,6},{6,2},{1... | collective-permute-start | bytes 4423688 | tf_op jit(solution)/shard_map/ppermute | solution.py:17
  108.2 45.5 %collective-permute-start.26 = (bf16[6,192,768]{2,1,0:T(8,128)(2,1)}, bf16[6,192,768]{2,1,0:T(8,128)(2,1)}, u32[]{:S(2)}, u32[]{:S(2)}) collective-permute-start(bf16[6,192,768]{2,1,0:T(8,128)(2,1)} %slice.48.refs_0_), channel_id=1, source_target_pairs={{0,8},{4,12},{8,0},{12,4},{1,9},{5,13},{9,1},{13,5},{2,10},{6,14},... | collective-permute-start | bytes 5308424 | tf_op jit(solution)/shard_map/ppermute | solution.py:17
  110.9 8.7 %collective-permute-start.18 = (bf16[96,768]{1,0:T(8,128)(2,1)S(1)}, bf16[96,768]{1,0:T(8,128)(2,1)S(1)}, u32[]{:S(2)}, u32[]{:S(2)}) collective-permute-start(bf16[96,768]{1,0:T(8,128)(2,1)S(1)} %constant_dynamic-update-slice_fusion.refs_4_), channel_id=1, source_target_pairs={{0,3},{1,2},{2,1},{3,0},{4,7},{5,6},{6,5},{7,4},{8,11},{9,10},{10,... | collective-permute-start | bytes 442376 | tf_op jit(solution)/shard_map/ppermute | solution.py:17
  113.5 12.0 %collective-permute-start.17 = (bf16[96,768]{1,0:T(8,128)(2,1)S(1)}, bf16[96,768]{1,0:T(8,128)(2,1)S(1)}, u32[]{:S(2)}, u32[]{:S(2)}) collective-permute-start(bf16[96,768]{1,0:T(8,128)(2,1)S(1)} %constant_dynamic-update-slice_fusion.refs_4_), channel_id=1, source_target_pairs={{0,2},{1,3},{2,0},{3,1},{4,6},{5,7},{6,4},{7,5},{8,10},{9,11},{10,... | collective-permute-start | bytes 442376 | tf_op jit(solution)/shard_map/ppermute | solution.py:17
  113.5 12.0 %collective-permute-start.16 = (bf16[96,768]{1,0:T(8,128)(2,1)S(1)}, bf16[96,768]{1,0:T(8,128)(2,1)S(1)}, u32[]{:S(2)}, u32[]{:S(2)}) collective-permute-start(bf16[96,768]{1,0:T(8,128)(2,1)S(1)} %constant_dynamic-update-slice_fusion.refs_4_), channel_id=1, source_target_pairs={{0,1},{1,0},{2,3},{3,2},{4,5},{5,4},{6,7},{7,6},{8,9},{9,8},{10,11... | collective-permute-start | bytes 442376 | tf_op jit(solution)/shard_map/ppermute | solution.py:17
  142.5 10.9 %collective-permute-start.25 = (bf16[192,192]{1,0:T(8,128)(2,1)S(1)}, bf16[192,192]{1,0:T(8,128)(2,1)S(1)}, u32[]{:S(2)}, u32[]{:S(2)}) collective-permute-start(bf16[192,192]{1,0:T(8,128)(2,1)S(1)} %get-tuple-element.107), channel_id=1, source_target_pairs={{0,3},{1,2},{2,1},{3,0},{4,7},{5,6},{6,5},{7,4},{8,11},{9,10},{10,... | collective-permute-start | bytes 221192 | tf_op jit(solution)/shard_map/ppermute | solution.py:17
  145.0 8.7 %collective-permute-start.24 = (bf16[192,192]{1,0:T(8,128)(2,1)S(1)}, bf16[192,192]{1,0:T(8,128)(2,1)S(1)}, u32[]{:S(2)}, u32[]{:S(2)}) collective-permute-start(bf16[192,192]{1,0:T(8,128)(2,1)S(1)} %get-tuple-element.108), channel_id=1, source_target_pairs={{0,2},{1,3},{2,0},{3,1},{4,6},{5,7},{6,4},{7,5},{8,10},{9,11},{10,... | collective-permute-start | bytes 221192 | tf_op jit(solution)/shard_map/ppermute | solution.py:17
  145.0 8.7 %collective-permute-start.23 = (bf16[192,192]{1,0:T(8,128)(2,1)S(1)}, bf16[192,192]{1,0:T(8,128)(2,1)S(1)}, u32[]{:S(2)}, u32[]{:S(2)}) collective-permute-start(bf16[192,192]{1,0:T(8,128)(2,1)S(1)} %get-tuple-element.109), channel_id=1, source_target_pairs={{0,1},{1,0},{2,3},{3,2},{4,5},{5,4},{6,7},{7,6},{8,9},{9,8},{10,11... | collective-permute-start | bytes 221192 | tf_op jit(solution)/shard_map/ppermute | solution.py:17
  153.7 4.0 %collective-permute-start.27 = (bf16[6,192,768]{2,1,0:T(8,128)(2,1)}, bf16[6,192,768]{2,1,0:T(8,128)(2,1)S(1)}, u32[]{:S(2)}, u32[]{:S(2)}) collective-permute-start(bf16[6,192,768]{2,1,0:T(8,128)(2,1)} %collective-permute-done.26.refs_2_), channel_id=1, source_target_pairs={{0,4},{4,0},{8,12},{12,8},{1,5},{5,1},{9,13},{13,9},{2,6},{6,2},{1... | collective-permute-start | bytes 5308424 | tf_op jit(solution)/shard_map/ppermute | solution.py:17
  (13 other events, 88.0 us)

commit v3 on v2

v3 whole, which is shorter than its diff:
```python
import functools

import jax
import jax.numpy as jnp
from jax import lax
from jax.experimental import pallas as pl
from jax.experimental.pallas import tpu as pltpu
from jax.sharding import PartitionSpec as P

TILE = 128
F32, BF16 = jnp.float32, jnp.bfloat16
VMEM_LIMIT = 40 * 1024 * 1024


def swap(value, axis, offset):
    size = lax.axis_size(axis)
    return lax.ppermute(value, axis, [(i, i ^ offset) for i in range(size)])


def after(value, *earlier):
    return lax.optimization_barrier((value, *earlier))[0]


def dot(a, b, dims=((1,), (0,))):
    return lax.dot_general(a, b, (dims, ((), ())), preferred_element_type=F32)


def call(kernel, name, grid, in_specs, out_specs, out_shape, scratch, flops, nbytes, prefetch, args):
    return pl.pallas_call(
        kernel,
        grid_spec=pltpu.PrefetchScalarGridSpec(
            num_scalar_prefetch=prefetch,
            grid=grid,
            in_specs=in_specs,
            out_specs=out_specs,
            scratch_shapes=scratch,
        ),
        out_shape=out_shape,
        name=name,
        compiler_params=pltpu.CompilerParams(vmem_limit_bytes=VMEM_LIMIT),
        cost_estimate=pl.CostEstimate(flops=1000, bytes_accessed=1000, transcendentals=0),
    )(*args)


def keep_columns(shape, first, count):
    return lax.broadcasted_iota(jnp.int32, shape, 1) + first < count * TILE


def whole(shape):
    return pl.BlockSpec(shape, lambda k, *s: (0,) * len(shape))


def group(size, shape, column=0, first=0):
    return pl.BlockSpec((size, *shape), lambda k, *s: (k + first, 0, column))


def sizes(mesh_rows, width):
    n, n_sec = lax.axis_size("env"), lax.axis_size("sec")
    return n, n_sec, n // 2, width // (n * n_sec)


def place(me, m_core, m_sec, m_y, n_sec, n_y, piece):
    core, y = me[0] & 1, me[0] >> 1
    at = (((core ^ m_core) * n_sec + (me[1] ^ m_sec)) * n_y + (y ^ m_y)) * piece
    return pl.multiple_of(at, piece)


def fetch(per, ref, buffer, rows, sems):
    copies = []
    for k in range(ref.shape[0] // per):
        at = pl.ds(k * per, per)
        copies.append(pltpu.make_async_copy(ref.at[at], buffer.at[at, rows], sems.at[k]))
        copies[-1].start()
    return copies


def begin_kernel(per, c_ref, own, near, out):
    for i in range(per):
        out[i] = dot(c_ref[0], own[i]) + dot(c_ref[1], near[i])


def begin(c_parts, own, near):
    slices, rows, width = own.shape
    per = 3 if slices % 3 == 0 else 1
    return call(
        functools.partial(begin_kernel, per),
        "begin",
        (slices // per,),
        [whole(c_parts.shape)] + [group(per, (rows, width))] * 2,
        group(per, (c_parts.shape[1], width)),
        jax.ShapeDtypeStruct((slices, c_parts.shape[1], width), F32),
        [],
        0,
        0,
        0,
        (c_parts, own, near),
    )


def absorb_kernel(n, n_sec, piece, per, me, counts, c_ref, p_ref, begun, fwd, *refs):
    far_refs, (enl_ref, keep_ref, send_ref, held, enl, acc, sems, out_sems) = refs[:-8], refs[-8:]
    n_y = n // 2
    slices, rows, width = p_ref.shape
    copies = [
        fetch(per, far_refs[m], held.at[m], pl.ds(0, rows), sems.at[m]) for m in range(n - 3)
    ]
    stores = []
    for k in range(slices // per):
        at = pl.ds(k * per, per)
        for m in range(n - 3):
            copies[m][k].wait()
        for i in range(k * per, k * per + per):
            x = begun[i] + dot(c_ref[n - 1], fwd[i])
            for m in range(n - 3):
                x = x + dot(c_ref[2 + m], held[m, i])
            enl[i] = jnp.where(keep_columns(x.shape, 0, counts[i]), x, 0.0).astype(BF16)
        stores.append(pltpu.make_async_copy(enl.at[at], enl_ref.at[at], out_sems.at[k]))
        stores[-1].start()
    half = width // 2
    for first in (0, half):
        acc[first : first + half, :] = dot(
            p_ref[:, :, first : first + half].reshape(slices * rows, half),
            enl[...].reshape(slices * rows, width),
            ((0,), (0,)),
        )
    if piece % 16:
        keep_ref[...] = acc[...]
        send_ref[...] = acc[...].astype(BF16)
    else:
        for m_sec in range(n_sec):
            for m_y in range(n_y):
                at = (m_sec * n_y + m_y) * piece
                for m_core, ref in ((0, keep_ref), (1, send_ref)):
                    part = acc[pl.ds(place(me, m_core, m_sec, m_y, n_sec, n_y, piece), piece), :]
                    ref[at : at + piece] = part.astype(ref.dtype)
    for store in stores:
        store.wait()


SCALARS = pl.BlockSpec(memory_space=pltpu.SMEM)
ARRAY = pl.BlockSpec(memory_space=pltpu.VMEM)
FAR = pl.BlockSpec(memory_space=pl.ANY)


def at_once(
    kernel, name, out_shape, out_specs, scratch, scalars, near, far, aliases=None, vmem=VMEM_LIMIT, nbytes=1000
):
    return pl.pallas_call(
        kernel,
        in_specs=[SCALARS] * len(scalars) + [ARRAY] * len(near) + [FAR] * len(far),
        out_specs=out_specs,
        out_shape=out_shape,
        scratch_shapes=scratch,
        input_output_aliases=aliases or {},
        name=name,
        compiler_params=pltpu.CompilerParams(vmem_limit_bytes=vmem),
        cost_estimate=pl.CostEstimate(flops=1000, bytes_accessed=nbytes, transcendentals=0),
    )(*scalars, *near, *far)


def absorb(me, counts, c_parts, begun, e_far, projectors):
    slices, rows, width = projectors.shape
    n, n_sec, n_y, piece = sizes(rows, width)
    per = 3 if slices % 3 == 0 else 1
    half = (width if piece % 16 else width // 2, width)
    held = (slices, rows, width)
    enlarged, keep, send = at_once(
        functools.partial(absorb_kernel, n, n_sec, piece, per),
        "absorb",
        [
            jax.ShapeDtypeStruct(held, BF16),
            jax.ShapeDtypeStruct(half, F32),
            jax.ShapeDtypeStruct(half, BF16),
        ],
        [FAR, ARRAY, ARRAY],
        [
            pltpu.VMEM((n - 3, *held), BF16),
            pltpu.VMEM(held, BF16),
            pltpu.VMEM((width, width), F32),
            pltpu.SemaphoreType.DMA((n - 3, slices // per)),
            pltpu.SemaphoreType.DMA((slices // per,)),
        ],
        (me, counts),
        (c_parts, projectors, begun, e_far[-1]),
        tuple(e_far[:-1]),
        vmem=16 * 1024 * 1024,
    )
    if piece % 16:
        keep = relative(keep, me, n_sec, n_y)[0]
        send = relative(send, me, n_sec, n_y)[1]
    shape = (n_sec, n_y * piece, width)
    return enlarged, keep.reshape(shape), send.reshape(shape)


def relative(value, me, n_sec, n_y):
    rows, cols = value.shape
    value = value.reshape(2, n_sec, n_y, rows // (2 * n_sec * n_y), cols)
    value = jnp.take(value, jnp.arange(2) ^ (me[0] & 1), axis=0)
    value = jnp.take(value, jnp.arange(n_sec) ^ me[1], axis=1)
    return jnp.take(value, jnp.arange(n_y) ^ (me[0] >> 1), axis=2).reshape(2, rows // 2, cols)


class Order:
    def __init__(self):
        self.last = None

    def __call__(self, step, *args):
        if self.last is not None:
            args = lax.optimization_barrier((*args, self.last))[:-1]
        out = step(*args)
        self.last = jax.tree.leaves(out)[0]
        return out


def add_core(keep, arrived):
    total = keep + arrived.astype(F32)
    return total.astype(BF16), total[0]


def add_sec(total, *arrived):
    for block in arrived:
        total = total + block.astype(F32)
    total = total.reshape(lax.axis_size("env") // 2, -1, total.shape[-1])
    return total.astype(BF16), total[0]


def add_chips(total, *arrived):
    for block in arrived:
        total = total + block.astype(F32)
    return total.astype(BF16)


def join(*blocks):
    return jnp.concatenate(blocks, axis=0)


def to_sec(blocks):
    return [swap(blocks[m], "sec", m) for m in range(1, lax.axis_size("sec"))]


def to_chips(blocks):
    return [swap(blocks[m], "env", 2 * m) for m in range(1, lax.axis_size("env") // 2)]


def all_chips(block):
    return [block] + to_chips([block] * (lax.axis_size("env") // 2))


def all_sec(block):
    return [block] + to_sec([block] * lax.axis_size("sec"))


def gradient_kernel(n, n_sec, piece, per, slot, me, counts, *refs):
    blocks, refs = refs[: 2 * n_sec], refs[2 * n_sec :]
    p_ref, last_e, refs = refs[0], refs[1], refs[2:]
    cot_refs, far_refs, refs = refs[:n], refs[n : 2 * n - 1], refs[2 * n - 1 :]
    g_ref, own_ref, out, full, cot, held, grad, acc, sems, cot_sems = refs
    slices, rows, width = p_ref.shape
    cols = width // n_sec
    n_y = n // 2
    cot_copies = [
        pltpu.make_async_copy(cot_refs[m].at[slot], cot.at[m], cot_sems.at[m]) for m in range(n)
    ]
    for copy in cot_copies:
        copy.start()
    e_copies = [
        pltpu.make_async_copy(far_refs[m], held.at[m], sems.at[m]) for m in range(n - 1)
    ]
    for copy in e_copies:
        copy.start()
    e_refs = [*[held.at[m] for m in range(n - 1)], last_e]

    for m_core in range(2):
        for m_sec in range(n_sec):
            block = blocks[m_core * n_sec + m_sec]
            if piece % 16:
                at = (m_core * n_sec + m_sec) * n_y * piece
                full[at : at + n_y * piece] = block[...]
                continue
            for m_y in range(n_y):
                to = place(me, m_core, m_sec, m_y, n_sec, n_y, piece)
                full[pl.ds(to, piece), :] = block[m_y * piece : (m_y + 1) * piece]
    for copy in cot_copies:
        copy.wait()
    step = 16
    sums = (jnp.zeros((step, width), F32),) * 2

    def place_of(m, i):
        return pl.ds(pl.multiple_of((me[0] ^ m) * rows + i * step, step), step)

    def cot_of(m, i):
        return cot[m, pl.ds(pl.multiple_of(i * step, step), step), :].astype(F32)

    for m in range(n):

        def add(i, sums, m=m):
            x, c = full[place_of(m, i), :].astype(F32), cot_of(m, i)
            return sums[0] + x * x, sums[1] + c * x

        sums = lax.fori_loop(0, rows // step, add, sums, unroll=3)
    norm_sq = jnp.sum(sums[0], keepdims=True)
    cross = jnp.sum(sums[1], keepdims=True)
    scale = width / jnp.sqrt(norm_sq)
    ratio = scale * cross * scale / (width * width)
    for m in range(n):

        def write(i, _, m=m):
            x = full[place_of(m, i), :].astype(F32)
            g_ref[place_of(m, i), :] = (scale * (cot_of(m, i) - x * ratio)).astype(BF16)
            return _

        lax.fori_loop(0, rows // step, write, 0, unroll=3)
    own = full[pl.ds(pl.multiple_of(me[0] * rows, rows), rows), :]
    picked = own[:, :cols]
    for q in range(1, n_sec):
        picked = jnp.where(me[1] == q, own[:, q * cols : (q + 1) * cols], picked)
    own_ref[...] = picked.astype(F32) * scale

    for k in range(slices // per):
        x = dot(p_ref[k * per : k * per + per].reshape(per * rows, width), g_ref[...])
        for i in range(per):
            part = x[i * rows : (i + 1) * rows]
            keep = keep_columns(part.shape, 0, counts[k * per + i])
            grad[k * per + i] = jnp.where(keep, part, 0.0).astype(BF16)
    for copy in e_copies:
        copy.wait()
    for m in range(n):
        x = None
        for k in range(slices):
            y = dot(e_refs[m][k], grad[k], ((1,), (1,)))
            x = y if x is None else x + y
        acc[pl.ds(pl.multiple_of((me[0] ^ m) * rows, rows), rows), :] = x
    for m in range(n_sec):
        at = pl.multiple_of((me[1] ^ m) * cols, cols)
        out[m] = acc[pl.ds(at, cols), :].T.astype(BF16)


def gradient(me, counts, halves, cots, slot, projectors, e_blocks):
    slices, rows, width = projectors.shape
    n, n_sec, _, piece = sizes(rows, width)
    per = 3 if slices % 3 == 0 else 1
    cols = width // n_sec
    held = (slices, rows, width)
    return at_once(
        functools.partial(gradient_kernel, n, n_sec, piece, per, slot),
        "gradient",
        [
            jax.ShapeDtypeStruct((width, width), BF16),
            jax.ShapeDtypeStruct((rows, cols), F32),
            jax.ShapeDtypeStruct((n_sec, rows, cols), BF16),
        ],
        [ARRAY] * 3,
        [
            pltpu.VMEM((width, width), BF16),
            pltpu.VMEM((n, rows, width), BF16),
            pltpu.VMEM((n - 1, *held), BF16),
            pltpu.VMEM(held, BF16),
            pltpu.VMEM((width, rows), F32),
            pltpu.SemaphoreType.DMA((n - 1,)),
            pltpu.SemaphoreType.DMA((n,)),
        ],
        (me, counts),
        (*halves, projectors, e_blocks[-1]),
        (*cots, *e_blocks[:-1]),
        vmem=24 * 1024 * 1024,
        nbytes=20 * slices * rows * width,
    )


def early_kernel(per, first, counts, g_ref, enl_ref, q_ref, *refs):
    proj, edge = refs[-2:]
    k = pl.program_id(0)
    for i in range(per):
        proj[i] = dot(enl_ref[i], g_ref[...], ((1,), (1,)))
    x = dot(q_ref[0], g_ref[...])
    edge[0] = jnp.where(keep_columns(x.shape, 0, counts[first + k]), x, 0.0)


def early_gradients(results, counts, g, enlarged, q, first, steps):
    slices, rows, width = enlarged.shape
    per = 3 if slices % 3 == 0 else 1
    last = q.shape[0] - 1
    out = jax.ShapeDtypeStruct((slices, rows, width), F32)
    return pl.pallas_call(
        functools.partial(early_kernel, per, first),
        grid_spec=pltpu.PrefetchScalarGridSpec(
            num_scalar_prefetch=1,
            grid=(steps,),
            in_specs=[
                whole((width, width)),
                group(per, (rows, width), 0, first),
                pl.BlockSpec((1, rows, width), lambda k, *s: (jnp.minimum(k + first, last), 0, 0)),
            ]
            + [FAR] * len(results),
            out_specs=[group(per, (rows, width), 0, first), group(1, (rows, width), 0, first)],
        ),
        out_shape=[out, out],
        input_output_aliases={4 + j: j for j in range(len(results))},
        name="early_gradients",
        compiler_params=pltpu.CompilerParams(vmem_limit_bytes=24 * 1024 * 1024),
        cost_estimate=pl.CostEstimate(flops=1000, bytes_accessed=1000, transcendentals=0),
    )(counts, g, enlarged, q, *results)


def finish(n, across, begun, p_refs, i):
    y = begun[i]
    for m in range(n - 2):
        y = y + dot(across[m], p_refs[m][i])
    return y.astype(BF16)


def mix_kernel(n, slices, c_ref, begun, *refs):
    across = [c_ref[m].T for m in range(n - 2)]
    for i in range(slices):
        refs[-1][i] = finish(n, across, begun, refs, i)


def mix(c_far, begun, p_far):
    slices, rows, width = begun.shape
    return call(
        functools.partial(mix_kernel, c_far.shape[0] + 2, slices),
        "mix",
        (1,),
        [whole(c_far.shape)] + [group(slices, (rows, width))] * (1 + len(p_far)),
        group(slices, (rows, width)),
        jax.ShapeDtypeStruct((slices, rows, width), BF16),
        [],
        0,
        0,
        0,
        (c_far, begun, *p_far),
    )


def spans(slices, per):
    return [(at, min(per, slices - at)) for at in range(0, slices, per)]


def late_kernel(n, first, groups, counts, g_ref, c_ref, fwd, *refs):
    far_refs, refs = refs[: n - 2], refs[n - 2 :]
    _, out, begun, held, q, x, sems, out_sems = refs
    slices, rows, width = begun.shape
    buffers = [begun, *[held.at[m] for m in range(n - 3)]]
    copies, stores = [], []
    for k, (at, size) in enumerate(groups):
        at = pl.ds(at, size)
        copies.append([
            pltpu.make_async_copy(far_refs[j].at[at], buffers[j].at[at], sems.at[j, k])
            for j in range(n - 2)
        ])
        for copy in copies[-1]:
            copy.start()
    across = [c_ref[m].T for m in range(n - 2)]
    p_refs = [*buffers[1:], fwd]
    for k, (at, size) in enumerate(groups):
        for copy in copies[k]:
            copy.wait()
        for i in range(size):
            q[i * rows : (i + 1) * rows] = finish(n, across, begun, p_refs, at + i)
        y = dot(q[: size * rows], g_ref[...])
        for i in range(size):
            part = y[i * rows : (i + 1) * rows]
            keep = keep_columns(part.shape, 0, counts[first + at + i])
            x[at + i] = jnp.where(keep, part, 0.0)
        to = out.at[pl.ds(first + at, size)]
        stores.append(pltpu.make_async_copy(x.at[pl.ds(at, size)], to, out_sems.at[k]))
        stores[-1].start()
    for store in stores:
        store.wait()


def late_edge_gradient(result, counts, g, c_far, begun, p_far, first):
    n = c_far.shape[0] + 2
    slices, rows, width = begun.shape
    groups = spans(slices, 2)
    return at_once(
        functools.partial(late_kernel, n, first, groups),
        "late_edge_gradient",
        jax.ShapeDtypeStruct(result.shape, F32),
        FAR,
        [
            pltpu.VMEM((slices, rows, width), F32),
            pltpu.VMEM((n - 3, slices, rows, width), BF16),
            pltpu.VMEM((2 * rows, width), BF16),
            pltpu.VMEM((slices, rows, width), F32),
            pltpu.SemaphoreType.DMA((n - 2, len(groups))),
            pltpu.SemaphoreType.DMA((len(groups),)),
        ],
        (counts,),
        (g, c_far, p_far[-1]),
        (begun, *p_far[:-1], result),
        {4 + n - 2: 0},
        vmem=48 * 1024 * 1024,
    )


def cotangent_order(*blocks):
    n_sec, s = lax.axis_size("sec"), lax.axis_index("sec")
    ordered = []
    for q in range(n_sec):
        block = blocks[0]
        for m in range(1, n_sec):
            block = jnp.where((s ^ m) == q, blocks[m], block)
        ordered.append(block)
    return jnp.concatenate(ordered, axis=1)


def per_device(corner, edges, projectors, tile_counts, cotangent):
    n, n_sec = lax.axis_size("env"), lax.axis_size("sec")
    e, s = lax.axis_index("env"), lax.axis_index("sec")
    slices, rows, width = edges.shape
    cols = cotangent.shape[1]
    piece = width // (n * n_sec)
    me = jnp.stack([e, s]).astype(jnp.int32)
    core, y = e & 1, e >> 1

    def from_chips(value):
        return to_chips([value] * (n // 2))

    def both_cores(arrived):
        return [b for block in arrived for b in (block, swap(block, "env", 1))]

    def barrier(value, *earlier):
        return lax.optimization_barrier((value, earlier))[0]

    far = from_chips(edges)
    cot = cotangent.astype(BF16)
    cot = cotangent_order(cot, *to_sec([cot] * n_sec))
    early = max(slices // 3, 1)
    pieces = [
        jnp.concatenate([projectors[:early], corner[None], cot[None]], axis=0),
        projectors[early:],
    ]
    near = [swap(p, "env", 1) for p in pieces]
    c_parts = jnp.stack(
        [lax.dynamic_slice_in_dim(corner, (e ^ m) * rows, rows, 1) for m in range(n)]
    )
    e_near = swap(edges, "env", 1)
    begun = begin(c_parts, edges, e_near)

    def corner_columns(piece):
        return lax.dynamic_slice_in_dim(piece[early], e * rows, rows, 1)

    c_near = jnp.stack([corner_columns(pieces[0]).T, corner_columns(near[0]).T])
    mixing = [begin(c_near, p, q) for p, q in zip(pieces, near)]
    mixing[0] = mixing[0][:early]
    far = barrier(far, begun, mixing)
    p_far = [from_chips(barrier(pieces[0], far))]
    e_blocks = [edges, e_near, *both_cores(far)]

    order = Order()

    enlarged, keep, send = order(
        lambda *f: absorb(me, tile_counts, c_parts, begun, f, projectors), *e_blocks[2:])
    moved, total = order(add_core, keep, swap(send, "env", 1))
    sec = to_sec(moved)
    total = barrier(total, p_far[0])
    moved, total = order(add_sec, total, *sec)
    own = order(add_chips, total, *to_chips(moved))
    some = order(join, *all_chips(own))
    half = all_sec(some)
    p_far += [from_chips(barrier(p, some)) for p in pieces[1:]]
    p_far[0] = both_cores(barrier(p_far[0], some))
    cots = [pieces[0], near[0], *p_far[0]]
    c_far = jnp.stack([corner_columns(p) for p in p_far[0]])
    q = order(lambda c: mix(c, mixing[0], p_far[0]), c_far)
    half = barrier(half, order.last)
    halves = half + [swap(h, "env", 1) for h in half]
    if piece % 16:
        halves = list(
            relative(jnp.concatenate(halves), me, n_sec, n // 2).reshape(2 * n_sec, -1, width))
    g, corner_new, part = order(
        lambda *h: gradient(me, tile_counts, h, cots, early + 1, projectors, e_blocks), *halves)
    moved = to_sec(part)
    steps = slices // 3 if slices % 3 == 0 else slices
    some_steps = max(steps - 1, 1)
    results = order(
        lambda g: early_gradients((), tile_counts, g, enlarged, q, 0, some_steps), g)
    corner_grad = order(
        lambda *b: sum((x.astype(F32) for x in b[1:]), b[0].astype(F32)), part[0], *moved)
    p_far = both_cores(barrier(p_far[1], corner_grad))
    proj_grad, edge_grad = order(
        lambda *r: early_gradients(
            r, tile_counts, g, enlarged, q, some_steps, steps - some_steps), *results)
    edge_grad = order(
        lambda r, *p: late_edge_gradient(r, tile_counts, g, c_far, mixing[1], p, early),
        edge_grad, *p_far)
    return (corner_new, corner_grad, edge_grad, proj_grad)


def solution(mesh):
    placed = (
        P(("sweep", "env"), None),
        P(("sweep", "sec"), "env", None),
        P(("sweep", "sec"), "env", None),
        P(("sweep", "sec")),
        P(("sweep", "env"), "sec"),
    )
    return jax.shard_map(
        per_device,
        mesh=mesh,
        in_specs=placed,
        out_specs=(
            P(("sweep", "env"), "sec"),
            P(("sweep", "env"), "sec"),
            P(("sweep", "sec"), "env", None),
            P(("sweep", "sec"), "env", None),
        ),
        check_vma=False,
    )
```

time: 167 us -> 160 us (0.958)
  waiting for transfers between devices: 82.3 us -> 73.7 us
  local copies, waits for them, and re-layouts: 11.1 us -> 7.15 us
  other arithmetic: 1.88 us -> 5.64 us
    ppermute x28, waiting for transfers between devices: 82.3 us -> 73.7 us  [swap(): return lax.ppermute(value, axis, [(i, i ^ offset) for i in range(size)])]
    concatenate x2 -> x1, other arithmetic: 0.31 us -> 2.4 us  [per_device(): jnp.concatenate([projectors[:early], corner[None], cot[None]], axis=0)]
    pallas_call x2 -> x3, Pallas kernels: 20.3 us -> 22.4 us  [at_once(): pl.pallas_call(kernel, in_specs=[SCALARS] * len(scalars) + [ARRAY] * len(...]
    unnamed x18 -> x22, local copies, waits for them, and re-layouts: 4.88 us -> 3.35 us
    slice x6 -> x7, local copies, waits for them, and re-layouts: 3.89 us -> 2.47 us  [the longest x1 1.33 us: per_device(): projectors[early:]]
    pallas_call x3 -> x4, Pallas kernels: 12.1 us -> 11.2 us  [call(): pl.pallas_call(kernel, grid_spec=pltpu.PrefetchScalarGridSpec(num_scalar_...]
    pallas_call x1 -> x2, Pallas kernels: 8.51 us -> 8.22 us  [early_gradients(): pl.pallas_call(functools.partial(early_kernel, per, first), grid_spec=plt...]
  transfers between devices with their start and end apart: 28 -> 28, of which waited for: 17 -> 17; matrix products, arithmetic and copies ran while one was open for 5% -> 6% of each run, Pallas kernels for 19% -> 22%
where the time goes in v3:
time: 160 us; the launch traced here: 159 us
  waiting for transfers between devices  73.7 us (46%)
  Pallas kernels  41.8 us (26%)
  starting transfers between devices  29.9 us (19%)
  local copies, waits for them, and re-layouts  7.15 us (4%)
  other arithmetic  5.64 us (4%)
    ppermute x28, waiting for transfers between devices, swap(): return lax.ppermute(value, axis, [(i, i ^ offset) for i in range(size)])  73.7 us
    ppermute x28, starting transfers between devices, swap(): return lax.ppermute(value, axis, [(i, i ^ offset) for i in range(size)])  29.9 us
    pallas_call x3, Pallas kernels, at_once(): pl.pallas_call(kernel, in_specs=[SCALARS] * len(scalars) + [ARRAY] * len(...  22.4 us
    pallas_call x4, Pallas kernels, call(): pl.pallas_call(kernel, grid_spec=pltpu.PrefetchScalarGridSpec(num_scalar_...  11.2 us
    pallas_call x2, Pallas kernels, early_gradients(): pl.pallas_call(functools.partial(early_kernel, per, first), grid_spec=plt...  8.22 us
    unnamed x22, local copies, waits for them, and re-layouts  3.35 us
  transfers between devices with their start and end apart: 28, of which 17 were waited for; matrix products, arithmetic and copies ran while one was open for 6% of the time, Pallas kernels for 22%

profile of v3, /device:TPU:0, one launch (start us, length us, event | category | flops | bytes accessed | tf_op | source)
XLA Modules:
  0.0 159.3 jit_solution(6562145284608832043)
XLA Ops:
  1.2 2.6 %collective-permute-start.1 = (bf16[9,192,768]{2,1,0:T(8,128)(2,1)}, bf16[9,192,768]{2,1,0:T(8,128)(2,1)}, u32[]{:S(2)}, u32[]{:S(2)}) collective-permute-start(bf16[9,192,768]{2,1,0:T(8,128)(2,1)} %refs_14_.1), channel_id=1, source_target_pairs={{0,8},{4,12},{8,0},{12,4},{1,9},{5,13},{9,1},{13,5},{2,10},{6,14},... | collective-permute-start | bytes 7962632 | tf_op jit(solution)/shard_map/ppermute | solution.py:17
  6.4 2.6 %collective-permute-start.3 = (bf16[192,192]{1,0:T(8,128)(2,1)S(1)}, bf16[192,192]{1,0:T(8,128)(2,1)S(1)}, u32[]{:S(2)}, u32[]{:S(2)}) collective-permute-start(bf16[192,192]{1,0:T(8,128)(2,1)S(1)} %convert_element_type.40), channel_id=1, source_target_pairs={{0,2},{1,3},{2,0},{3,1},{4,6},{5,7},{6,4},{7,5},{8,10},{9,11},{10,... | collective-permute-start | bytes 221192 | tf_op jit(solution)/shard_map/ppermute | solution.py:17
  9.6 7.4 %collective-permute-done.3 = bf16[192,192]{1,0:T(8,128)(2,1)S(1)} collective-permute-done((bf16[192,192]{1,0:T(8,128)(2,1)S(1)}, bf16[192,192]{1,0:T(8,128)(2,1)S(1)}, u32[]{:S(2)}, u32[]{:S(2)}) %collective-permute-start.3) | collective-permute-done | bytes 73760 | tf_op jit(solution)/shard_map/ppermute | solution.py:17
  17.2 2.4 %pad_maximum_fusion.own.refs_10_ = bf16[5,192,768]{2,1,0:T(8,128)(2,1)} fusion(bf16[1,192,768]{2,1,0:T(8,128)(2,1)S(1)} %maximum_bitcast_fusion, bf16[1,192,768]{2,1,0:T(8,128)(2,1)} %bitcast.40, bf16[3,192,768]{2,1,0:T(8,128)(2,1)S(1)} %slice-done), kind=kLoop, calls=%fused_computation | loop fusion | flops 1474560 | bytes 2949120 | tf_op jit(solution)/shard_map/concatenate | solution.py:531
  25.5 4.1 %begin.4 = f32[5,192,768]{2,1,0:T(8,128)S(1)} custom-call(bf16[2,192,192]{2,1,0:T(8,128)(2,1)S(1)} %pad_maximum_fusion.2.c_ref, bf16[5,192,768]{2,1,0:T(8,128)(2,1)} %pad_maximum_fusion.own.refs_10_, bf16[5,192,768]{2,1,0:T(8,128)(2,1)} %collective-permute-done.5.near.refs_11_), custom_call_target="tpu_custom_call" | custom-call | flops 1000 | bytes 1000 | tf_op jit(solution)/shard_map/begin/pallas_call | solution.py:29
  29.7 2.8 %begin.5.refs_0_ = f32[6,192,768]{2,1,0:T(8,128)S(1)} custom-call(bf16[2,192,192]{2,1,0:T(8,128)(2,1)S(1)} %pad_maximum_fusion.2.c_ref, bf16[6,192,768]{2,1,0:T(8,128)(2,1)} %slice.53.own, bf16[6,192,768]{2,1,0:T(8,128)(2,1)} %collective-permute-done.6.near), custom_call_target="tpu_custom_call" | custom-call | flops 1000 | bytes 1000 | tf_op jit(solution)/shard_map/begin/pallas_call | solution.py:29
  34.3 3.6 %begin.3.begun = f32[9,192,768]{2,1,0:T(8,128)S(1)} custom-call(bf16[4,192,192]{2,1,0:T(8,128)(2,1)S(1)} %pad_maximum_fusion.1.c_ref, bf16[9,192,768]{2,1,0:T(8,128)(2,1)S(1)} %copy-done.2, bf16[9,192,768]{2,1,0:T(8,128)(2,1)} %collective-permute-done.near.refs_15_), custom_call_target="tpu_custom_call" | custom-call | flops 1000 | bytes 1000 | tf_op jit(solution)/shard_map/begin/pallas_call | solution.py:29
  37.9 24.3 %collective-permute-done.1.refs_0_.refs_16_ = bf16[9,192,768]{2,1,0:T(8,128)(2,1)} collective-permute-done((bf16[9,192,768]{2,1,0:T(8,128)(2,1)}, bf16[9,192,768]{2,1,0:T(8,128)(2,1)}, u32[]{:S(2)}, u32[]{:S(2)}) %collective-permute-start.1) | collective-permute-done | bytes 2654240 | tf_op jit(solution)/shard_map/ppermute | solution.py:17
  64.1 3.3 %collective-permute-done.7.fwd.refs_9_ = bf16[9,192,768]{2,1,0:T(8,128)(2,1)S(1)} collective-permute-done((bf16[9,192,768]{2,1,0:T(8,128)(2,1)}, bf16[9,192,768]{2,1,0:T(8,128)(2,1)S(1)}, u32[]{:S(2)}, u32[]{:S(2)}) %collective-permute-start.7) | collective-permute-done | bytes 2654240 | tf_op jit(solution)/shard_map/ppermute | solution.py:17
  67.4 6.8 %absorb.1 = (bf16[9,192,768]{2,1,0:T(8,128)(2,1)S(1)}, f32[384,768]{1,0:T(8,128)S(1)}, bf16[384,768]{1,0:T(8,128)(2,1)S(1)}) custom-call(s32[2]{0:T(128)S(1)} %pad_add_fusion.me, s32[9]{0:T(128)S(1)} %copy-done.7, bf16[4,192,192]{2,1,0:T(8,128)(2,1)S(1)} %pad_maximum_fusion.1.c_ref, bf16[9,192,768]{2,1,0:T(8,128)(2,1)S(1)} %copy-done, ...), custom_call_target="tpu_custom_call" | custom-call | flops 1000 | bytes 1000 | tf_op jit(solution)/shard_map/absorb/pallas_call | solution.py:148
  74.4 1.9 %collective-permute-done.8 = bf16[4,96,768]{2,1,0:T(8,128)(2,1)S(1)} collective-permute-done((bf16[4,96,768]{2,1,0:T(8,128)(2,1)S(1)}, bf16[4,96,768]{2,1,0:T(8,128)(2,1)S(1)}, u32[]{:S(2)}, u32[]{:S(2)}) %collective-permute-start.8) | collective-permute-done | bytes 589856 | tf_op jit(solution)/shard_map/ppermute | solution.py:17
  76.5 3.9 %collective-permute-start.12 = (bf16[96,768]{1,0:T(8,128)(2,1)S(1)}, bf16[96,768]{1,0:T(8,128)(2,1)S(1)}, u32[]{:S(2)}, u32[]{:S(2)}) collective-permute-start(bf16[96,768]{1,0:T(8,128)(2,1)S(1)} %get-tuple-element.104), channel_id=1, source_target_pairs={{0,3},{1,2},{2,1},{3,0},{4,7},{5,6},{6,5},{7,4},{8,11},{9,10},{10,... | collective-permute-start | bytes 442376 | tf_op jit(solution)/shard_map/ppermute | solution.py:17
  81.0 16.1 %collective-permute-done.9.refs_0_.refs_12_ = bf16[5,192,768]{2,1,0:T(8,128)(2,1)S(1)} collective-permute-done((bf16[5,192,768]{2,1,0:T(8,128)(2,1)}, bf16[5,192,768]{2,1,0:T(8,128)(2,1)S(1)}, u32[]{:S(2)}, u32[]{:S(2)}) %collective-permute-start.9) | collective-permute-done | bytes 1474592 | tf_op jit(solution)/shard_map/ppermute | solution.py:17
  99.1 2.6 %collective-permute-done.13 = bf16[48,768]{1,0:T(8,128)(2,1)S(1)} collective-permute-done((bf16[48,768]{1,0:T(8,128)(2,1)S(1)}, bf16[48,768]{1,0:T(8,128)(2,1)S(1)}, u32[]{:S(2)}, u32[]{:S(2)}) %collective-permute-start.13) | collective-permute-done | bytes 73760 | tf_op jit(solution)/shard_map/ppermute | solution.py:17
  103.5 2.6 %collective-permute-done.14 = bf16[48,768]{1,0:T(8,128)(2,1)S(1)} collective-permute-done((bf16[48,768]{1,0:T(8,128)(2,1)S(1)}, bf16[48,768]{1,0:T(8,128)(2,1)S(1)}, u32[]{:S(2)}, u32[]{:S(2)}) %collective-permute-start.14) | collective-permute-done | bytes 73760 | tf_op jit(solution)/shard_map/ppermute | solution.py:17
  108.0 3.6 %collective-permute-start.17 = (bf16[96,768]{1,0:T(8,128)(2,1)S(1)}, bf16[96,768]{1,0:T(8,128)(2,1)S(1)}, u32[]{:S(2)}, u32[]{:S(2)}) collective-permute-start(bf16[96,768]{1,0:T(8,128)(2,1)S(1)} %constant_dynamic-update-slice_fusion.refs_0_), channel_id=1, source_target_pairs={{0,3},{1,2},{2,1},{3,0},{4,7},{5,6},{6,5},{7,4},{8,11},{9,10},{10,... | collective-permute-start | bytes 442376 | tf_op jit(solution)/shard_map/ppermute | solution.py:17
  113.4 3.2 %collective-permute-done.17.refs_3_ = bf16[96,768]{1,0:T(8,128)(2,1)S(1)} collective-permute-done((bf16[96,768]{1,0:T(8,128)(2,1)S(1)}, bf16[96,768]{1,0:T(8,128)(2,1)S(1)}, u32[]{:S(2)}, u32[]{:S(2)}) %collective-permute-start.17) | collective-permute-done | bytes 147488 | tf_op jit(solution)/shard_map/ppermute | solution.py:17
  116.6 7.8 %collective-permute-done.16.refs_2_ = bf16[96,768]{1,0:T(8,128)(2,1)S(1)} collective-permute-done((bf16[96,768]{1,0:T(8,128)(2,1)S(1)}, bf16[96,768]{1,0:T(8,128)(2,1)S(1)}, u32[]{:S(2)}, u32[]{:S(2)}) %collective-permute-start.16) | collective-permute-done | bytes 147488 | tf_op jit(solution)/shard_map/ppermute | solution.py:17
  126.5 9.3 %gradient.1 = (bf16[768,768]{1,0:T(8,128)(2,1)S(1)}, f32[192,192]{1,0:T(8,128)}, bf16[4,192,192]{2,1,0:T(8,128)(2,1)S(1)}) custom-call(s32[2]{0:T(128)S(1)} %pad_add_fusion.me, s32[9]{0:T(128)S(1)} %copy-done.7, bf16[96,768]{1,0:T(8,128)(2,1)S(1)} %constant_dynamic-update-slice_fusion.refs_0_, bf16[96,768]{1,0:T(8,128)(2,1)S(1)} %collective-permute-done.15.refs_1_, ...), custom_call_target="tpu_custom_call" | custom-call | flops 1000 | bytes 26542080 | tf_op jit(solution)/shard_map/gradient/pallas_call | solution.py:148
  135.8 2.5 %collective-permute-start.25 = (bf16[192,192]{1,0:T(8,128)(2,1)S(1)}, bf16[192,192]{1,0:T(8,128)(2,1)S(1)}, u32[]{:S(2)}, u32[]{:S(2)}) collective-permute-start(bf16[192,192]{1,0:T(8,128)(2,1)S(1)} %get-tuple-element.107), channel_id=1, source_target_pairs={{0,3},{1,2},{2,1},{3,0},{4,7},{5,6},{6,5},{7,4},{8,11},{9,10},{10,... | collective-permute-start | bytes 221192 | tf_op jit(solution)/shard_map/ppermute | solution.py:17
  138.4 1.9 %collective-permute-start.23 = (bf16[192,192]{1,0:T(8,128)(2,1)S(1)}, bf16[192,192]{1,0:T(8,128)(2,1)S(1)}, u32[]{:S(2)}, u32[]{:S(2)}) collective-permute-start(bf16[192,192]{1,0:T(8,128)(2,1)S(1)} %get-tuple-element.109), channel_id=1, source_target_pairs={{0,1},{1,0},{2,3},{3,2},{4,5},{5,4},{6,7},{7,6},{8,9},{9,8},{10,11... | collective-permute-start | bytes 221192 | tf_op jit(solution)/shard_map/ppermute | solution.py:17
  140.3 4.9 %early_gradients.2 = (f32[9,192,768]{2,1,0:T(8,128)}, f32[9,192,768]{2,1,0:T(8,128)}) custom-call(s32[9]{0:T(128)S(1)} %copy-done.7, bf16[768,768]{1,0:T(8,128)(2,1)S(1)} %get-tuple-element.86.g_ref, bf16[9,192,768]{2,1,0:T(8,128)(2,1)S(1)} %copy-done.4, bf16[3,192,768]{2,1,0:T(8,128)(2,1)S(1)} %mix.1.q_ref), custom_call_target="tpu_custom_call" | custom-call | flops 1000 | bytes 1000 | tf_op jit(solution)/shard_map/early_gradients/pallas_call | solution.py:384
  147.7 3.3 %early_gradients.3 = (f32[9,192,768]{2,1,0:T(8,128)}, f32[9,192,768]{2,1,0:T(8,128)}) custom-call(s32[9]{0:T(128)S(1)} %copy-done.7, bf16[768,768]{1,0:T(8,128)(2,1)S(1)} %get-tuple-element.86.g_ref, bf16[9,192,768]{2,1,0:T(8,128)(2,1)S(1)} %copy-done.4, bf16[3,192,768]{2,1,0:T(8,128)(2,1)S(1)} %mix.1.q_ref, ...), custom_call_target="tpu_custom_call", output_to_operand_aliasing={{0}: (4, {}), {1}: (5, {})} | custom-call | flops 1000 | bytes 1000 | tf_op jit(solution)/shard_map/early_gradients/pallas_call | solution.py:384
  152.8 6.4 %late_edge_gradient.1 = f32[9,192,768]{2,1,0:T(8,128)} custom-call(s32[9]{0:T(128)S(1)} %copy-done.7, bf16[768,768]{1,0:T(8,128)(2,1)S(1)} %get-tuple-element.86.g_ref, bf16[2,192,192]{2,1,0:T(8,128)(2,1)S(1)} %pad_maximum_fusion.3.c_ref, bf16[6,192,768]{2,1,0:T(8,128)(2,1)S(1)} %collective-permute-done.27.fwd, ...), custom_call_target="tpu_custom_call", output_to_operand_aliasing={{}: (6, {})} | custom-call | flops 1000 | bytes 1000 | tf_op jit(solution)/shard_map/late_edge_gradient/pallas_call | solution.py:148
  (93 shorter events, 28.4 us)
Async XLA Ops:
  0.6 33.7 %collective-permute-start = (bf16[9,192,768]{2,1,0:T(8,128)(2,1)}, bf16[9,192,768]{2,1,0:T(8,128)(2,1)}, u32[]{:S(2)}, u32[]{:S(2)}) collective-permute-start(bf16[9,192,768]{2,1,0:T(8,128)(2,1)} %refs_14_.1), channel_id=1, source_target_pairs={{0,4},{4,0},{8,12},{12,8},{1,5},{5,1},{9,13},{13,9},{2,6},{6,2},{1... | collective-permute-start | bytes 7962632 | tf_op jit(solution)/shard_map/ppermute | solution.py:17
  1.2 61.1 %collective-permute-start.1 = (bf16[9,192,768]{2,1,0:T(8,128)(2,1)}, bf16[9,192,768]{2,1,0:T(8,128)(2,1)}, u32[]{:S(2)}, u32[]{:S(2)}) collective-permute-start(bf16[9,192,768]{2,1,0:T(8,128)(2,1)} %refs_14_.1), channel_id=1, source_target_pairs={{0,8},{4,12},{8,0},{12,4},{1,9},{5,13},{9,1},{13,5},{2,10},{6,14},... | collective-permute-start | bytes 7962632 | tf_op jit(solution)/shard_map/ppermute | solution.py:17
  4.7 4.9 %collective-permute-start.4 = (bf16[192,192]{1,0:T(8,128)(2,1)S(1)}, bf16[192,192]{1,0:T(8,128)(2,1)S(1)}, u32[]{:S(2)}, u32[]{:S(2)}) collective-permute-start(bf16[192,192]{1,0:T(8,128)(2,1)S(1)} %convert_element_type.40), channel_id=1, source_target_pairs={{0,1},{1,0},{2,3},{3,2},{4,5},{5,4},{6,7},{7,6},{8,9},{9,8},{10,11... | collective-permute-start | bytes 221192 | tf_op jit(solution)/shard_map/ppermute | solution.py:17
  6.4 10.6 %collective-permute-start.3 = (bf16[192,192]{1,0:T(8,128)(2,1)S(1)}, bf16[192,192]{1,0:T(8,128)(2,1)S(1)}, u32[]{:S(2)}, u32[]{:S(2)}) collective-permute-start(bf16[192,192]{1,0:T(8,128)(2,1)S(1)} %convert_element_type.40), channel_id=1, source_target_pairs={{0,2},{1,3},{2,0},{3,1},{4,6},{5,7},{6,4},{7,5},{8,10},{9,11},{10,... | collective-permute-start | bytes 221192 | tf_op jit(solution)/shard_map/ppermute | solution.py:17
  8.9 8.1 %collective-permute-start.2 = (bf16[192,192]{1,0:T(8,128)(2,1)S(1)}, bf16[192,192]{1,0:T(8,128)(2,1)S(1)}, u32[]{:S(2)}, u32[]{:S(2)}) collective-permute-start(bf16[192,192]{1,0:T(8,128)(2,1)S(1)} %convert_element_type.40), channel_id=1, source_target_pairs={{0,3},{1,2},{2,1},{3,0},{4,7},{5,6},{6,5},{7,4},{8,11},{9,10},{10,... | collective-permute-start | bytes 221192 | tf_op jit(solution)/shard_map/ppermute | solution.py:17
  19.6 3.6 %collective-permute-start.5 = (bf16[5,192,768]{2,1,0:T(8,128)(2,1)}, bf16[5,192,768]{2,1,0:T(8,128)(2,1)}, u32[]{:S(2)}, u32[]{:S(2)}) collective-permute-start(bf16[5,192,768]{2,1,0:T(8,128)(2,1)} %pad_maximum_fusion.own.refs_10_), channel_id=1, source_target_pairs={{0,4},{4,0},{8,12},{12,8},{1,5},{5,1},{9,13},{13,9},{2,6},{6,2},{1... | collective-permute-start | bytes 4423688 | tf_op jit(solution)/shard_map/ppermute | solution.py:17
  21.0 8.8 %collective-permute-start.6 = (bf16[6,192,768]{2,1,0:T(8,128)(2,1)}, bf16[6,192,768]{2,1,0:T(8,128)(2,1)}, u32[]{:S(2)}, u32[]{:S(2)}) collective-permute-start(bf16[6,192,768]{2,1,0:T(8,128)(2,1)} %slice.53.own), channel_id=1, source_target_pairs={{0,4},{4,0},{8,12},{12,8},{1,5},{5,1},{9,13},{13,9},{2,6},{6,2},{1... | collective-permute-start | bytes 5308424 | tf_op jit(solution)/shard_map/ppermute | solution.py:17
  62.2 5.2 %collective-permute-start.7 = (bf16[9,192,768]{2,1,0:T(8,128)(2,1)}, bf16[9,192,768]{2,1,0:T(8,128)(2,1)S(1)}, u32[]{:S(2)}, u32[]{:S(2)}) collective-permute-start(bf16[9,192,768]{2,1,0:T(8,128)(2,1)} %collective-permute-done.1.refs_0_.refs_16_), channel_id=1, source_target_pairs={{0,4},{4,0},{8,12},{12,8},{1,5},{5,1},{9,13},{13,9},{2,6},{6,2},{1... | collective-permute-start | bytes 7962632 | tf_op jit(solution)/shard_map/ppermute | solution.py:17
  62.2 34.9 %collective-permute-start.9 = (bf16[5,192,768]{2,1,0:T(8,128)(2,1)}, bf16[5,192,768]{2,1,0:T(8,128)(2,1)S(1)}, u32[]{:S(2)}, u32[]{:S(2)}) collective-permute-start(bf16[5,192,768]{2,1,0:T(8,128)(2,1)} %pad_maximum_fusion.own.refs_10_), channel_id=1, source_target_pairs={{0,8},{4,12},{8,0},{12,4},{1,9},{5,13},{9,1},{13,5},{2,10},{6,14},... | collective-permute-start | bytes 4423688 | tf_op jit(solution)/shard_map/ppermute | solution.py:17
  74.2 2.1 %collective-permute-start.8 = (bf16[4,96,768]{2,1,0:T(8,128)(2,1)S(1)}, bf16[4,96,768]{2,1,0:T(8,128)(2,1)S(1)}, u32[]{:S(2)}, u32[]{:S(2)}) collective-permute-start(bf16[4,96,768]{2,1,0:T(8,128)(2,1)S(1)} %bitcast.39), channel_id=1, source_target_pairs={{0,4},{4,0},{8,12},{12,8},{1,5},{5,1},{9,13},{13,9},{2,6},{6,2},{1... | collective-permute-start | bytes 1769480 | tf_op jit(solution)/shard_map/ppermute | solution.py:17
  76.5 20.7 %collective-permute-start.12 = (bf16[96,768]{1,0:T(8,128)(2,1)S(1)}, bf16[96,768]{1,0:T(8,128)(2,1)S(1)}, u32[]{:S(2)}, u32[]{:S(2)}) collective-permute-start(bf16[96,768]{1,0:T(8,128)(2,1)S(1)} %get-tuple-element.104), channel_id=1, source_target_pairs={{0,3},{1,2},{2,1},{3,0},{4,7},{5,6},{6,5},{7,4},{8,11},{9,10},{10,... | collective-permute-start | bytes 442376 | tf_op jit(solution)/shard_map/ppermute | solution.py:17
  80.4 16.8 %collective-permute-start.11 = (bf16[96,768]{1,0:T(8,128)(2,1)S(1)}, bf16[96,768]{1,0:T(8,128)(2,1)S(1)}, u32[]{:S(2)}, u32[]{:S(2)}) collective-permute-start(bf16[96,768]{1,0:T(8,128)(2,1)S(1)} %get-tuple-element.105), channel_id=1, source_target_pairs={{0,2},{1,3},{2,0},{3,1},{4,6},{5,7},{6,4},{7,5},{8,10},{9,11},{10,... | collective-permute-start | bytes 442376 | tf_op jit(solution)/shard_map/ppermute | solution.py:17
  80.4 16.8 %collective-permute-start.10 = (bf16[96,768]{1,0:T(8,128)(2,1)S(1)}, bf16[96,768]{1,0:T(8,128)(2,1)S(1)}, u32[]{:S(2)}, u32[]{:S(2)}) collective-permute-start(bf16[96,768]{1,0:T(8,128)(2,1)S(1)} %get-tuple-element.106), channel_id=1, source_target_pairs={{0,1},{1,0},{2,3},{3,2},{4,5},{5,4},{6,7},{7,6},{8,9},{9,8},{10,11... | collective-permute-start | bytes 442376 | tf_op jit(solution)/shard_map/ppermute | solution.py:17
  97.3 4.4 %collective-permute-start.13 = (bf16[48,768]{1,0:T(8,128)(2,1)S(1)}, bf16[48,768]{1,0:T(8,128)(2,1)S(1)}, u32[]{:S(2)}, u32[]{:S(2)}) collective-permute-start(bf16[48,768]{1,0:T(8,128)(2,1)S(1)} %slice.84), channel_id=1, source_target_pairs={{0,8},{4,12},{8,0},{12,4},{1,9},{5,13},{9,1},{13,5},{2,10},{6,14},... | collective-permute-start | bytes 221192 | tf_op jit(solution)/shard_map/ppermute | solution.py:17
  101.7 4.4 %collective-permute-start.14 = (bf16[48,768]{1,0:T(8,128)(2,1)S(1)}, bf16[48,768]{1,0:T(8,128)(2,1)S(1)}, u32[]{:S(2)}, u32[]{:S(2)}) collective-permute-start(bf16[48,768]{1,0:T(8,128)(2,1)S(1)} %add_convert_fusion), channel_id=1, source_target_pairs={{0,8},{4,12},{8,0},{12,4},{1,9},{5,13},{9,1},{13,5},{2,10},{6,14},... | collective-permute-start | bytes 221192 | tf_op jit(solution)/shard_map/ppermute | solution.py:17
  106.1 6.4 %collective-permute-start.18 = (bf16[5,192,768]{2,1,0:T(8,128)(2,1)S(1)}, bf16[5,192,768]{2,1,0:T(8,128)(2,1)S(1)}, u32[]{:S(2)}, u32[]{:S(2)}) collective-permute-start(bf16[5,192,768]{2,1,0:T(8,128)(2,1)S(1)} %collective-permute-done.9.refs_0_.refs_12_), channel_id=1, source_target_pairs={{0,4},{4,0},{8,12},{12,8},{1,5},{5,1},{9,13},{13,9},{2,6},{6,2},{1... | collective-permute-start | bytes 4423688 | tf_op jit(solution)/shard_map/ppermute | solution.py:17
  106.2 41.4 %collective-permute-start.26 = (bf16[6,192,768]{2,1,0:T(8,128)(2,1)}, bf16[6,192,768]{2,1,0:T(8,128)(2,1)S(1)}, u32[]{:S(2)}, u32[]{:S(2)}) collective-permute-start(bf16[6,192,768]{2,1,0:T(8,128)(2,1)} %slice.53.own), channel_id=1, source_target_pairs={{0,8},{4,12},{8,0},{12,4},{1,9},{5,13},{9,1},{13,5},{2,10},{6,14},... | collective-permute-start | bytes 5308424 | tf_op jit(solution)/shard_map/ppermute | solution.py:17
  108.0 8.6 %collective-permute-start.17 = (bf16[96,768]{1,0:T(8,128)(2,1)S(1)}, bf16[96,768]{1,0:T(8,128)(2,1)S(1)}, u32[]{:S(2)}, u32[]{:S(2)}) collective-permute-start(bf16[96,768]{1,0:T(8,128)(2,1)S(1)} %constant_dynamic-update-slice_fusion.refs_0_), channel_id=1, source_target_pairs={{0,3},{1,2},{2,1},{3,0},{4,7},{5,6},{6,5},{7,4},{8,11},{9,10},{10,... | collective-permute-start | bytes 442376 | tf_op jit(solution)/shard_map/ppermute | solution.py:17
  111.6 12.8 %collective-permute-start.16 = (bf16[96,768]{1,0:T(8,128)(2,1)S(1)}, bf16[96,768]{1,0:T(8,128)(2,1)S(1)}, u32[]{:S(2)}, u32[]{:S(2)}) collective-permute-start(bf16[96,768]{1,0:T(8,128)(2,1)S(1)} %constant_dynamic-update-slice_fusion.refs_0_), channel_id=1, source_target_pairs={{0,2},{1,3},{2,0},{3,1},{4,6},{5,7},{6,4},{7,5},{8,10},{9,11},{10,... | collective-permute-start | bytes 442376 | tf_op jit(solution)/shard_map/ppermute | solution.py:17
  111.6 12.8 %collective-permute-start.15 = (bf16[96,768]{1,0:T(8,128)(2,1)S(1)}, bf16[96,768]{1,0:T(8,128)(2,1)S(1)}, u32[]{:S(2)}, u32[]{:S(2)}) collective-permute-start(bf16[96,768]{1,0:T(8,128)(2,1)S(1)} %constant_dynamic-update-slice_fusion.refs_0_), channel_id=1, source_target_pairs={{0,1},{1,0},{2,3},{3,2},{4,5},{5,4},{6,7},{7,6},{8,9},{9,8},{10,11... | collective-permute-start | bytes 442376 | tf_op jit(solution)/shard_map/ppermute | solution.py:17
  135.8 9.3 %collective-permute-start.25 = (bf16[192,192]{1,0:T(8,128)(2,1)S(1)}, bf16[192,192]{1,0:T(8,128)(2,1)S(1)}, u32[]{:S(2)}, u32[]{:S(2)}) collective-permute-start(bf16[192,192]{1,0:T(8,128)(2,1)S(1)} %get-tuple-element.107), channel_id=1, source_target_pairs={{0,3},{1,2},{2,1},{3,0},{4,7},{5,6},{6,5},{7,4},{8,11},{9,10},{10,... | collective-permute-start | bytes 221192 | tf_op jit(solution)/shard_map/ppermute | solution.py:17
  138.4 8.5 %collective-permute-start.24 = (bf16[192,192]{1,0:T(8,128)(2,1)S(1)}, bf16[192,192]{1,0:T(8,128)(2,1)S(1)}, u32[]{:S(2)}, u32[]{:S(2)}) collective-permute-start(bf16[192,192]{1,0:T(8,128)(2,1)S(1)} %get-tuple-element.108), channel_id=1, source_target_pairs={{0,2},{1,3},{2,0},{3,1},{4,6},{5,7},{6,4},{7,5},{8,10},{9,11},{10,... | collective-permute-start | bytes 221192 | tf_op jit(solution)/shard_map/ppermute | solution.py:17
  138.4 8.5 %collective-permute-start.23 = (bf16[192,192]{1,0:T(8,128)(2,1)S(1)}, bf16[192,192]{1,0:T(8,128)(2,1)S(1)}, u32[]{:S(2)}, u32[]{:S(2)}) collective-permute-start(bf16[192,192]{1,0:T(8,128)(2,1)S(1)} %get-tuple-element.109), channel_id=1, source_target_pairs={{0,1},{1,0},{2,3},{3,2},{4,5},{5,4},{6,7},{7,6},{8,9},{9,8},{10,11... | collective-permute-start | bytes 221192 | tf_op jit(solution)/shard_map/ppermute | solution.py:17
  147.7 3.7 %collective-permute-start.27 = (bf16[6,192,768]{2,1,0:T(8,128)(2,1)S(1)}, bf16[6,192,768]{2,1,0:T(8,128)(2,1)S(1)}, u32[]{:S(2)}, u32[]{:S(2)}) collective-permute-start(bf16[6,192,768]{2,1,0:T(8,128)(2,1)S(1)} %collective-permute-done.26.refs_1_), channel_id=1, source_target_pairs={{0,4},{4,0},{8,12},{12,8},{1,5},{5,1},{9,13},{13,9},{2,6},{6,2},{1... | collective-permute-start | bytes 5308424 | tf_op jit(solution)/shard_map/ppermute | solution.py:17
  (15 other events, 99.5 us)

commit v4 on v3

--- a/solution.py
+++ b/solution.py
@@ -220,30 +220,25 @@
 def add_sec(total, *arrived):
     for block in arrived:
         total = total + block.astype(F32)
-    total = total.reshape(lax.axis_size("env") // 2, -1, total.shape[-1])
-    return total.astype(BF16), total[0]
-
-
-def add_chips(total, *arrived):
-    for block in arrived:
+    return total.astype(BF16)
+
+
+def add_chips(own, *arrived):
+    n_y = len(arrived) + 1
+    total = own.astype(F32)
+    for m, block in enumerate(arrived, 1):
+        pieces = block.reshape(n_y, -1, block.shape[-1])
+        block = jnp.concatenate([pieces[j ^ m] for j in range(n_y)], axis=0)
         total = total + block.astype(F32)
     return total.astype(BF16)
 
 
-def join(*blocks):
-    return jnp.concatenate(blocks, axis=0)
-
-
 def to_sec(blocks):
     return [swap(blocks[m], "sec", m) for m in range(1, lax.axis_size("sec"))]
 
 
 def to_chips(blocks):
     return [swap(blocks[m], "env", 2 * m) for m in range(1, lax.axis_size("env") // 2)]
-
-
-def all_chips(block):
-    return [block] + to_chips([block] * (lax.axis_size("env") // 2))
 
 
 def all_sec(block):
@@ -332,7 +327,7 @@
         acc[pl.ds(pl.multiple_of((me[0] ^ m) * rows, rows), rows), :] = x
     for m in range(n_sec):
         at = pl.multiple_of((me[1] ^ m) * cols, cols)
-        out[m] = acc[pl.ds(at, cols), :].T.astype(BF16)
+        out[m] = acc[pl.ds(at, cols), :].astype(BF16).T
 
 
 def gradient(me, counts, halves, cots, slot, projectors, e_blocks):
@@ -367,39 +362,38 @@
     )
 
 
-def early_kernel(per, first, counts, g_ref, enl_ref, q_ref, *refs):
-    proj, edge = refs[-2:]
-    k = pl.program_id(0)
-    for i in range(per):
-        proj[i] = dot(enl_ref[i], g_ref[...], ((1,), (1,)))
-    x = dot(q_ref[0], g_ref[...])
-    edge[0] = jnp.where(keep_columns(x.shape, 0, counts[first + k]), x, 0.0)
-
-
-def early_gradients(results, counts, g, enlarged, q, first, steps):
-    slices, rows, width = enlarged.shape
-    per = 3 if slices % 3 == 0 else 1
-    last = q.shape[0] - 1
-    out = jax.ShapeDtypeStruct((slices, rows, width), F32)
-    return pl.pallas_call(
-        functools.partial(early_kernel, per, first),
-        grid_spec=pltpu.PrefetchScalarGridSpec(
-            num_scalar_prefetch=1,
-            grid=(steps,),
-            in_specs=[
-                whole((width, width)),
-                group(per, (rows, width), 0, first),
-                pl.BlockSpec((1, rows, width), lambda k, *s: (jnp.minimum(k + first, last), 0, 0)),
-            ]
-            + [FAR] * len(results),
-            out_specs=[group(per, (rows, width), 0, first), group(1, (rows, width), 0, first)],
-        ),
-        out_shape=[out, out],
-        input_output_aliases={4 + j: j for j in range(len(results))},
-        name="early_gradients",
-        compiler_params=pltpu.CompilerParams(vmem_limit_bytes=24 * 1024 * 1024),
-        cost_estimate=pl.CostEstimate(flops=1000, bytes_accessed=1000, transcendentals=0),
-    )(counts, g, enlarged, q, *results)
+def outputs_kernel(per, dims, counts, g_ref, x_ref, out, held, sems):
+    slices, rows, width = x_ref.shape
+    stores = []
+    for k in range(slices // per):
+        at = pl.ds(k * per, per)
+        y = dot(x_ref[k * per : k * per + per].reshape(per * rows, width), g_ref[...], dims)
+        for i in range(per):
+            part = y[i * rows : (i + 1) * rows]
+            if dims[1] == (0,):
+                keep = keep_columns(part.shape, 0, counts[k * per + i])
+                part = jnp.where(keep, part, 0.0)
+            held[k * per + i] = part
+        stores.append(pltpu.make_async_copy(held.at[at], out.at[at], sems.at[k]))
+        stores[-1].start()
+    for copy in stores:
+        copy.wait()
+
+
+def outputs(name, counts, g, x, slices, dims):
+    count, rows, width = x.shape
+    per = 3 if count % 3 == 0 else 1
+    return at_once(
+        functools.partial(outputs_kernel, per, dims),
+        name,
+        jax.ShapeDtypeStruct((slices, rows, width), F32),
+        FAR,
+        [pltpu.VMEM((count, rows, width), F32), pltpu.SemaphoreType.DMA((count // per,))],
+        (counts,),
+        (g, x),
+        (),
+        vmem=24 * 1024 * 1024,
+    )
 
 
 def finish(n, across, begun, p_refs, i):
@@ -436,27 +430,42 @@
     return [(at, min(per, slices - at)) for at in range(0, slices, per)]
 
 
-def late_kernel(n, first, groups, counts, g_ref, c_ref, fwd, *refs):
-    far_refs, refs = refs[: n - 2], refs[n - 2 :]
-    _, out, begun, held, q, x, sems, out_sems = refs
+def add_far_kernel(n, per, c_ref, begun, *refs):
+    across = [c_ref[m].T for m in range(n - 3)]
+    for i in range(per):
+        y = begun[i]
+        for m in range(n - 3):
+            y = y + dot(across[m], refs[m][i])
+        refs[-1][i] = y
+
+
+def add_far(c_far, begun, far):
     slices, rows, width = begun.shape
-    buffers = [begun, *[held.at[m] for m in range(n - 3)]]
-    copies, stores = [], []
+    n = c_far.shape[0] + 2
+    per = 3 if slices % 3 == 0 else 1
+    return call(
+        functools.partial(add_far_kernel, n, per),
+        "add_far",
+        (slices // per,),
+        [whole(c_far.shape)] + [group(per, (rows, width))] * (n - 2),
+        group(per, (rows, width)),
+        jax.ShapeDtypeStruct((slices, rows, width), F32),
+        [],
+        0,
+        0,
+        0,
+        (c_far, begun, *far),
+    )
+
+
+def late_kernel(first, groups, counts, g_ref, c_ref, begun, fwd, _, out, q, x, out_sems):
+    slices, rows, width = begun.shape
+    across = c_ref[...].T
+    stores = []
     for k, (at, size) in enumerate(groups):
-        at = pl.ds(at, size)
-        copies.append([
-            pltpu.make_async_copy(far_refs[j].at[at], buffers[j].at[at], sems.at[j, k])
-            for j in range(n - 2)
-        ])
-        for copy in copies[-1]:
-            copy.start()
-    across = [c_ref[m].T for m in range(n - 2)]
-    p_refs = [*buffers[1:], fwd]
-    for k, (at, size) in enumerate(groups):
-        for copy in copies[k]:
-            copy.wait()
         for i in range(size):
-            q[i * rows : (i + 1) * rows] = finish(n, across, begun, p_refs, at + i)
+            y = begun[at + i] + dot(across, fwd[at + i])
+            q[i * rows : (i + 1) * rows] = y.astype(BF16)
         y = dot(q[: size * rows], g_ref[...])
         for i in range(size):
             part = y[i * rows : (i + 1) * rows]
@@ -469,28 +478,24 @@
         store.wait()
 
 
-def late_edge_gradient(result, counts, g, c_far, begun, p_far, first):
-    n = c_far.shape[0] + 2
+def late_edge_gradient(result, counts, g, c_last, begun, fwd, first):
     slices, rows, width = begun.shape
     groups = spans(slices, 2)
     return at_once(
-        functools.partial(late_kernel, n, first, groups),
+        functools.partial(late_kernel, first, groups),
         "late_edge_gradient",
         jax.ShapeDtypeStruct(result.shape, F32),
         FAR,
         [
-            pltpu.VMEM((slices, rows, width), F32),
-            pltpu.VMEM((n - 3, slices, rows, width), BF16),
             pltpu.VMEM((2 * rows, width), BF16),
             pltpu.VMEM((slices, rows, width), F32),
-            pltpu.SemaphoreType.DMA((n - 2, len(groups))),
             pltpu.SemaphoreType.DMA((len(groups),)),
         ],
         (counts,),
-        (g, c_far, p_far[-1]),
-        (begun, *p_far[:-1], result),
-        {4 + n - 2: 0},
-        vmem=48 * 1024 * 1024,
+        (g, c_last, begun, fwd),
+        (result,),
+        {5: 0},
+        vmem=16 * 1024 * 1024,
     )
 
 
@@ -545,7 +550,7 @@
     mixing = [begin(c_near, p, q) for p, q in zip(pieces, near)]
     mixing[0] = mixing[0][:early]
     far = barrier(far, begun, mixing)
-    p_far = [from_chips(barrier(pieces[0], far))]
+    p_far = [from_chips(pieces[0])]
     e_blocks = [edges, e_near, *both_cores(far)]
 
     order = Order()
@@ -555,9 +560,8 @@
     moved, total = order(add_core, keep, swap(send, "env", 1))
     sec = to_sec(moved)
     total = barrier(total, p_far[0])
-    moved, total = order(add_sec, total, *sec)
-    own = order(add_chips, total, *to_chips(moved))
-    some = order(join, *all_chips(own))
+    some = order(add_sec, total, *sec)
+    some = order(add_chips, some, *from_chips(some))
     half = all_sec(some)
     p_far += [from_chips(barrier(p, some)) for p in pieces[1:]]
     p_far[0] = both_cores(barrier(p_far[0], some))
@@ -572,19 +576,18 @@
     g, corner_new, part = order(
         lambda *h: gradient(me, tile_counts, h, cots, early + 1, projectors, e_blocks), *halves)
     moved = to_sec(part)
-    steps = slices // 3 if slices % 3 == 0 else slices
-    some_steps = max(steps - 1, 1)
-    results = order(
-        lambda g: early_gradients((), tile_counts, g, enlarged, q, 0, some_steps), g)
+    proj_grad = order(
+        lambda g: outputs(
+            "proj_gradient", tile_counts, g, enlarged, slices, ((1,), (1,))), g)
+    edge_grad = order(
+        lambda g: outputs("edge_gradient", tile_counts, g, q, slices, ((1,), (0,))), g)
     corner_grad = order(
         lambda *b: sum((x.astype(F32) for x in b[1:]), b[0].astype(F32)), part[0], *moved)
     p_far = both_cores(barrier(p_far[1], corner_grad))
-    proj_grad, edge_grad = order(
-        lambda *r: early_gradients(
-            r, tile_counts, g, enlarged, q, some_steps, steps - some_steps), *results)
+    begun = order(lambda b, *p: add_far(c_far, b, p), mixing[1], *p_far[:-1])
     edge_grad = order(
-        lambda r, *p: late_edge_gradient(r, tile_counts, g, c_far, mixing[1], p, early),
-        edge_grad, *p_far)
+        lambda r, b, p: late_edge_gradient(r, tile_counts, g, c_far[-1], b, p, early),
+        edge_grad, begun, p_far[-1])
     return (corner_new, corner_grad, edge_grad, proj_grad)
 
 

time: 160 us -> 154 us (0.963)
  waiting for transfers between devices: 73.7 us -> 71.4 us
  Pallas kernels: 41.8 us -> 39.9 us
    pallas_call x2 -> x0, Pallas kernels: 8.22 us -> none  [early_gradients(): pl.pallas_call(functools.partial(early_kernel, per, first), grid_spec=plt...]
    pallas_call x3 -> x5, Pallas kernels: 22.4 us -> 26.6 us  [at_once(): pl.pallas_call(kernel, in_specs=[SCALARS] * len(scalars) + [ARRAY] * len(...]
    unnamed x22 -> x17, local copies, waits for them, and re-layouts: 3.35 us -> 0.79 us
    ppermute x28 -> x27, waiting for transfers between devices: 73.7 us -> 71.4 us  [swap(): return lax.ppermute(value, axis, [(i, i ^ offset) for i in range(size)])]
    pallas_call x4 -> x5, Pallas kernels: 11.2 us -> 13.2 us  [call(): pl.pallas_call(kernel, grid_spec=pltpu.PrefetchScalarGridSpec(num_scalar_...]
    ppermute x28 -> x27, starting transfers between devices: 29.9 us -> 28.9 us  [swap(): return lax.ppermute(value, axis, [(i, i ^ offset) for i in range(size)])]
  transfers between devices with their start and end apart: 28 -> 27, of which waited for: 17 -> 16; matrix products, arithmetic and copies ran while one was open for 6% -> 8% of each run, Pallas kernels for 22% -> 23%
where the time goes in v4:
time: 154 us
  waiting for transfers between devices  71.4 us (46%)
  Pallas kernels  39.9 us (26%)
  starting transfers between devices  28.9 us (19%)
  other arithmetic  6.63 us (4%)
  local copies, waits for them, and re-layouts  5.94 us (4%)
    ppermute x27, waiting for transfers between devices, swap(): return lax.ppermute(value, axis, [(i, i ^ offset) for i in range(size)])  71.4 us
    ppermute x27, starting transfers between devices, swap(): return lax.ppermute(value, axis, [(i, i ^ offset) for i in range(size)])  28.9 us
    pallas_call x5, Pallas kernels, at_once(): pl.pallas_call(kernel, in_specs=[SCALARS] * len(scalars) + [ARRAY] * len(...  26.6 us
    pallas_call x5, Pallas kernels, call(): pl.pallas_call(kernel, grid_spec=pltpu.PrefetchScalarGridSpec(num_scalar_...  13.2 us
  transfers between devices with their start and end apart: 27, of which 16 were waited for; matrix products, arithmetic and copies ran while one was open for 8% of the time, Pallas kernels for 23%

profile of v4, /device:TPU:0, one launch (start us, length us, event | category | flops | bytes accessed | tf_op | source)
XLA Modules:
  0.0 153.8 jit_solution(11017558319810703084)
XLA Ops:
  1.2 2.6 %collective-permute-start.1 = (bf16[9,192,768]{2,1,0:T(8,128)(2,1)}, bf16[9,192,768]{2,1,0:T(8,128)(2,1)}, u32[]{:S(2)}, u32[]{:S(2)}) collective-permute-start(bf16[9,192,768]{2,1,0:T(8,128)(2,1)} %refs_14_.1), channel_id=1, source_target_pairs={{0,8},{4,12},{8,0},{12,4},{1,9},{5,13},{9,1},{13,5},{2,10},{6,14},... | collective-permute-start | bytes 7962632 | tf_op jit(solution)/shard_map/ppermute | solution.py:17
  4.7 3.7 %collective-permute-start.2 = (bf16[192,192]{1,0:T(8,128)(2,1)S(1)}, bf16[192,192]{1,0:T(8,128)(2,1)S(1)}, u32[]{:S(2)}, u32[]{:S(2)}) collective-permute-start(bf16[192,192]{1,0:T(8,128)(2,1)S(1)} %convert_element_type.42), channel_id=1, source_target_pairs={{0,3},{1,2},{2,1},{3,0},{4,7},{5,6},{6,5},{7,4},{8,11},{9,10},{10,... | collective-permute-start | bytes 221192 | tf_op jit(solution)/shard_map/ppermute | solution.py:17
  9.2 3.1 %collective-permute-done.2 = bf16[192,192]{1,0:T(8,128)(2,1)S(1)} collective-permute-done((bf16[192,192]{1,0:T(8,128)(2,1)S(1)}, bf16[192,192]{1,0:T(8,128)(2,1)S(1)}, u32[]{:S(2)}, u32[]{:S(2)}) %collective-permute-start.2) | collective-permute-done | bytes 73760 | tf_op jit(solution)/shard_map/ppermute | solution.py:17
  12.3 4.7 %collective-permute-done.3 = bf16[192,192]{1,0:T(8,128)(2,1)S(1)} collective-permute-done((bf16[192,192]{1,0:T(8,128)(2,1)S(1)}, bf16[192,192]{1,0:T(8,128)(2,1)S(1)}, u32[]{:S(2)}, u32[]{:S(2)}) %collective-permute-start.3) | collective-permute-done | bytes 73760 | tf_op jit(solution)/shard_map/ppermute | solution.py:17
  17.2 2.4 %pad_maximum_fusion.own.refs_10_ = bf16[5,192,768]{2,1,0:T(8,128)(2,1)} fusion(bf16[1,192,768]{2,1,0:T(8,128)(2,1)S(1)} %maximum_bitcast_fusion, bf16[1,192,768]{2,1,0:T(8,128)(2,1)} %bitcast.42, bf16[3,192,768]{2,1,0:T(8,128)(2,1)S(1)} %slice-done), kind=kLoop, calls=%fused_computation | loop fusion | flops 1474560 | bytes 2949120 | tf_op jit(solution)/shard_map/concatenate | solution.py:536
  26.4 4.1 %begin.4 = f32[5,192,768]{2,1,0:T(8,128)S(1)} custom-call(bf16[2,192,192]{2,1,0:T(8,128)(2,1)S(1)} %pad_maximum_fusion.2.c_ref, bf16[5,192,768]{2,1,0:T(8,128)(2,1)} %pad_maximum_fusion.own.refs_10_, bf16[5,192,768]{2,1,0:T(8,128)(2,1)} %collective-permute-done.5.near.refs_11_), custom_call_target="tpu_custom_call" | custom-call | flops 1000 | bytes 1000 | tf_op jit(solution)/shard_map/begin/pallas_call | solution.py:29
  31.9 2.8 %begin.5.begun = f32[6,192,768]{2,1,0:T(8,128)S(1)} custom-call(bf16[2,192,192]{2,1,0:T(8,128)(2,1)S(1)} %pad_maximum_fusion.2.c_ref, bf16[6,192,768]{2,1,0:T(8,128)(2,1)} %slice.53.own, bf16[6,192,768]{2,1,0:T(8,128)(2,1)} %collective-permute-done.6.near), custom_call_target="tpu_custom_call" | custom-call | flops 1000 | bytes 1000 | tf_op jit(solution)/shard_map/begin/pallas_call | solution.py:29
  34.7 3.6 %begin.3.begun = f32[9,192,768]{2,1,0:T(8,128)S(1)} custom-call(bf16[4,192,192]{2,1,0:T(8,128)(2,1)S(1)} %pad_maximum_fusion.1.c_ref, bf16[9,192,768]{2,1,0:T(8,128)(2,1)S(1)} %copy-done.1, bf16[9,192,768]{2,1,0:T(8,128)(2,1)} %collective-permute-done.near.refs_15_), custom_call_target="tpu_custom_call" | custom-call | flops 1000 | bytes 1000 | tf_op jit(solution)/shard_map/begin/pallas_call | solution.py:29
  38.3 23.9 %collective-permute-done.1.refs_0_.refs_16_ = bf16[9,192,768]{2,1,0:T(8,128)(2,1)} collective-permute-done((bf16[9,192,768]{2,1,0:T(8,128)(2,1)}, bf16[9,192,768]{2,1,0:T(8,128)(2,1)}, u32[]{:S(2)}, u32[]{:S(2)}) %collective-permute-start.1) | collective-permute-done | bytes 2654240 | tf_op jit(solution)/shard_map/ppermute | solution.py:17
  64.1 3.3 %collective-permute-done.7.fwd.refs_9_ = bf16[9,192,768]{2,1,0:T(8,128)(2,1)S(1)} collective-permute-done((bf16[9,192,768]{2,1,0:T(8,128)(2,1)}, bf16[9,192,768]{2,1,0:T(8,128)(2,1)S(1)}, u32[]{:S(2)}, u32[]{:S(2)}) %collective-permute-start.7) | collective-permute-done | bytes 2654240 | tf_op jit(solution)/shard_map/ppermute | solution.py:17
  67.4 6.7 %absorb.1 = (bf16[9,192,768]{2,1,0:T(8,128)(2,1)S(1)}, f32[384,768]{1,0:T(8,128)S(1)}, bf16[384,768]{1,0:T(8,128)(2,1)S(1)}) custom-call(s32[2]{0:T(128)S(1)} %pad_add_fusion.me, s32[9]{0:T(128)S(1)} %copy-done.5, bf16[4,192,192]{2,1,0:T(8,128)(2,1)S(1)} %pad_maximum_fusion.1.c_ref, bf16[9,192,768]{2,1,0:T(8,128)(2,1)S(1)} %copy-done, ...), custom_call_target="tpu_custom_call" | custom-call | flops 1000 | bytes 1000 | tf_op jit(solution)/shard_map/absorb/pallas_call | solution.py:148
  76.4 1.9 %collective-permute-start.10 = (bf16[96,768]{1,0:T(8,128)(2,1)S(1)}, bf16[96,768]{1,0:T(8,128)(2,1)S(1)}, u32[]{:S(2)}, u32[]{:S(2)}) collective-permute-start(bf16[96,768]{1,0:T(8,128)(2,1)S(1)} %get-tuple-element.94), channel_id=1, source_target_pairs={{0,1},{1,0},{2,3},{3,2},{4,5},{5,4},{6,7},{7,6},{8,9},{9,8},{10,11... | collective-permute-start | bytes 442376 | tf_op jit(solution)/shard_map/ppermute | solution.py:17
  78.3 2.6 %collective-permute-start.11 = (bf16[96,768]{1,0:T(8,128)(2,1)S(1)}, bf16[96,768]{1,0:T(8,128)(2,1)S(1)}, u32[]{:S(2)}, u32[]{:S(2)}) collective-permute-start(bf16[96,768]{1,0:T(8,128)(2,1)S(1)} %get-tuple-element.93), channel_id=1, source_target_pairs={{0,2},{1,3},{2,0},{3,1},{4,6},{5,7},{6,4},{7,5},{8,10},{9,11},{10,... | collective-permute-start | bytes 442376 | tf_op jit(solution)/shard_map/ppermute | solution.py:17
  80.9 16.2 %collective-permute-done.9.refs_0_.refs_12_ = bf16[5,192,768]{2,1,0:T(8,128)(2,1)S(1)} collective-permute-done((bf16[5,192,768]{2,1,0:T(8,128)(2,1)}, bf16[5,192,768]{2,1,0:T(8,128)(2,1)S(1)}, u32[]{:S(2)}, u32[]{:S(2)}) %collective-permute-start.9) | collective-permute-done | bytes 1474592 | tf_op jit(solution)/shard_map/ppermute | solution.py:17
  99.1 3.8 %collective-permute-done.13 = bf16[96,768]{1,0:T(8,128)(2,1)S(1)} collective-permute-done((bf16[96,768]{1,0:T(8,128)(2,1)S(1)}, bf16[96,768]{1,0:T(8,128)(2,1)S(1)}, u32[]{:S(2)}, u32[]{:S(2)}) %collective-permute-start.13) | collective-permute-done | bytes 147488 | tf_op jit(solution)/shard_map/ppermute | solution.py:17
  106.4 2.6 %collective-permute-start.15 = (bf16[96,768]{1,0:T(8,128)(2,1)S(1)}, bf16[96,768]{1,0:T(8,128)(2,1)S(1)}, u32[]{:S(2)}, u32[]{:S(2)}) collective-permute-start(bf16[96,768]{1,0:T(8,128)(2,1)S(1)} %add_convert_fusion.refs_0_), channel_id=1, source_target_pairs={{0,2},{1,3},{2,0},{3,1},{4,6},{5,7},{6,4},{7,5},{8,10},{9,11},{10,... | collective-permute-start | bytes 442376 | tf_op jit(solution)/shard_map/ppermute | solution.py:17
  110.2 3.0 %collective-permute-done.14.refs_1_ = bf16[96,768]{1,0:T(8,128)(2,1)S(1)} collective-permute-done((bf16[96,768]{1,0:T(8,128)(2,1)S(1)}, bf16[96,768]{1,0:T(8,128)(2,1)S(1)}, u32[]{:S(2)}, u32[]{:S(2)}) %collective-permute-start.14) | collective-permute-done | bytes 147488 | tf_op jit(solution)/shard_map/ppermute | solution.py:17
  113.2 7.2 %collective-permute-done.15.refs_2_ = bf16[96,768]{1,0:T(8,128)(2,1)S(1)} collective-permute-done((bf16[96,768]{1,0:T(8,128)(2,1)S(1)}, bf16[96,768]{1,0:T(8,128)(2,1)S(1)}, u32[]{:S(2)}, u32[]{:S(2)}) %collective-permute-start.15) | collective-permute-done | bytes 147488 | tf_op jit(solution)/shard_map/ppermute | solution.py:17
  122.5 9.3 %gradient.1 = (bf16[768,768]{1,0:T(8,128)(2,1)S(1)}, f32[192,192]{1,0:T(8,128)}, bf16[4,192,192]{2,1,0:T(8,128)(2,1)S(1)}) custom-call(s32[2]{0:T(128)S(1)} %pad_add_fusion.me, s32[9]{0:T(128)S(1)} %copy-done.5, bf16[96,768]{1,0:T(8,128)(2,1)S(1)} %add_convert_fusion.refs_0_, bf16[96,768]{1,0:T(8,128)(2,1)S(1)} %collective-permute-done.14.refs_1_, ...), custom_call_target="tpu_custom_call" | custom-call | flops 1000 | bytes 26542080 | tf_op jit(solution)/shard_map/gradient/pallas_call | solution.py:148
  131.8 2.7 %collective-permute-start.22 = (bf16[192,192]{1,0:T(8,128)(2,1)S(1)}, bf16[192,192]{1,0:T(8,128)(2,1)S(1)}, u32[]{:S(2)}, u32[]{:S(2)}) collective-permute-start(bf16[192,192]{1,0:T(8,128)(2,1)S(1)} %get-tuple-element.97), channel_id=1, source_target_pairs={{0,1},{1,0},{2,3},{3,2},{4,5},{5,4},{6,7},{7,6},{8,9},{9,8},{10,11... | collective-permute-start | bytes 221192 | tf_op jit(solution)/shard_map/ppermute | solution.py:17
  137.0 4.2 %proj_gradient.1 = f32[9,192,768]{2,1,0:T(8,128)} custom-call(s32[9]{0:T(128)S(1)} %copy-done.5, bf16[768,768]{1,0:T(8,128)(2,1)S(1)} %get-tuple-element.78.g_ref, bf16[9,192,768]{2,1,0:T(8,128)(2,1)S(1)} %copy-done.4), custom_call_target="tpu_custom_call" | custom-call | flops 1000 | bytes 1000 | tf_op jit(solution)/shard_map/proj_gradient/pallas_call | solution.py:148
  141.2 2.6 %edge_gradient.1._ = f32[9,192,768]{2,1,0:T(8,128)} custom-call(s32[9]{0:T(128)S(1)} %copy-done.5, bf16[768,768]{1,0:T(8,128)(2,1)S(1)} %get-tuple-element.78.g_ref, bf16[3,192,768]{2,1,0:T(8,128)(2,1)S(1)} %mix.1.x_ref), custom_call_target="tpu_custom_call" | custom-call | flops 1000 | bytes 1000 | tf_op jit(solution)/shard_map/edge_gradient/pallas_call | solution.py:148
  146.0 2.1 %add_far.1.begun = f32[6,192,768]{2,1,0:T(8,128)S(1)} custom-call(bf16[2,192,192]{2,1,0:T(8,128)(2,1)S(1)} %pad_maximum_fusion.3.c_ref, f32[6,192,768]{2,1,0:T(8,128)S(1)} %begin.5.begun, bf16[6,192,768]{2,1,0:T(8,128)(2,1)} %collective-permute-done.25.refs_0_), custom_call_target="tpu_custom_call" | custom-call | flops 1000 | bytes 1000 | tf_op jit(solution)/shard_map/add_far/pallas_call | solution.py:29
  149.8 3.8 %late_edge_gradient.1 = f32[9,192,768]{2,1,0:T(8,128)} custom-call(s32[9]{0:T(128)S(1)} %copy-done.5, bf16[768,768]{1,0:T(8,128)(2,1)S(1)} %get-tuple-element.78.g_ref, bf16[192,192]{1,0:T(8,128)(2,1)S(1)} %fusion.2.c_ref, f32[6,192,768]{2,1,0:T(8,128)S(1)} %add_far.1.begun, ...), custom_call_target="tpu_custom_call", output_to_operand_aliasing={{}: (5, {})} | custom-call | flops 1000 | bytes 1000 | tf_op jit(solution)/shard_map/late_edge_gradient/pallas_call | solution.py:148
  (86 shorter events, 29.8 us)
Async XLA Ops:
  0.6 34.1 %collective-permute-start = (bf16[9,192,768]{2,1,0:T(8,128)(2,1)}, bf16[9,192,768]{2,1,0:T(8,128)(2,1)}, u32[]{:S(2)}, u32[]{:S(2)}) collective-permute-start(bf16[9,192,768]{2,1,0:T(8,128)(2,1)} %refs_14_.1), channel_id=1, source_target_pairs={{0,4},{4,0},{8,12},{12,8},{1,5},{5,1},{9,13},{13,9},{2,6},{6,2},{1... | collective-permute-start | bytes 7962632 | tf_op jit(solution)/shard_map/ppermute | solution.py:17
  1.2 61.1 %collective-permute-start.1 = (bf16[9,192,768]{2,1,0:T(8,128)(2,1)}, bf16[9,192,768]{2,1,0:T(8,128)(2,1)}, u32[]{:S(2)}, u32[]{:S(2)}) collective-permute-start(bf16[9,192,768]{2,1,0:T(8,128)(2,1)} %refs_14_.1), channel_id=1, source_target_pairs={{0,8},{4,12},{8,0},{12,4},{1,9},{5,13},{9,1},{13,5},{2,10},{6,14},... | collective-permute-start | bytes 7962632 | tf_op jit(solution)/shard_map/ppermute | solution.py:17
  4.7 7.6 %collective-permute-start.2 = (bf16[192,192]{1,0:T(8,128)(2,1)S(1)}, bf16[192,192]{1,0:T(8,128)(2,1)S(1)}, u32[]{:S(2)}, u32[]{:S(2)}) collective-permute-start(bf16[192,192]{1,0:T(8,128)(2,1)S(1)} %convert_element_type.42), channel_id=1, source_target_pairs={{0,3},{1,2},{2,1},{3,0},{4,7},{5,6},{6,5},{7,4},{8,11},{9,10},{10,... | collective-permute-start | bytes 221192 | tf_op jit(solution)/shard_map/ppermute | solution.py:17
  8.4 8.6 %collective-permute-start.3 = (bf16[192,192]{1,0:T(8,128)(2,1)S(1)}, bf16[192,192]{1,0:T(8,128)(2,1)S(1)}, u32[]{:S(2)}, u32[]{:S(2)}) collective-permute-start(bf16[192,192]{1,0:T(8,128)(2,1)S(1)} %convert_element_type.42), channel_id=1, source_target_pairs={{0,2},{1,3},{2,0},{3,1},{4,6},{5,7},{6,4},{7,5},{8,10},{9,11},{10,... | collective-permute-start | bytes 221192 | tf_op jit(solution)/shard_map/ppermute | solution.py:17
  8.4 8.6 %collective-permute-start.4 = (bf16[192,192]{1,0:T(8,128)(2,1)S(1)}, bf16[192,192]{1,0:T(8,128)(2,1)S(1)}, u32[]{:S(2)}, u32[]{:S(2)}) collective-permute-start(bf16[192,192]{1,0:T(8,128)(2,1)S(1)} %convert_element_type.42), channel_id=1, source_target_pairs={{0,1},{1,0},{2,3},{3,2},{4,5},{5,4},{6,7},{7,6},{8,9},{9,8},{10,11... | collective-permute-start | bytes 221192 | tf_op jit(solution)/shard_map/ppermute | solution.py:17
  19.6 3.6 %collective-permute-start.5 = (bf16[5,192,768]{2,1,0:T(8,128)(2,1)}, bf16[5,192,768]{2,1,0:T(8,128)(2,1)}, u32[]{:S(2)}, u32[]{:S(2)}) collective-permute-start(bf16[5,192,768]{2,1,0:T(8,128)(2,1)} %pad_maximum_fusion.own.refs_10_), channel_id=1, source_target_pairs={{0,4},{4,0},{8,12},{12,8},{1,5},{5,1},{9,13},{13,9},{2,6},{6,2},{1... | collective-permute-start | bytes 4423688 | tf_op jit(solution)/shard_map/ppermute | solution.py:17
  21.0 10.9 %collective-permute-start.6 = (bf16[6,192,768]{2,1,0:T(8,128)(2,1)}, bf16[6,192,768]{2,1,0:T(8,128)(2,1)}, u32[]{:S(2)}, u32[]{:S(2)}) collective-permute-start(bf16[6,192,768]{2,1,0:T(8,128)(2,1)} %slice.53.own), channel_id=1, source_target_pairs={{0,4},{4,0},{8,12},{12,8},{1,5},{5,1},{9,13},{13,9},{2,6},{6,2},{1... | collective-permute-start | bytes 5308424 | tf_op jit(solution)/shard_map/ppermute | solution.py:17
  62.2 5.2 %collective-permute-start.7 = (bf16[9,192,768]{2,1,0:T(8,128)(2,1)}, bf16[9,192,768]{2,1,0:T(8,128)(2,1)S(1)}, u32[]{:S(2)}, u32[]{:S(2)}) collective-permute-start(bf16[9,192,768]{2,1,0:T(8,128)(2,1)} %collective-permute-done.1.refs_0_.refs_16_), channel_id=1, source_target_pairs={{0,4},{4,0},{8,12},{12,8},{1,5},{5,1},{9,13},{13,9},{2,6},{6,2},{1... | collective-permute-start | bytes 7962632 | tf_op jit(solution)/shard_map/ppermute | solution.py:17
  62.2 34.9 %collective-permute-start.9 = (bf16[5,192,768]{2,1,0:T(8,128)(2,1)}, bf16[5,192,768]{2,1,0:T(8,128)(2,1)S(1)}, u32[]{:S(2)}, u32[]{:S(2)}) collective-permute-start(bf16[5,192,768]{2,1,0:T(8,128)(2,1)} %pad_maximum_fusion.own.refs_10_), channel_id=1, source_target_pairs={{0,8},{4,12},{8,0},{12,4},{1,9},{5,13},{9,1},{13,5},{2,10},{6,14},... | collective-permute-start | bytes 4423688 | tf_op jit(solution)/shard_map/ppermute | solution.py:17
  74.1 2.1 %collective-permute-start.8 = (bf16[4,96,768]{2,1,0:T(8,128)(2,1)S(1)}, bf16[4,96,768]{2,1,0:T(8,128)(2,1)S(1)}, u32[]{:S(2)}, u32[]{:S(2)}) collective-permute-start(bf16[4,96,768]{2,1,0:T(8,128)(2,1)S(1)} %bitcast.41), channel_id=1, source_target_pairs={{0,4},{4,0},{8,12},{12,8},{1,5},{5,1},{9,13},{13,9},{2,6},{6,2},{1... | collective-permute-start | bytes 1769480 | tf_op jit(solution)/shard_map/ppermute | solution.py:17
  76.4 20.7 %collective-permute-start.10 = (bf16[96,768]{1,0:T(8,128)(2,1)S(1)}, bf16[96,768]{1,0:T(8,128)(2,1)S(1)}, u32[]{:S(2)}, u32[]{:S(2)}) collective-permute-start(bf16[96,768]{1,0:T(8,128)(2,1)S(1)} %get-tuple-element.94), channel_id=1, source_target_pairs={{0,1},{1,0},{2,3},{3,2},{4,5},{5,4},{6,7},{7,6},{8,9},{9,8},{10,11... | collective-permute-start | bytes 442376 | tf_op jit(solution)/shard_map/ppermute | solution.py:17
  78.3 18.8 %collective-permute-start.11 = (bf16[96,768]{1,0:T(8,128)(2,1)S(1)}, bf16[96,768]{1,0:T(8,128)(2,1)S(1)}, u32[]{:S(2)}, u32[]{:S(2)}) collective-permute-start(bf16[96,768]{1,0:T(8,128)(2,1)S(1)} %get-tuple-element.93), channel_id=1, source_target_pairs={{0,2},{1,3},{2,0},{3,1},{4,6},{5,7},{6,4},{7,5},{8,10},{9,11},{10,... | collective-permute-start | bytes 442376 | tf_op jit(solution)/shard_map/ppermute | solution.py:17
  80.9 16.3 %collective-permute-start.12 = (bf16[96,768]{1,0:T(8,128)(2,1)S(1)}, bf16[96,768]{1,0:T(8,128)(2,1)S(1)}, u32[]{:S(2)}, u32[]{:S(2)}) collective-permute-start(bf16[96,768]{1,0:T(8,128)(2,1)S(1)} %get-tuple-element.92), channel_id=1, source_target_pairs={{0,3},{1,2},{2,1},{3,0},{4,7},{5,6},{6,5},{7,4},{8,11},{9,10},{10,... | collective-permute-start | bytes 442376 | tf_op jit(solution)/shard_map/ppermute | solution.py:17
  97.2 5.6 %collective-permute-start.13 = (bf16[96,768]{1,0:T(8,128)(2,1)S(1)}, bf16[96,768]{1,0:T(8,128)(2,1)S(1)}, u32[]{:S(2)}, u32[]{:S(2)}) collective-permute-start(bf16[96,768]{1,0:T(8,128)(2,1)S(1)} %add_convert_fusion.1), channel_id=1, source_target_pairs={{0,8},{4,12},{8,0},{12,4},{1,9},{5,13},{9,1},{13,5},{2,10},{6,14},... | collective-permute-start | bytes 442376 | tf_op jit(solution)/shard_map/ppermute | solution.py:17
  102.9 6.5 %collective-permute-start.17 = (bf16[5,192,768]{2,1,0:T(8,128)(2,1)S(1)}, bf16[5,192,768]{2,1,0:T(8,128)(2,1)S(1)}, u32[]{:S(2)}, u32[]{:S(2)}) collective-permute-start(bf16[5,192,768]{2,1,0:T(8,128)(2,1)S(1)} %collective-permute-done.9.refs_0_.refs_12_), channel_id=1, source_target_pairs={{0,4},{4,0},{8,12},{12,8},{1,5},{5,1},{9,13},{13,9},{2,6},{6,2},{1... | collective-permute-start | bytes 4423688 | tf_op jit(solution)/shard_map/ppermute | solution.py:17
  102.9 42.9 %collective-permute-start.25 = (bf16[6,192,768]{2,1,0:T(8,128)(2,1)}, bf16[6,192,768]{2,1,0:T(8,128)(2,1)}, u32[]{:S(2)}, u32[]{:S(2)}) collective-permute-start(bf16[6,192,768]{2,1,0:T(8,128)(2,1)} %slice.53.own), channel_id=1, source_target_pairs={{0,8},{4,12},{8,0},{12,4},{1,9},{5,13},{9,1},{13,5},{2,10},{6,14},... | collective-permute-start | bytes 5308424 | tf_op jit(solution)/shard_map/ppermute | solution.py:17
  104.8 8.4 %collective-permute-start.14 = (bf16[96,768]{1,0:T(8,128)(2,1)S(1)}, bf16[96,768]{1,0:T(8,128)(2,1)S(1)}, u32[]{:S(2)}, u32[]{:S(2)}) collective-permute-start(bf16[96,768]{1,0:T(8,128)(2,1)S(1)} %add_convert_fusion.refs_0_), channel_id=1, source_target_pairs={{0,1},{1,0},{2,3},{3,2},{4,5},{5,4},{6,7},{7,6},{8,9},{9,8},{10,11... | collective-permute-start | bytes 442376 | tf_op jit(solution)/shard_map/ppermute | solution.py:17
  106.4 14.0 %collective-permute-start.15 = (bf16[96,768]{1,0:T(8,128)(2,1)S(1)}, bf16[96,768]{1,0:T(8,128)(2,1)S(1)}, u32[]{:S(2)}, u32[]{:S(2)}) collective-permute-start(bf16[96,768]{1,0:T(8,128)(2,1)S(1)} %add_convert_fusion.refs_0_), channel_id=1, source_target_pairs={{0,2},{1,3},{2,0},{3,1},{4,6},{5,7},{6,4},{7,5},{8,10},{9,11},{10,... | collective-permute-start | bytes 442376 | tf_op jit(solution)/shard_map/ppermute | solution.py:17
  109.0 11.4 %collective-permute-start.16 = (bf16[96,768]{1,0:T(8,128)(2,1)S(1)}, bf16[96,768]{1,0:T(8,128)(2,1)S(1)}, u32[]{:S(2)}, u32[]{:S(2)}) collective-permute-start(bf16[96,768]{1,0:T(8,128)(2,1)S(1)} %add_convert_fusion.refs_0_), channel_id=1, source_target_pairs={{0,3},{1,2},{2,1},{3,0},{4,7},{5,6},{6,5},{7,4},{8,11},{9,10},{10,... | collective-permute-start | bytes 442376 | tf_op jit(solution)/shard_map/ppermute | solution.py:17
  120.4 1.6 %collective-permute-start.19 = (bf16[96,768]{1,0:T(8,128)(2,1)S(1)}, bf16[96,768]{1,0:T(8,128)(2,1)S(1)}, u32[]{:S(2)}, u32[]{:S(2)}) collective-permute-start(bf16[96,768]{1,0:T(8,128)(2,1)S(1)} %collective-permute-done.14.refs_1_), channel_id=1, source_target_pairs={{0,4},{4,0},{8,12},{12,8},{1,5},{5,1},{9,13},{13,9},{2,6},{6,2},{1... | collective-permute-start | bytes 442376 | tf_op jit(solution)/shard_map/ppermute | solution.py:17
  131.8 12.0 %collective-permute-start.22 = (bf16[192,192]{1,0:T(8,128)(2,1)S(1)}, bf16[192,192]{1,0:T(8,128)(2,1)S(1)}, u32[]{:S(2)}, u32[]{:S(2)}) collective-permute-start(bf16[192,192]{1,0:T(8,128)(2,1)S(1)} %get-tuple-element.97), channel_id=1, source_target_pairs={{0,1},{1,0},{2,3},{3,2},{4,5},{5,4},{6,7},{7,6},{8,9},{9,8},{10,11... | collective-permute-start | bytes 221192 | tf_op jit(solution)/shard_map/ppermute | solution.py:17
  134.5 10.6 %collective-permute-start.23 = (bf16[192,192]{1,0:T(8,128)(2,1)S(1)}, bf16[192,192]{1,0:T(8,128)(2,1)S(1)}, u32[]{:S(2)}, u32[]{:S(2)}) collective-permute-start(bf16[192,192]{1,0:T(8,128)(2,1)S(1)} %get-tuple-element.96), channel_id=1, source_target_pairs={{0,2},{1,3},{2,0},{3,1},{4,6},{5,7},{6,4},{7,5},{8,10},{9,11},{10,... | collective-permute-start | bytes 221192 | tf_op jit(solution)/shard_map/ppermute | solution.py:17
  135.6 9.5 %collective-permute-start.24 = (bf16[192,192]{1,0:T(8,128)(2,1)S(1)}, bf16[192,192]{1,0:T(8,128)(2,1)S(1)}, u32[]{:S(2)}, u32[]{:S(2)}) collective-permute-start(bf16[192,192]{1,0:T(8,128)(2,1)S(1)} %get-tuple-element.95), channel_id=1, source_target_pairs={{0,3},{1,2},{2,1},{3,0},{4,7},{5,6},{6,5},{7,4},{8,11},{9,10},{10,... | collective-permute-start | bytes 221192 | tf_op jit(solution)/shard_map/ppermute | solution.py:17
  145.9 3.9 %collective-permute-start.26 = (bf16[6,192,768]{2,1,0:T(8,128)(2,1)}, bf16[6,192,768]{2,1,0:T(8,128)(2,1)S(1)}, u32[]{:S(2)}, u32[]{:S(2)}) collective-permute-start(bf16[6,192,768]{2,1,0:T(8,128)(2,1)} %collective-permute-done.25.refs_0_), channel_id=1, source_target_pairs={{0,4},{4,0},{8,12},{12,8},{1,5},{5,1},{9,13},{13,9},{2,6},{6,2},{1... | collective-permute-start | bytes 5308424 | tf_op jit(solution)/shard_map/ppermute | solution.py:17
  (12 other events, 118.6 us)

commit v5 on v4

--- a/solution.py
+++ b/solution.py
@@ -212,9 +212,10 @@
         return out
 
 
-def add_core(keep, arrived):
-    total = keep + arrived.astype(F32)
-    return total.astype(BF16), total[0]
+def add_core(keep, *arrived):
+    arrived = [block for part in arrived for block in part]
+    total = [keep[m] + arrived[m].astype(F32) for m in range(len(arrived))]
+    return [block.astype(BF16) for block in total], total[0]
 
 
 def add_sec(total, *arrived):
@@ -245,7 +246,7 @@
     return [block] + to_sec([block] * lax.axis_size("sec"))
 
 
-def gradient_kernel(n, n_sec, piece, per, slot, me, counts, *refs):
+def gradient_kernel(n, n_sec, piece, per, ahead, me, counts, *refs):
     blocks, refs = refs[: 2 * n_sec], refs[2 * n_sec :]
     p_ref, last_e, refs = refs[0], refs[1], refs[2:]
     cot_refs, far_refs, refs = refs[:n], refs[n : 2 * n - 1], refs[2 * n - 1 :]
@@ -254,7 +255,8 @@
     cols = width // n_sec
     n_y = n // 2
     cot_copies = [
-        pltpu.make_async_copy(cot_refs[m].at[slot], cot.at[m], cot_sems.at[m]) for m in range(n)
+        pltpu.make_async_copy(cot_refs[m].at[pl.ds(ahead, rows)], cot.at[m], cot_sems.at[m])
+        for m in range(n)
     ]
     for copy in cot_copies:
         copy.start()
@@ -330,14 +332,14 @@
         out[m] = acc[pl.ds(at, cols), :].astype(BF16).T
 
 
-def gradient(me, counts, halves, cots, slot, projectors, e_blocks):
+def gradient(me, counts, halves, cots, ahead, projectors, e_blocks):
     slices, rows, width = projectors.shape
     n, n_sec, _, piece = sizes(rows, width)
     per = 3 if slices % 3 == 0 else 1
     cols = width // n_sec
     held = (slices, rows, width)
     return at_once(
-        functools.partial(gradient_kernel, n, n_sec, piece, per, slot),
+        functools.partial(gradient_kernel, n, n_sec, piece, per, ahead),
         "gradient",
         [
             jax.ShapeDtypeStruct((width, width), BF16),
@@ -382,7 +384,7 @@
 
 def outputs(name, counts, g, x, slices, dims):
     count, rows, width = x.shape
-    per = 3 if count % 3 == 0 else 1
+    per = 3 if count % 3 == 0 else 2 if count % 2 == 0 else 1
     return at_once(
         functools.partial(outputs_kernel, per, dims),
         name,
@@ -396,26 +398,23 @@
     )
 
 
-def finish(n, across, begun, p_refs, i):
-    y = begun[i]
-    for m in range(n - 2):
-        y = y + dot(across[m], p_refs[m][i])
-    return y.astype(BF16)
-
-
-def mix_kernel(n, slices, c_ref, begun, *refs):
+def mix_kernel(n, slices, rows, c_ref, begun, *refs):
     across = [c_ref[m].T for m in range(n - 2)]
     for i in range(slices):
-        refs[-1][i] = finish(n, across, begun, refs, i)
+        y = begun[i]
+        for m in range(n - 2):
+            y = y + dot(across[m], refs[m][i * rows : (i + 1) * rows])
+        refs[-1][i] = y.astype(BF16)
 
 
 def mix(c_far, begun, p_far):
     slices, rows, width = begun.shape
     return call(
-        functools.partial(mix_kernel, c_far.shape[0] + 2, slices),
+        functools.partial(mix_kernel, c_far.shape[0] + 2, slices, rows),
         "mix",
         (1,),
-        [whole(c_far.shape)] + [group(slices, (rows, width))] * (1 + len(p_far)),
+        [whole(c_far.shape), group(slices, (rows, width))]
+        + [whole((slices * rows, width))] * len(p_far),
         group(slices, (rows, width)),
         jax.ShapeDtypeStruct((slices, rows, width), BF16),
         [],
@@ -532,11 +531,17 @@
     cot = cotangent.astype(BF16)
     cot = cotangent_order(cot, *to_sec([cot] * n_sec))
     early = max(slices // 3, 1)
-    pieces = [
-        jnp.concatenate([projectors[:early], corner[None], cot[None]], axis=0),
-        projectors[early:],
-    ]
-    near = [swap(p, "env", 1) for p in pieces]
+    ahead = early * rows
+
+    def first_piece(m):
+        block = lax.dynamic_slice_in_dim(corner, (y ^ m) * 2 * rows, 2 * rows, 1)
+        block = jnp.concatenate([block[: rows // 2], block[rows // 2 :]], axis=1)
+        block = jnp.pad(block, ((0, 0), (0, width - block.shape[1])))
+        return jnp.concatenate([projectors[:early].reshape(ahead, width), cot, block], axis=0)
+
+    first = [first_piece(m) for m in range(n // 2)]
+    second = projectors[early:]
+    near = [swap(first[0], "env", 1), swap(second, "env", 1)]
     c_parts = jnp.stack(
         [lax.dynamic_slice_in_dim(corner, (e ^ m) * rows, rows, 1) for m in range(n)]
     )
@@ -544,37 +549,44 @@
     begun = begin(c_parts, edges, e_near)
 
     def corner_columns(piece):
-        return lax.dynamic_slice_in_dim(piece[early], e * rows, rows, 1)
-
-    c_near = jnp.stack([corner_columns(pieces[0]).T, corner_columns(near[0]).T])
-    mixing = [begin(c_near, p, q) for p, q in zip(pieces, near)]
-    mixing[0] = mixing[0][:early]
+        block = piece[ahead + rows :]
+        block = jnp.concatenate([block[:, : 2 * rows], block[:, 2 * rows : 4 * rows]], axis=0)
+        return lax.dynamic_slice_in_dim(block, core * rows, rows, 1)
+
+    c_near = jnp.stack([corner_columns(first[0]).T, corner_columns(near[0]).T])
+    near_early = near[0][:ahead].reshape(early, rows, width)
+    mixing = [
+        begin(c_near, projectors[:early], near_early),
+        begin(c_near, second, near[1]),
+    ]
     far = barrier(far, begun, mixing)
-    p_far = [from_chips(pieces[0])]
+    p_far = to_chips(first)
     e_blocks = [edges, e_near, *both_cores(far)]
 
     order = Order()
 
     enlarged, keep, send = order(
         lambda *f: absorb(me, tile_counts, c_parts, begun, f, projectors), *e_blocks[2:])
-    moved, total = order(add_core, keep, swap(send, "env", 1))
+    half = n_sec // 2
+    moved, total = order(
+        add_core, keep, swap(send[:half], "env", 1), swap(send[half:], "env", 1))
     sec = to_sec(moved)
-    total = barrier(total, p_far[0])
+    total = barrier(total, p_far)
     some = order(add_sec, total, *sec)
     some = order(add_chips, some, *from_chips(some))
     half = all_sec(some)
-    p_far += [from_chips(barrier(p, some)) for p in pieces[1:]]
-    p_far[0] = both_cores(barrier(p_far[0], some))
-    cots = [pieces[0], near[0], *p_far[0]]
-    c_far = jnp.stack([corner_columns(p) for p in p_far[0]])
-    q = order(lambda c: mix(c, mixing[0], p_far[0]), c_far)
+    second_far = from_chips(barrier(second, some))
+    p_far = both_cores(barrier(p_far, some))
+    cots = [first[0], near[0], *p_far]
+    c_far = jnp.stack([corner_columns(p) for p in p_far])
+    q = order(lambda c: mix(c, mixing[0], p_far), c_far)
     half = barrier(half, order.last)
     halves = half + [swap(h, "env", 1) for h in half]
     if piece % 16:
         halves = list(
             relative(jnp.concatenate(halves), me, n_sec, n // 2).reshape(2 * n_sec, -1, width))
     g, corner_new, part = order(
-        lambda *h: gradient(me, tile_counts, h, cots, early + 1, projectors, e_blocks), *halves)
+        lambda *h: gradient(me, tile_counts, h, cots, ahead, projectors, e_blocks), *halves)
     moved = to_sec(part)
     proj_grad = order(
         lambda g: outputs(
@@ -583,7 +595,7 @@
         lambda g: outputs("edge_gradient", tile_counts, g, q, slices, ((1,), (0,))), g)
     corner_grad = order(
         lambda *b: sum((x.astype(F32) for x in b[1:]), b[0].astype(F32)), part[0], *moved)
-    p_far = both_cores(barrier(p_far[1], corner_grad))
+    p_far = both_cores(barrier(second_far, corner_grad))
     begun = order(lambda b, *p: add_far(c_far, b, p), mixing[1], *p_far[:-1])
     edge_grad = order(
         lambda r, b, p: late_edge_gradient(r, tile_counts, g, c_far[-1], b, p, early),

time: 154 us -> 149 us (0.968)
  waiting for transfers between devices: 71.4 us -> 59.4 us
  other arithmetic: 6.63 us -> 12.5 us
  local copies, waits for them, and re-layouts: 5.94 us -> 11.2 us
  Pallas kernels: 39.9 us -> 36.4 us
    ppermute x27 -> x28, waiting for transfers between devices: 71.4 us -> 59.4 us  [swap(): return lax.ppermute(value, axis, [(i, i ^ offset) for i in range(size)])]
    concatenate x1 -> x2, other arithmetic: 2.43 us -> 6.82 us  [the longest x1 6.66 us: first_piece(): jnp.concatenate([projectors[:early].reshape(ahead, width), cot, block], a...]
    pallas_call x5, Pallas kernels: 13.2 us -> 9.87 us  [call(): pl.pallas_call(kernel, grid_spec=pltpu.PrefetchScalarGridSpec(num_scalar_...]
    another operation x0 -> x2, local copies, waits for them, and re-layouts: none -> 3.13 us  [per_device(): c_near = jnp.stack([corner_columns(first[0]).T, corner_columns(near[0]).T])]
    slice x7 -> x8, local copies, waits for them, and re-layouts: 3.71 us -> 5.83 us  [the longest x1 1.33 us: per_device(): second = projectors[early:]]
    ppermute x27 -> x28, starting transfers between devices: 28.9 us -> 28.4 us  [swap(): return lax.ppermute(value, axis, [(i, i ^ offset) for i in range(size)])]
  transfers between devices with their start and end apart: 27 -> 28, of which waited for: 16 -> 14; matrix products, arithmetic and copies ran while one was open for 8% -> 14% of each run, Pallas kernels for 23% -> 22%
where the time goes in v5:
time: 149 us
  waiting for transfers between devices  59.4 us (40%)
  Pallas kernels  36.4 us (24%)
  starting transfers between devices  28.4 us (19%)
  other arithmetic  12.5 us (8%)
  local copies, waits for them, and re-layouts  11.2 us (8%)
    ppermute x28, waiting for transfers between devices, swap(): return lax.ppermute(value, axis, [(i, i ^ offset) for i in range(size)])  59.4 us
    ppermute x28, starting transfers between devices, swap(): return lax.ppermute(value, axis, [(i, i ^ offset) for i in range(size)])  28.4 us
    pallas_call x5, Pallas kernels, at_once(): pl.pallas_call(kernel, in_specs=[SCALARS] * len(scalars) + [ARRAY] * len(...  26.5 us
    pallas_call x5, Pallas kernels, call(): pl.pallas_call(kernel, grid_spec=pltpu.PrefetchScalarGridSpec(num_scalar_...  9.87 us
    concatenate x1, other arithmetic, first_piece(): jnp.concatenate([projectors[:early].reshape(ahead, width), cot, block], a...  6.66 us
    another operation x2, local copies, waits for them, and re-layouts, per_device(): c_near = jnp.stack([corner_columns(first[0]).T, corner_columns(near[0]).T])  3.13 us
  transfers between devices with their start and end apart: 28, of which 14 were waited for; matrix products, arithmetic and copies ran while one was open for 14% of the time, Pallas kernels for 22%

profile of v5, /device:TPU:0, one launch (start us, length us, event | category | flops | bytes accessed | tf_op | source)
XLA Modules:
  0.0 148.9 jit_solution(6146616908526372972)
XLA Ops:
  1.1 2.6 %collective-permute-start.1 = (bf16[9,192,768]{2,1,0:T(8,128)(2,1)}, bf16[9,192,768]{2,1,0:T(8,128)(2,1)}, u32[]{:S(2)}, u32[]{:S(2)}) collective-permute-start(bf16[9,192,768]{2,1,0:T(8,128)(2,1)} %refs_14_.1), channel_id=1, source_target_pairs={{0,8},{4,12},{8,0},{12,4},{1,9},{5,13},{9,1},{13,5},{2,10},{6,14},... | collective-permute-start | bytes 7962632 | tf_op jit(solution)/shard_map/ppermute | solution.py:17
  6.9 2.6 %collective-permute-start.3 = (bf16[192,192]{1,0:T(8,128)(2,1)}, bf16[192,192]{1,0:T(8,128)(2,1)}, u32[]{:S(2)}, u32[]{:S(2)}) collective-permute-start(bf16[192,192]{1,0:T(8,128)(2,1)} %convert_element_type.71), channel_id=1, source_target_pairs={{0,2},{1,3},{2,0},{3,1},{4,6},{5,7},{6,4},{7,5},{8,10},{9,11},{10,... | collective-permute-start | bytes 221192 | tf_op jit(solution)/shard_map/ppermute | solution.py:17
  12.0 5.9 %collective-permute-done.3 = bf16[192,192]{1,0:T(8,128)(2,1)} collective-permute-done((bf16[192,192]{1,0:T(8,128)(2,1)}, bf16[192,192]{1,0:T(8,128)(2,1)}, u32[]{:S(2)}, u32[]{:S(2)}) %collective-permute-start.3) | collective-permute-done | bytes 73760 | tf_op jit(solution)/shard_map/ppermute | solution.py:17
  19.0 6.7 %maximum_maximum_fusion.2 = (bf16[864,768]{1,0:T(8,128)(2,1)}, bf16[864,768]{1,0:T(8,128)(2,1)}) fusion(bf16[96,384]{1,0:T(8,128)(2,1)S(1)} %get-tuple-element.118, bf16[96,384]{1,0:T(8,128)(2,1)S(1)} %get-tuple-element.116, bf16[192,192]{1,0:T(8,128)(2,1)S(1)} %get-tuple-element.113, bf16[192,192]{1,0:T(8,128)(2,1)S(1)} %get-tuple-element.114, ...), kind=kLoop, calls=%fused_computation.2 | loop fusion | flops 12607488 | bytes 4128768 | tf_op jit(solution)/shard_map/concatenate | solution.py:540
  37.3 2.9 %begin.5.begun = f32[6,192,768]{2,1,0:T(8,128)S(1)} custom-call(bf16[2,192,192]{2,1,0:T(8,128)(2,1)S(1)} %copy-done.7, bf16[6,192,768]{2,1,0:T(8,128)(2,1)} %slice.103.own, bf16[6,192,768]{2,1,0:T(8,128)(2,1)} %collective-permute-done.6.near), custom_call_target="tpu_custom_call" | custom-call | flops 1000 | bytes 1000 | tf_op jit(solution)/shard_map/begin/pallas_call | solution.py:29
  40.2 3.7 %begin.3.begun = f32[9,192,768]{2,1,0:T(8,128)S(1)} custom-call(bf16[4,192,192]{2,1,0:T(8,128)(2,1)S(1)} %copy-done.4, bf16[9,192,768]{2,1,0:T(8,128)(2,1)S(1)} %copy-done.1, bf16[9,192,768]{2,1,0:T(8,128)(2,1)} %collective-permute-done.near.refs_15_), custom_call_target="tpu_custom_call" | custom-call | flops 1000 | bytes 1000 | tf_op jit(solution)/shard_map/begin/pallas_call | solution.py:29
  43.9 18.3 %collective-permute-done.1.refs_0_.refs_16_ = bf16[9,192,768]{2,1,0:T(8,128)(2,1)} collective-permute-done((bf16[9,192,768]{2,1,0:T(8,128)(2,1)}, bf16[9,192,768]{2,1,0:T(8,128)(2,1)}, u32[]{:S(2)}, u32[]{:S(2)}) %collective-permute-start.1) | collective-permute-done | bytes 2654240 | tf_op jit(solution)/shard_map/ppermute | solution.py:17
  64.1 3.3 %collective-permute-done.7.fwd.refs_9_ = bf16[9,192,768]{2,1,0:T(8,128)(2,1)S(1)} collective-permute-done((bf16[9,192,768]{2,1,0:T(8,128)(2,1)}, bf16[9,192,768]{2,1,0:T(8,128)(2,1)S(1)}, u32[]{:S(2)}, u32[]{:S(2)}) %collective-permute-start.7) | collective-permute-done | bytes 2654240 | tf_op jit(solution)/shard_map/ppermute | solution.py:17
  67.4 6.8 %absorb.1 = (bf16[9,192,768]{2,1,0:T(8,128)(2,1)S(1)}, f32[384,768]{1,0:T(8,128)S(1)}, bf16[384,768]{1,0:T(8,128)(2,1)S(1)}) custom-call(s32[2]{0:T(128)S(1)} %pad_add_fusion.me, s32[9]{0:T(128)S(1)} %copy-done.8, bf16[4,192,192]{2,1,0:T(8,128)(2,1)S(1)} %copy-done.4, bf16[9,192,768]{2,1,0:T(8,128)(2,1)S(1)} %copy-done, f32[9,192,768]{2,1,0:T(8,128)S(1)} %begin.3.begun, ...), custom_call_target="tpu_custom_call" | custom-call | flops 1000 | bytes 1000 | tf_op jit(solution)/shard_map/absorb/pallas_call | solution.py:148
  76.4 3.9 %collective-permute-start.13 = (bf16[96,768]{1,0:T(8,128)(2,1)S(1)}, bf16[96,768]{1,0:T(8,128)(2,1)S(1)}, u32[]{:S(2)}, u32[]{:S(2)}) collective-permute-start(bf16[96,768]{1,0:T(8,128)(2,1)S(1)} %get-tuple-element.92), channel_id=1, source_target_pairs={{0,3},{1,2},{2,1},{3,0},{4,7},{5,6},{6,5},{7,4},{8,11},{9,10},{10,... | collective-permute-start | bytes 442376 | tf_op jit(solution)/shard_map/ppermute | solution.py:17
  81.0 12.8 %collective-permute-done.10.refs_0_.refs_12_ = bf16[864,768]{1,0:T(8,128)(2,1)S(1)} collective-permute-done((bf16[864,768]{1,0:T(8,128)(2,1)S(1)}, bf16[864,768]{1,0:T(8,128)(2,1)S(1)}, u32[]{:S(2)}, u32[]{:S(2)}) %collective-permute-start.10) | collective-permute-done | bytes 1327136 | tf_op jit(solution)/shard_map/ppermute | solution.py:17
  93.9 1.8 %collective-permute-start.14 = (bf16[96,768]{1,0:T(8,128)(2,1)S(1)}, bf16[96,768]{1,0:T(8,128)(2,1)S(1)}, u32[]{:S(2)}, u32[]{:S(2)}) collective-permute-start(bf16[96,768]{1,0:T(8,128)(2,1)S(1)} %add_convert_fusion.1), channel_id=1, source_target_pairs={{0,8},{4,12},{8,0},{12,4},{1,9},{5,13},{9,1},{13,5},{2,10},{6,14},... | collective-permute-start | bytes 442376 | tf_op jit(solution)/shard_map/ppermute | solution.py:17
  95.7 3.8 %collective-permute-done.14 = bf16[96,768]{1,0:T(8,128)(2,1)S(1)} collective-permute-done((bf16[96,768]{1,0:T(8,128)(2,1)S(1)}, bf16[96,768]{1,0:T(8,128)(2,1)S(1)}, u32[]{:S(2)}, u32[]{:S(2)}) %collective-permute-start.14) | collective-permute-done | bytes 147488 | tf_op jit(solution)/shard_map/ppermute | solution.py:17
  101.4 3.6 %collective-permute-start.17 = (bf16[96,768]{1,0:T(8,128)(2,1)S(1)}, bf16[96,768]{1,0:T(8,128)(2,1)S(1)}, u32[]{:S(2)}, u32[]{:S(2)}) collective-permute-start(bf16[96,768]{1,0:T(8,128)(2,1)S(1)} %add_convert_fusion.refs_0_), channel_id=1, source_target_pairs={{0,3},{1,2},{2,1},{3,0},{4,7},{5,6},{6,5},{7,4},{8,11},{9,10},{10,... | collective-permute-start | bytes 442376 | tf_op jit(solution)/shard_map/ppermute | solution.py:17
  106.9 3.1 %collective-permute-done.17.refs_3_ = bf16[96,768]{1,0:T(8,128)(2,1)S(1)} collective-permute-done((bf16[96,768]{1,0:T(8,128)(2,1)S(1)}, bf16[96,768]{1,0:T(8,128)(2,1)S(1)}, u32[]{:S(2)}, u32[]{:S(2)}) %collective-permute-start.17) | collective-permute-done | bytes 147488 | tf_op jit(solution)/shard_map/ppermute | solution.py:17
  110.0 7.8 %collective-permute-done.16.refs_2_ = bf16[96,768]{1,0:T(8,128)(2,1)S(1)} collective-permute-done((bf16[96,768]{1,0:T(8,128)(2,1)S(1)}, bf16[96,768]{1,0:T(8,128)(2,1)S(1)}, u32[]{:S(2)}, u32[]{:S(2)}) %collective-permute-start.16) | collective-permute-done | bytes 147488 | tf_op jit(solution)/shard_map/ppermute | solution.py:17
  119.9 9.0 %gradient.1 = (bf16[768,768]{1,0:T(8,128)(2,1)S(1)}, f32[192,192]{1,0:T(8,128)}, bf16[4,192,192]{2,1,0:T(8,128)(2,1)S(1)}) custom-call(s32[2]{0:T(128)S(1)} %pad_add_fusion.me, s32[9]{0:T(128)S(1)} %copy-done.8, bf16[96,768]{1,0:T(8,128)(2,1)S(1)} %add_convert_fusion.refs_0_, bf16[96,768]{1,0:T(8,128)(2,1)S(1)} %collective-permute-done.15.refs_1_, ...), custom_call_target="tpu_custom_call" | custom-call | flops 1000 | bytes 26542080 | tf_op jit(solution)/shard_map/gradient/pallas_call | solution.py:148
  129.0 2.5 %collective-permute-start.25 = (bf16[192,192]{1,0:T(8,128)(2,1)S(1)}, bf16[192,192]{1,0:T(8,128)(2,1)S(1)}, u32[]{:S(2)}, u32[]{:S(2)}) collective-permute-start(bf16[192,192]{1,0:T(8,128)(2,1)S(1)} %get-tuple-element.108), channel_id=1, source_target_pairs={{0,3},{1,2},{2,1},{3,0},{4,7},{5,6},{6,5},{7,4},{8,11},{9,10},{10,... | collective-permute-start | bytes 221192 | tf_op jit(solution)/shard_map/ppermute | solution.py:17
  131.5 1.9 %collective-permute-start.23 = (bf16[192,192]{1,0:T(8,128)(2,1)S(1)}, bf16[192,192]{1,0:T(8,128)(2,1)S(1)}, u32[]{:S(2)}, u32[]{:S(2)}) collective-permute-start(bf16[192,192]{1,0:T(8,128)(2,1)S(1)} %get-tuple-element.110), channel_id=1, source_target_pairs={{0,1},{1,0},{2,3},{3,2},{4,5},{5,4},{6,7},{7,6},{8,9},{9,8},{10,11... | collective-permute-start | bytes 221192 | tf_op jit(solution)/shard_map/ppermute | solution.py:17
  133.4 4.2 %proj_gradient.1 = f32[9,192,768]{2,1,0:T(8,128)} custom-call(s32[9]{0:T(128)S(1)} %copy-done.8, bf16[768,768]{1,0:T(8,128)(2,1)S(1)} %get-tuple-element.80.g_ref, bf16[9,192,768]{2,1,0:T(8,128)(2,1)S(1)} %copy-done.6), custom_call_target="tpu_custom_call" | custom-call | flops 1000 | bytes 1000 | tf_op jit(solution)/shard_map/proj_gradient/pallas_call | solution.py:148
  137.6 2.6 %edge_gradient.1._ = f32[9,192,768]{2,1,0:T(8,128)} custom-call(s32[9]{0:T(128)S(1)} %copy-done.8, bf16[768,768]{1,0:T(8,128)(2,1)S(1)} %get-tuple-element.80.g_ref, bf16[3,192,768]{2,1,0:T(8,128)(2,1)S(1)} %mix.1.x_ref), custom_call_target="tpu_custom_call" | custom-call | flops 1000 | bytes 1000 | tf_op jit(solution)/shard_map/edge_gradient/pallas_call | solution.py:148
  141.0 2.1 %add_far.1.begun = f32[6,192,768]{2,1,0:T(8,128)S(1)} custom-call(bf16[2,192,192]{2,1,0:T(8,128)(2,1)S(1)} %pad_maximum_fusion.2.c_ref, f32[6,192,768]{2,1,0:T(8,128)S(1)} %begin.5.begun, bf16[6,192,768]{2,1,0:T(8,128)(2,1)} %collective-permute-done.26.refs_0_), custom_call_target="tpu_custom_call" | custom-call | flops 1000 | bytes 1000 | tf_op jit(solution)/shard_map/add_far/pallas_call | solution.py:29
  143.0 1.8 %collective-permute-done.27.fwd = bf16[6,192,768]{2,1,0:T(8,128)(2,1)S(1)} collective-permute-done((bf16[6,192,768]{2,1,0:T(8,128)(2,1)}, bf16[6,192,768]{2,1,0:T(8,128)(2,1)S(1)}, u32[]{:S(2)}, u32[]{:S(2)}) %collective-permute-start.27) | collective-permute-done | bytes 1769504 | tf_op jit(solution)/shard_map/ppermute | solution.py:17
  144.9 3.9 %late_edge_gradient.1 = f32[9,192,768]{2,1,0:T(8,128)} custom-call(s32[9]{0:T(128)S(1)} %copy-done.8, bf16[768,768]{1,0:T(8,128)(2,1)S(1)} %get-tuple-element.80.g_ref, bf16[192,192]{1,0:T(8,128)(2,1)S(1)} %fusion.3.c_ref, f32[6,192,768]{2,1,0:T(8,128)S(1)} %add_far.1.begun, ...), custom_call_target="tpu_custom_call", output_to_operand_aliasing={{}: (5, {})} | custom-call | flops 1000 | bytes 1000 | tf_op jit(solution)/shard_map/late_edge_gradient/pallas_call | solution.py:148
  (88 shorter events, 30.3 us)
Async XLA Ops:
  0.6 39.5 %collective-permute-start = (bf16[9,192,768]{2,1,0:T(8,128)(2,1)}, bf16[9,192,768]{2,1,0:T(8,128)(2,1)}, u32[]{:S(2)}, u32[]{:S(2)}) collective-permute-start(bf16[9,192,768]{2,1,0:T(8,128)(2,1)} %refs_14_.1), channel_id=1, source_target_pairs={{0,4},{4,0},{8,12},{12,8},{1,5},{5,1},{9,13},{13,9},{2,6},{6,2},{1... | collective-permute-start | bytes 7962632 | tf_op jit(solution)/shard_map/ppermute | solution.py:17
  1.1 61.1 %collective-permute-start.1 = (bf16[9,192,768]{2,1,0:T(8,128)(2,1)}, bf16[9,192,768]{2,1,0:T(8,128)(2,1)}, u32[]{:S(2)}, u32[]{:S(2)}) collective-permute-start(bf16[9,192,768]{2,1,0:T(8,128)(2,1)} %refs_14_.1), channel_id=1, source_target_pairs={{0,8},{4,12},{8,0},{12,4},{1,9},{5,13},{9,1},{13,5},{2,10},{6,14},... | collective-permute-start | bytes 7962632 | tf_op jit(solution)/shard_map/ppermute | solution.py:17
  5.3 6.7 %collective-permute-start.4 = (bf16[192,192]{1,0:T(8,128)(2,1)}, bf16[192,192]{1,0:T(8,128)(2,1)}, u32[]{:S(2)}, u32[]{:S(2)}) collective-permute-start(bf16[192,192]{1,0:T(8,128)(2,1)} %convert_element_type.71), channel_id=1, source_target_pairs={{0,1},{1,0},{2,3},{3,2},{4,5},{5,4},{6,7},{7,6},{8,9},{9,8},{10,11... | collective-permute-start | bytes 221192 | tf_op jit(solution)/shard_map/ppermute | solution.py:17
  6.9 11.0 %collective-permute-start.3 = (bf16[192,192]{1,0:T(8,128)(2,1)}, bf16[192,192]{1,0:T(8,128)(2,1)}, u32[]{:S(2)}, u32[]{:S(2)}) collective-permute-start(bf16[192,192]{1,0:T(8,128)(2,1)} %convert_element_type.71), channel_id=1, source_target_pairs={{0,2},{1,3},{2,0},{3,1},{4,6},{5,7},{6,4},{7,5},{8,10},{9,11},{10,... | collective-permute-start | bytes 221192 | tf_op jit(solution)/shard_map/ppermute | solution.py:17
  9.5 8.4 %collective-permute-start.2 = (bf16[192,192]{1,0:T(8,128)(2,1)}, bf16[192,192]{1,0:T(8,128)(2,1)}, u32[]{:S(2)}, u32[]{:S(2)}) collective-permute-start(bf16[192,192]{1,0:T(8,128)(2,1)} %convert_element_type.71), channel_id=1, source_target_pairs={{0,3},{1,2},{2,1},{3,0},{4,7},{5,6},{6,5},{7,4},{8,11},{9,10},{10,... | collective-permute-start | bytes 221192 | tf_op jit(solution)/shard_map/ppermute | solution.py:17
  25.6 4.1 %collective-permute-start.5 = (bf16[864,768]{1,0:T(8,128)(2,1)}, bf16[864,768]{1,0:T(8,128)(2,1)}, u32[]{:S(2)}, u32[]{:S(2)}) collective-permute-start(bf16[864,768]{1,0:T(8,128)(2,1)} %get-tuple-element.103.refs_10_), channel_id=1, source_target_pairs={{0,4},{4,0},{8,12},{12,8},{1,5},{5,1},{9,13},{13,9},{2,6},{6,2},{1... | collective-permute-start | bytes 3981320 | tf_op jit(solution)/shard_map/ppermute | solution.py:17
  27.0 10.3 %collective-permute-start.6 = (bf16[6,192,768]{2,1,0:T(8,128)(2,1)}, bf16[6,192,768]{2,1,0:T(8,128)(2,1)}, u32[]{:S(2)}, u32[]{:S(2)}) collective-permute-start(bf16[6,192,768]{2,1,0:T(8,128)(2,1)} %slice.103.own), channel_id=1, source_target_pairs={{0,4},{4,0},{8,12},{12,8},{1,5},{5,1},{9,13},{13,9},{2,6},{6,2},{1... | collective-permute-start | bytes 5308424 | tf_op jit(solution)/shard_map/ppermute | solution.py:17
  62.2 5.2 %collective-permute-start.7 = (bf16[9,192,768]{2,1,0:T(8,128)(2,1)}, bf16[9,192,768]{2,1,0:T(8,128)(2,1)S(1)}, u32[]{:S(2)}, u32[]{:S(2)}) collective-permute-start(bf16[9,192,768]{2,1,0:T(8,128)(2,1)} %collective-permute-done.1.refs_0_.refs_16_), channel_id=1, source_target_pairs={{0,4},{4,0},{8,12},{12,8},{1,5},{5,1},{9,13},{13,9},{2,6},{6,2},{1... | collective-permute-start | bytes 7962632 | tf_op jit(solution)/shard_map/ppermute | solution.py:17
  62.2 31.6 %collective-permute-start.10 = (bf16[864,768]{1,0:T(8,128)(2,1)S(1)}, bf16[864,768]{1,0:T(8,128)(2,1)S(1)}, u32[]{:S(2)}, u32[]{:S(2)}) collective-permute-start(bf16[864,768]{1,0:T(8,128)(2,1)S(1)} %copy-done.9), channel_id=1, source_target_pairs={{0,8},{4,12},{8,0},{12,4},{1,9},{5,13},{9,1},{13,5},{2,10},{6,14},... | collective-permute-start | bytes 3981320 | tf_op jit(solution)/shard_map/ppermute | solution.py:17
  74.3 1.6 %collective-permute-start.8 = (bf16[2,96,768]{2,1,0:T(8,128)(2,1)S(1)}, bf16[2,96,768]{2,1,0:T(8,128)(2,1)S(1)}, u32[]{:S(2)}, u32[]{:S(2)}) collective-permute-start(bf16[2,96,768]{2,1,0:T(8,128)(2,1)S(1)} %bitcast.47), channel_id=1, source_target_pairs={{0,4},{4,0},{8,12},{12,8},{1,5},{5,1},{9,13},{13,9},{2,6},{6,2},{1... | collective-permute-start | bytes 884744 | tf_op jit(solution)/shard_map/ppermute | solution.py:17
  74.5 1.9 %collective-permute-start.9 = (bf16[2,96,768]{2,1,0:T(8,128)(2,1)S(1)}, bf16[2,96,768]{2,1,0:T(8,128)(2,1)S(1)}, u32[]{:S(2)}, u32[]{:S(2)}) collective-permute-start(bf16[2,96,768]{2,1,0:T(8,128)(2,1)S(1)} %bitcast.46), channel_id=1, source_target_pairs={{0,4},{4,0},{8,12},{12,8},{1,5},{5,1},{9,13},{13,9},{2,6},{6,2},{1... | collective-permute-start | bytes 884744 | tf_op jit(solution)/shard_map/ppermute | solution.py:17
  76.4 17.3 %collective-permute-start.13 = (bf16[96,768]{1,0:T(8,128)(2,1)S(1)}, bf16[96,768]{1,0:T(8,128)(2,1)S(1)}, u32[]{:S(2)}, u32[]{:S(2)}) collective-permute-start(bf16[96,768]{1,0:T(8,128)(2,1)S(1)} %get-tuple-element.92), channel_id=1, source_target_pairs={{0,3},{1,2},{2,1},{3,0},{4,7},{5,6},{6,5},{7,4},{8,11},{9,10},{10,... | collective-permute-start | bytes 442376 | tf_op jit(solution)/shard_map/ppermute | solution.py:17
  80.3 13.4 %collective-permute-start.12 = (bf16[96,768]{1,0:T(8,128)(2,1)S(1)}, bf16[96,768]{1,0:T(8,128)(2,1)S(1)}, u32[]{:S(2)}, u32[]{:S(2)}) collective-permute-start(bf16[96,768]{1,0:T(8,128)(2,1)S(1)} %get-tuple-element.93), channel_id=1, source_target_pairs={{0,2},{1,3},{2,0},{3,1},{4,6},{5,7},{6,4},{7,5},{8,10},{9,11},{10,... | collective-permute-start | bytes 442376 | tf_op jit(solution)/shard_map/ppermute | solution.py:17
  80.3 13.4 %collective-permute-start.11 = (bf16[96,768]{1,0:T(8,128)(2,1)S(1)}, bf16[96,768]{1,0:T(8,128)(2,1)S(1)}, u32[]{:S(2)}, u32[]{:S(2)}) collective-permute-start(bf16[96,768]{1,0:T(8,128)(2,1)S(1)} %get-tuple-element.105), channel_id=1, source_target_pairs={{0,1},{1,0},{2,3},{3,2},{4,5},{5,4},{6,7},{7,6},{8,9},{9,8},{10,11... | collective-permute-start | bytes 442376 | tf_op jit(solution)/shard_map/ppermute | solution.py:17
  93.9 5.6 %collective-permute-start.14 = (bf16[96,768]{1,0:T(8,128)(2,1)S(1)}, bf16[96,768]{1,0:T(8,128)(2,1)S(1)}, u32[]{:S(2)}, u32[]{:S(2)}) collective-permute-start(bf16[96,768]{1,0:T(8,128)(2,1)S(1)} %add_convert_fusion.1), channel_id=1, source_target_pairs={{0,8},{4,12},{8,0},{12,4},{1,9},{5,13},{9,1},{13,5},{2,10},{6,14},... | collective-permute-start | bytes 442376 | tf_op jit(solution)/shard_map/ppermute | solution.py:17
  99.5 6.5 %collective-permute-start.18 = (bf16[864,768]{1,0:T(8,128)(2,1)S(1)}, bf16[864,768]{1,0:T(8,128)(2,1)S(1)}, u32[]{:S(2)}, u32[]{:S(2)}) collective-permute-start(bf16[864,768]{1,0:T(8,128)(2,1)S(1)} %collective-permute-done.10.refs_0_.refs_12_), channel_id=1, source_target_pairs={{0,4},{4,0},{8,12},{12,8},{1,5},{5,1},{9,13},{13,9},{2,6},{6,2},{1... | collective-permute-start | bytes 3981320 | tf_op jit(solution)/shard_map/ppermute | solution.py:17
  99.6 41.4 %collective-permute-start.26 = (bf16[6,192,768]{2,1,0:T(8,128)(2,1)}, bf16[6,192,768]{2,1,0:T(8,128)(2,1)}, u32[]{:S(2)}, u32[]{:S(2)}) collective-permute-start(bf16[6,192,768]{2,1,0:T(8,128)(2,1)} %slice.103.own), channel_id=1, source_target_pairs={{0,8},{4,12},{8,0},{12,4},{1,9},{5,13},{9,1},{13,5},{2,10},{6,14},... | collective-permute-start | bytes 5308424 | tf_op jit(solution)/shard_map/ppermute | solution.py:17
  101.4 8.6 %collective-permute-start.17 = (bf16[96,768]{1,0:T(8,128)(2,1)S(1)}, bf16[96,768]{1,0:T(8,128)(2,1)S(1)}, u32[]{:S(2)}, u32[]{:S(2)}) collective-permute-start(bf16[96,768]{1,0:T(8,128)(2,1)S(1)} %add_convert_fusion.refs_0_), channel_id=1, source_target_pairs={{0,3},{1,2},{2,1},{3,0},{4,7},{5,6},{6,5},{7,4},{8,11},{9,10},{10,... | collective-permute-start | bytes 442376 | tf_op jit(solution)/shard_map/ppermute | solution.py:17
  105.0 12.8 %collective-permute-start.16 = (bf16[96,768]{1,0:T(8,128)(2,1)S(1)}, bf16[96,768]{1,0:T(8,128)(2,1)S(1)}, u32[]{:S(2)}, u32[]{:S(2)}) collective-permute-start(bf16[96,768]{1,0:T(8,128)(2,1)S(1)} %add_convert_fusion.refs_0_), channel_id=1, source_target_pairs={{0,2},{1,3},{2,0},{3,1},{4,6},{5,7},{6,4},{7,5},{8,10},{9,11},{10,... | collective-permute-start | bytes 442376 | tf_op jit(solution)/shard_map/ppermute | solution.py:17
  105.0 12.8 %collective-permute-start.15 = (bf16[96,768]{1,0:T(8,128)(2,1)S(1)}, bf16[96,768]{1,0:T(8,128)(2,1)S(1)}, u32[]{:S(2)}, u32[]{:S(2)}) collective-permute-start(bf16[96,768]{1,0:T(8,128)(2,1)S(1)} %add_convert_fusion.refs_0_), channel_id=1, source_target_pairs={{0,1},{1,0},{2,3},{3,2},{4,5},{5,4},{6,7},{7,6},{8,9},{9,8},{10,11... | collective-permute-start | bytes 442376 | tf_op jit(solution)/shard_map/ppermute | solution.py:17
  129.0 11.2 %collective-permute-start.25 = (bf16[192,192]{1,0:T(8,128)(2,1)S(1)}, bf16[192,192]{1,0:T(8,128)(2,1)S(1)}, u32[]{:S(2)}, u32[]{:S(2)}) collective-permute-start(bf16[192,192]{1,0:T(8,128)(2,1)S(1)} %get-tuple-element.108), channel_id=1, source_target_pairs={{0,3},{1,2},{2,1},{3,0},{4,7},{5,6},{6,5},{7,4},{8,11},{9,10},{10,... | collective-permute-start | bytes 221192 | tf_op jit(solution)/shard_map/ppermute | solution.py:17
  131.5 8.7 %collective-permute-start.24 = (bf16[192,192]{1,0:T(8,128)(2,1)S(1)}, bf16[192,192]{1,0:T(8,128)(2,1)S(1)}, u32[]{:S(2)}, u32[]{:S(2)}) collective-permute-start(bf16[192,192]{1,0:T(8,128)(2,1)S(1)} %get-tuple-element.109), channel_id=1, source_target_pairs={{0,2},{1,3},{2,0},{3,1},{4,6},{5,7},{6,4},{7,5},{8,10},{9,11},{10,... | collective-permute-start | bytes 221192 | tf_op jit(solution)/shard_map/ppermute | solution.py:17
  131.5 8.7 %collective-permute-start.23 = (bf16[192,192]{1,0:T(8,128)(2,1)S(1)}, bf16[192,192]{1,0:T(8,128)(2,1)S(1)}, u32[]{:S(2)}, u32[]{:S(2)}) collective-permute-start(bf16[192,192]{1,0:T(8,128)(2,1)S(1)} %get-tuple-element.110), channel_id=1, source_target_pairs={{0,1},{1,0},{2,3},{3,2},{4,5},{5,4},{6,7},{7,6},{8,9},{9,8},{10,11... | collective-permute-start | bytes 221192 | tf_op jit(solution)/shard_map/ppermute | solution.py:17
  141.0 3.9 %collective-permute-start.27 = (bf16[6,192,768]{2,1,0:T(8,128)(2,1)}, bf16[6,192,768]{2,1,0:T(8,128)(2,1)S(1)}, u32[]{:S(2)}, u32[]{:S(2)}) collective-permute-start(bf16[6,192,768]{2,1,0:T(8,128)(2,1)} %collective-permute-done.26.refs_0_), channel_id=1, source_target_pairs={{0,4},{4,0},{8,12},{12,8},{1,5},{5,1},{9,13},{13,9},{2,6},{6,2},{1... | collective-permute-start | bytes 5308424 | tf_op jit(solution)/shard_map/ppermute | solution.py:17
  (14 other events, 158.5 us)

commit v6 on v5

--- a/solution.py
+++ b/solution.py
@@ -313,12 +313,10 @@
         picked = jnp.where(me[1] == q, own[:, q * cols : (q + 1) * cols], picked)
     own_ref[...] = picked.astype(F32) * scale
 
-    for k in range(slices // per):
-        x = dot(p_ref[k * per : k * per + per].reshape(per * rows, width), g_ref[...])
-        for i in range(per):
-            part = x[i * rows : (i + 1) * rows]
-            keep = keep_columns(part.shape, 0, counts[k * per + i])
-            grad[k * per + i] = jnp.where(keep, part, 0.0).astype(BF16)
+    x = dot(p_ref[...].reshape(slices * rows, width), g_ref[...])
+    for k in range(slices):
+        part = x[k * rows : (k + 1) * rows]
+        grad[k] = jnp.where(keep_columns(part.shape, 0, counts[k]), part, 0.0).astype(BF16)
     for copy in e_copies:
         copy.wait()
     for m in range(n):

time: 149 us -> 149 us (level)
  no operation moved by 1% of the time
where the time goes in v6:
time: 149 us
  waiting for transfers between devices  59.4 us (40%)
  Pallas kernels  36.4 us (24%)
  starting transfers between devices  28.4 us (19%)
  other arithmetic  12.5 us (8%)
  local copies, waits for them, and re-layouts  11.2 us (8%)
    ppermute x28, waiting for transfers between devices, swap(): return lax.ppermute(value, axis, [(i, i ^ offset) for i in range(size)])  59.4 us
    ppermute x28, starting transfers between devices, swap(): return lax.ppermute(value, axis, [(i, i ^ offset) for i in range(size)])  28.4 us
    pallas_call x5, Pallas kernels, at_once(): pl.pallas_call(kernel, in_specs=[SCALARS] * len(scalars) + [ARRAY] * len(...  26.5 us
    pallas_call x5, Pallas kernels, call(): pl.pallas_call(kernel, grid_spec=pltpu.PrefetchScalarGridSpec(num_scalar_...  9.87 us
    concatenate x1, other arithmetic, first_piece(): jnp.concatenate([projectors[:early].reshape(ahead, width), cot, block], a...  6.66 us
    another operation x2, local copies, waits for them, and re-layouts, per_device(): c_near = jnp.stack([corner_columns(first[0]).T, corner_columns(near[0]).T])  3.13 us
  transfers between devices with their start and end apart: 28, of which 14 were waited for; matrix products, arithmetic and copies ran while one was open for 14% of the time, Pallas kernels for 22%

profile of v6, /device:TPU:0, one launch (start us, length us, event | category | flops | bytes accessed | tf_op | source)
XLA Modules:
  0.0 149.0 jit_solution(5750498408660284457)
XLA Ops:
  1.1 2.6 %collective-permute-start.1 = (bf16[9,192,768]{2,1,0:T(8,128)(2,1)}, bf16[9,192,768]{2,1,0:T(8,128)(2,1)}, u32[]{:S(2)}, u32[]{:S(2)}) collective-permute-start(bf16[9,192,768]{2,1,0:T(8,128)(2,1)} %refs_14_.1), channel_id=1, source_target_pairs={{0,8},{4,12},{8,0},{12,4},{1,9},{5,13},{9,1},{13,5},{2,10},{6,14},... | collective-permute-start | bytes 7962632 | tf_op jit(solution)/shard_map/ppermute | solution.py:17
  6.9 2.6 %collective-permute-start.3 = (bf16[192,192]{1,0:T(8,128)(2,1)}, bf16[192,192]{1,0:T(8,128)(2,1)}, u32[]{:S(2)}, u32[]{:S(2)}) collective-permute-start(bf16[192,192]{1,0:T(8,128)(2,1)} %convert_element_type.71), channel_id=1, source_target_pairs={{0,2},{1,3},{2,0},{3,1},{4,6},{5,7},{6,4},{7,5},{8,10},{9,11},{10,... | collective-permute-start | bytes 221192 | tf_op jit(solution)/shard_map/ppermute | solution.py:17
  12.0 5.9 %collective-permute-done.3 = bf16[192,192]{1,0:T(8,128)(2,1)} collective-permute-done((bf16[192,192]{1,0:T(8,128)(2,1)}, bf16[192,192]{1,0:T(8,128)(2,1)}, u32[]{:S(2)}, u32[]{:S(2)}) %collective-permute-start.3) | collective-permute-done | bytes 73760 | tf_op jit(solution)/shard_map/ppermute | solution.py:17
  19.0 6.7 %maximum_maximum_fusion.2 = (bf16[864,768]{1,0:T(8,128)(2,1)}, bf16[864,768]{1,0:T(8,128)(2,1)}) fusion(bf16[96,384]{1,0:T(8,128)(2,1)S(1)} %get-tuple-element.118, bf16[96,384]{1,0:T(8,128)(2,1)S(1)} %get-tuple-element.116, bf16[192,192]{1,0:T(8,128)(2,1)S(1)} %get-tuple-element.113, bf16[192,192]{1,0:T(8,128)(2,1)S(1)} %get-tuple-element.114, ...), kind=kLoop, calls=%fused_computation.2 | loop fusion | flops 12607488 | bytes 4128768 | tf_op jit(solution)/shard_map/concatenate | solution.py:538
  37.3 2.9 %begin.5.begun = f32[6,192,768]{2,1,0:T(8,128)S(1)} custom-call(bf16[2,192,192]{2,1,0:T(8,128)(2,1)S(1)} %copy-done.7, bf16[6,192,768]{2,1,0:T(8,128)(2,1)} %slice.103.own, bf16[6,192,768]{2,1,0:T(8,128)(2,1)} %collective-permute-done.6.near), custom_call_target="tpu_custom_call" | custom-call | flops 1000 | bytes 1000 | tf_op jit(solution)/shard_map/begin/pallas_call | solution.py:29
  40.2 3.7 %begin.3.begun = f32[9,192,768]{2,1,0:T(8,128)S(1)} custom-call(bf16[4,192,192]{2,1,0:T(8,128)(2,1)S(1)} %copy-done.4, bf16[9,192,768]{2,1,0:T(8,128)(2,1)S(1)} %copy-done.1, bf16[9,192,768]{2,1,0:T(8,128)(2,1)} %collective-permute-done.near.refs_15_), custom_call_target="tpu_custom_call" | custom-call | flops 1000 | bytes 1000 | tf_op jit(solution)/shard_map/begin/pallas_call | solution.py:29
  43.9 18.3 %collective-permute-done.1.refs_0_.refs_16_ = bf16[9,192,768]{2,1,0:T(8,128)(2,1)} collective-permute-done((bf16[9,192,768]{2,1,0:T(8,128)(2,1)}, bf16[9,192,768]{2,1,0:T(8,128)(2,1)}, u32[]{:S(2)}, u32[]{:S(2)}) %collective-permute-start.1) | collective-permute-done | bytes 2654240 | tf_op jit(solution)/shard_map/ppermute | solution.py:17
  64.1 3.3 %collective-permute-done.7.fwd.refs_9_ = bf16[9,192,768]{2,1,0:T(8,128)(2,1)S(1)} collective-permute-done((bf16[9,192,768]{2,1,0:T(8,128)(2,1)}, bf16[9,192,768]{2,1,0:T(8,128)(2,1)S(1)}, u32[]{:S(2)}, u32[]{:S(2)}) %collective-permute-start.7) | collective-permute-done | bytes 2654240 | tf_op jit(solution)/shard_map/ppermute | solution.py:17
  67.4 6.8 %absorb.1 = (bf16[9,192,768]{2,1,0:T(8,128)(2,1)S(1)}, f32[384,768]{1,0:T(8,128)S(1)}, bf16[384,768]{1,0:T(8,128)(2,1)S(1)}) custom-call(s32[2]{0:T(128)S(1)} %pad_add_fusion.me, s32[9]{0:T(128)S(1)} %copy-done.8, bf16[4,192,192]{2,1,0:T(8,128)(2,1)S(1)} %copy-done.4, bf16[9,192,768]{2,1,0:T(8,128)(2,1)S(1)} %copy-done, f32[9,192,768]{2,1,0:T(8,128)S(1)} %begin.3.begun, ...), custom_call_target="tpu_custom_call" | custom-call | flops 1000 | bytes 1000 | tf_op jit(solution)/shard_map/absorb/pallas_call | solution.py:148
  76.4 3.9 %collective-permute-start.13 = (bf16[96,768]{1,0:T(8,128)(2,1)S(1)}, bf16[96,768]{1,0:T(8,128)(2,1)S(1)}, u32[]{:S(2)}, u32[]{:S(2)}) collective-permute-start(bf16[96,768]{1,0:T(8,128)(2,1)S(1)} %get-tuple-element.92), channel_id=1, source_target_pairs={{0,3},{1,2},{2,1},{3,0},{4,7},{5,6},{6,5},{7,4},{8,11},{9,10},{10,... | collective-permute-start | bytes 442376 | tf_op jit(solution)/shard_map/ppermute | solution.py:17
  81.0 12.8 %collective-permute-done.10.refs_0_.refs_12_ = bf16[864,768]{1,0:T(8,128)(2,1)S(1)} collective-permute-done((bf16[864,768]{1,0:T(8,128)(2,1)S(1)}, bf16[864,768]{1,0:T(8,128)(2,1)S(1)}, u32[]{:S(2)}, u32[]{:S(2)}) %collective-permute-start.10) | collective-permute-done | bytes 1327136 | tf_op jit(solution)/shard_map/ppermute | solution.py:17
  93.9 1.8 %collective-permute-start.14 = (bf16[96,768]{1,0:T(8,128)(2,1)S(1)}, bf16[96,768]{1,0:T(8,128)(2,1)S(1)}, u32[]{:S(2)}, u32[]{:S(2)}) collective-permute-start(bf16[96,768]{1,0:T(8,128)(2,1)S(1)} %add_convert_fusion.1), channel_id=1, source_target_pairs={{0,8},{4,12},{8,0},{12,4},{1,9},{5,13},{9,1},{13,5},{2,10},{6,14},... | collective-permute-start | bytes 442376 | tf_op jit(solution)/shard_map/ppermute | solution.py:17
  95.7 3.8 %collective-permute-done.14 = bf16[96,768]{1,0:T(8,128)(2,1)S(1)} collective-permute-done((bf16[96,768]{1,0:T(8,128)(2,1)S(1)}, bf16[96,768]{1,0:T(8,128)(2,1)S(1)}, u32[]{:S(2)}, u32[]{:S(2)}) %collective-permute-start.14) | collective-permute-done | bytes 147488 | tf_op jit(solution)/shard_map/ppermute | solution.py:17
  101.4 3.6 %collective-permute-start.17 = (bf16[96,768]{1,0:T(8,128)(2,1)S(1)}, bf16[96,768]{1,0:T(8,128)(2,1)S(1)}, u32[]{:S(2)}, u32[]{:S(2)}) collective-permute-start(bf16[96,768]{1,0:T(8,128)(2,1)S(1)} %add_convert_fusion.refs_0_), channel_id=1, source_target_pairs={{0,3},{1,2},{2,1},{3,0},{4,7},{5,6},{6,5},{7,4},{8,11},{9,10},{10,... | collective-permute-start | bytes 442376 | tf_op jit(solution)/shard_map/ppermute | solution.py:17
  106.9 3.1 %collective-permute-done.17.refs_3_ = bf16[96,768]{1,0:T(8,128)(2,1)S(1)} collective-permute-done((bf16[96,768]{1,0:T(8,128)(2,1)S(1)}, bf16[96,768]{1,0:T(8,128)(2,1)S(1)}, u32[]{:S(2)}, u32[]{:S(2)}) %collective-permute-start.17) | collective-permute-done | bytes 147488 | tf_op jit(solution)/shard_map/ppermute | solution.py:17
  110.0 7.8 %collective-permute-done.16.refs_2_ = bf16[96,768]{1,0:T(8,128)(2,1)S(1)} collective-permute-done((bf16[96,768]{1,0:T(8,128)(2,1)S(1)}, bf16[96,768]{1,0:T(8,128)(2,1)S(1)}, u32[]{:S(2)}, u32[]{:S(2)}) %collective-permute-start.16) | collective-permute-done | bytes 147488 | tf_op jit(solution)/shard_map/ppermute | solution.py:17
  119.9 9.1 %gradient.1 = (bf16[768,768]{1,0:T(8,128)(2,1)S(1)}, f32[192,192]{1,0:T(8,128)}, bf16[4,192,192]{2,1,0:T(8,128)(2,1)S(1)}) custom-call(s32[2]{0:T(128)S(1)} %pad_add_fusion.me, s32[9]{0:T(128)S(1)} %copy-done.8, bf16[96,768]{1,0:T(8,128)(2,1)S(1)} %add_convert_fusion.refs_0_, bf16[96,768]{1,0:T(8,128)(2,1)S(1)} %collective-permute-done.15.refs_1_, ...), custom_call_target="tpu_custom_call" | custom-call | flops 1000 | bytes 26542080 | tf_op jit(solution)/shard_map/gradient/pallas_call | solution.py:148
  129.0 2.5 %collective-permute-start.25 = (bf16[192,192]{1,0:T(8,128)(2,1)S(1)}, bf16[192,192]{1,0:T(8,128)(2,1)S(1)}, u32[]{:S(2)}, u32[]{:S(2)}) collective-permute-start(bf16[192,192]{1,0:T(8,128)(2,1)S(1)} %get-tuple-element.108), channel_id=1, source_target_pairs={{0,3},{1,2},{2,1},{3,0},{4,7},{5,6},{6,5},{7,4},{8,11},{9,10},{10,... | collective-permute-start | bytes 221192 | tf_op jit(solution)/shard_map/ppermute | solution.py:17
  131.5 1.9 %collective-permute-start.23 = (bf16[192,192]{1,0:T(8,128)(2,1)S(1)}, bf16[192,192]{1,0:T(8,128)(2,1)S(1)}, u32[]{:S(2)}, u32[]{:S(2)}) collective-permute-start(bf16[192,192]{1,0:T(8,128)(2,1)S(1)} %get-tuple-element.110), channel_id=1, source_target_pairs={{0,1},{1,0},{2,3},{3,2},{4,5},{5,4},{6,7},{7,6},{8,9},{9,8},{10,11... | collective-permute-start | bytes 221192 | tf_op jit(solution)/shard_map/ppermute | solution.py:17
  133.4 4.2 %proj_gradient.1 = f32[9,192,768]{2,1,0:T(8,128)} custom-call(s32[9]{0:T(128)S(1)} %copy-done.8, bf16[768,768]{1,0:T(8,128)(2,1)S(1)} %get-tuple-element.80.g_ref, bf16[9,192,768]{2,1,0:T(8,128)(2,1)S(1)} %copy-done.6), custom_call_target="tpu_custom_call" | custom-call | flops 1000 | bytes 1000 | tf_op jit(solution)/shard_map/proj_gradient/pallas_call | solution.py:148
  137.6 2.6 %edge_gradient.1._ = f32[9,192,768]{2,1,0:T(8,128)} custom-call(s32[9]{0:T(128)S(1)} %copy-done.8, bf16[768,768]{1,0:T(8,128)(2,1)S(1)} %get-tuple-element.80.g_ref, bf16[3,192,768]{2,1,0:T(8,128)(2,1)S(1)} %mix.1.x_ref), custom_call_target="tpu_custom_call" | custom-call | flops 1000 | bytes 1000 | tf_op jit(solution)/shard_map/edge_gradient/pallas_call | solution.py:148
  141.0 2.1 %add_far.1.begun = f32[6,192,768]{2,1,0:T(8,128)S(1)} custom-call(bf16[2,192,192]{2,1,0:T(8,128)(2,1)S(1)} %pad_maximum_fusion.2.c_ref, f32[6,192,768]{2,1,0:T(8,128)S(1)} %begin.5.begun, bf16[6,192,768]{2,1,0:T(8,128)(2,1)} %collective-permute-done.26.refs_0_), custom_call_target="tpu_custom_call" | custom-call | flops 1000 | bytes 1000 | tf_op jit(solution)/shard_map/add_far/pallas_call | solution.py:29
  143.0 1.8 %collective-permute-done.27.fwd = bf16[6,192,768]{2,1,0:T(8,128)(2,1)S(1)} collective-permute-done((bf16[6,192,768]{2,1,0:T(8,128)(2,1)}, bf16[6,192,768]{2,1,0:T(8,128)(2,1)S(1)}, u32[]{:S(2)}, u32[]{:S(2)}) %collective-permute-start.27) | collective-permute-done | bytes 1769504 | tf_op jit(solution)/shard_map/ppermute | solution.py:17
  144.9 3.9 %late_edge_gradient.1 = f32[9,192,768]{2,1,0:T(8,128)} custom-call(s32[9]{0:T(128)S(1)} %copy-done.8, bf16[768,768]{1,0:T(8,128)(2,1)S(1)} %get-tuple-element.80.g_ref, bf16[192,192]{1,0:T(8,128)(2,1)S(1)} %fusion.3.c_ref, f32[6,192,768]{2,1,0:T(8,128)S(1)} %add_far.1.begun, ...), custom_call_target="tpu_custom_call", output_to_operand_aliasing={{}: (5, {})} | custom-call | flops 1000 | bytes 1000 | tf_op jit(solution)/shard_map/late_edge_gradient/pallas_call | solution.py:148
  (88 shorter events, 30.3 us)
Async XLA Ops:
  0.6 39.5 %collective-permute-start = (bf16[9,192,768]{2,1,0:T(8,128)(2,1)}, bf16[9,192,768]{2,1,0:T(8,128)(2,1)}, u32[]{:S(2)}, u32[]{:S(2)}) collective-permute-start(bf16[9,192,768]{2,1,0:T(8,128)(2,1)} %refs_14_.1), channel_id=1, source_target_pairs={{0,4},{4,0},{8,12},{12,8},{1,5},{5,1},{9,13},{13,9},{2,6},{6,2},{1... | collective-permute-start | bytes 7962632 | tf_op jit(solution)/shard_map/ppermute | solution.py:17
  1.1 61.1 %collective-permute-start.1 = (bf16[9,192,768]{2,1,0:T(8,128)(2,1)}, bf16[9,192,768]{2,1,0:T(8,128)(2,1)}, u32[]{:S(2)}, u32[]{:S(2)}) collective-permute-start(bf16[9,192,768]{2,1,0:T(8,128)(2,1)} %refs_14_.1), channel_id=1, source_target_pairs={{0,8},{4,12},{8,0},{12,4},{1,9},{5,13},{9,1},{13,5},{2,10},{6,14},... | collective-permute-start | bytes 7962632 | tf_op jit(solution)/shard_map/ppermute | solution.py:17
  5.3 6.7 %collective-permute-start.4 = (bf16[192,192]{1,0:T(8,128)(2,1)}, bf16[192,192]{1,0:T(8,128)(2,1)}, u32[]{:S(2)}, u32[]{:S(2)}) collective-permute-start(bf16[192,192]{1,0:T(8,128)(2,1)} %convert_element_type.71), channel_id=1, source_target_pairs={{0,1},{1,0},{2,3},{3,2},{4,5},{5,4},{6,7},{7,6},{8,9},{9,8},{10,11... | collective-permute-start | bytes 221192 | tf_op jit(solution)/shard_map/ppermute | solution.py:17
  6.9 11.0 %collective-permute-start.3 = (bf16[192,192]{1,0:T(8,128)(2,1)}, bf16[192,192]{1,0:T(8,128)(2,1)}, u32[]{:S(2)}, u32[]{:S(2)}) collective-permute-start(bf16[192,192]{1,0:T(8,128)(2,1)} %convert_element_type.71), channel_id=1, source_target_pairs={{0,2},{1,3},{2,0},{3,1},{4,6},{5,7},{6,4},{7,5},{8,10},{9,11},{10,... | collective-permute-start | bytes 221192 | tf_op jit(solution)/shard_map/ppermute | solution.py:17
  9.5 8.4 %collective-permute-start.2 = (bf16[192,192]{1,0:T(8,128)(2,1)}, bf16[192,192]{1,0:T(8,128)(2,1)}, u32[]{:S(2)}, u32[]{:S(2)}) collective-permute-start(bf16[192,192]{1,0:T(8,128)(2,1)} %convert_element_type.71), channel_id=1, source_target_pairs={{0,3},{1,2},{2,1},{3,0},{4,7},{5,6},{6,5},{7,4},{8,11},{9,10},{10,... | collective-permute-start | bytes 221192 | tf_op jit(solution)/shard_map/ppermute | solution.py:17
  25.6 4.1 %collective-permute-start.5 = (bf16[864,768]{1,0:T(8,128)(2,1)}, bf16[864,768]{1,0:T(8,128)(2,1)}, u32[]{:S(2)}, u32[]{:S(2)}) collective-permute-start(bf16[864,768]{1,0:T(8,128)(2,1)} %get-tuple-element.103.refs_10_), channel_id=1, source_target_pairs={{0,4},{4,0},{8,12},{12,8},{1,5},{5,1},{9,13},{13,9},{2,6},{6,2},{1... | collective-permute-start | bytes 3981320 | tf_op jit(solution)/shard_map/ppermute | solution.py:17
  27.0 10.3 %collective-permute-start.6 = (bf16[6,192,768]{2,1,0:T(8,128)(2,1)}, bf16[6,192,768]{2,1,0:T(8,128)(2,1)}, u32[]{:S(2)}, u32[]{:S(2)}) collective-permute-start(bf16[6,192,768]{2,1,0:T(8,128)(2,1)} %slice.103.own), channel_id=1, source_target_pairs={{0,4},{4,0},{8,12},{12,8},{1,5},{5,1},{9,13},{13,9},{2,6},{6,2},{1... | collective-permute-start | bytes 5308424 | tf_op jit(solution)/shard_map/ppermute | solution.py:17
  62.2 5.2 %collective-permute-start.7 = (bf16[9,192,768]{2,1,0:T(8,128)(2,1)}, bf16[9,192,768]{2,1,0:T(8,128)(2,1)S(1)}, u32[]{:S(2)}, u32[]{:S(2)}) collective-permute-start(bf16[9,192,768]{2,1,0:T(8,128)(2,1)} %collective-permute-done.1.refs_0_.refs_16_), channel_id=1, source_target_pairs={{0,4},{4,0},{8,12},{12,8},{1,5},{5,1},{9,13},{13,9},{2,6},{6,2},{1... | collective-permute-start | bytes 7962632 | tf_op jit(solution)/shard_map/ppermute | solution.py:17
  62.2 31.6 %collective-permute-start.10 = (bf16[864,768]{1,0:T(8,128)(2,1)S(1)}, bf16[864,768]{1,0:T(8,128)(2,1)S(1)}, u32[]{:S(2)}, u32[]{:S(2)}) collective-permute-start(bf16[864,768]{1,0:T(8,128)(2,1)S(1)} %copy-done.9), channel_id=1, source_target_pairs={{0,8},{4,12},{8,0},{12,4},{1,9},{5,13},{9,1},{13,5},{2,10},{6,14},... | collective-permute-start | bytes 3981320 | tf_op jit(solution)/shard_map/ppermute | solution.py:17
  74.3 1.6 %collective-permute-start.8 = (bf16[2,96,768]{2,1,0:T(8,128)(2,1)S(1)}, bf16[2,96,768]{2,1,0:T(8,128)(2,1)S(1)}, u32[]{:S(2)}, u32[]{:S(2)}) collective-permute-start(bf16[2,96,768]{2,1,0:T(8,128)(2,1)S(1)} %bitcast.47), channel_id=1, source_target_pairs={{0,4},{4,0},{8,12},{12,8},{1,5},{5,1},{9,13},{13,9},{2,6},{6,2},{1... | collective-permute-start | bytes 884744 | tf_op jit(solution)/shard_map/ppermute | solution.py:17
  74.5 1.9 %collective-permute-start.9 = (bf16[2,96,768]{2,1,0:T(8,128)(2,1)S(1)}, bf16[2,96,768]{2,1,0:T(8,128)(2,1)S(1)}, u32[]{:S(2)}, u32[]{:S(2)}) collective-permute-start(bf16[2,96,768]{2,1,0:T(8,128)(2,1)S(1)} %bitcast.46), channel_id=1, source_target_pairs={{0,4},{4,0},{8,12},{12,8},{1,5},{5,1},{9,13},{13,9},{2,6},{6,2},{1... | collective-permute-start | bytes 884744 | tf_op jit(solution)/shard_map/ppermute | solution.py:17
  76.4 17.3 %collective-permute-start.13 = (bf16[96,768]{1,0:T(8,128)(2,1)S(1)}, bf16[96,768]{1,0:T(8,128)(2,1)S(1)}, u32[]{:S(2)}, u32[]{:S(2)}) collective-permute-start(bf16[96,768]{1,0:T(8,128)(2,1)S(1)} %get-tuple-element.92), channel_id=1, source_target_pairs={{0,3},{1,2},{2,1},{3,0},{4,7},{5,6},{6,5},{7,4},{8,11},{9,10},{10,... | collective-permute-start | bytes 442376 | tf_op jit(solution)/shard_map/ppermute | solution.py:17
  80.3 13.4 %collective-permute-start.12 = (bf16[96,768]{1,0:T(8,128)(2,1)S(1)}, bf16[96,768]{1,0:T(8,128)(2,1)S(1)}, u32[]{:S(2)}, u32[]{:S(2)}) collective-permute-start(bf16[96,768]{1,0:T(8,128)(2,1)S(1)} %get-tuple-element.93), channel_id=1, source_target_pairs={{0,2},{1,3},{2,0},{3,1},{4,6},{5,7},{6,4},{7,5},{8,10},{9,11},{10,... | collective-permute-start | bytes 442376 | tf_op jit(solution)/shard_map/ppermute | solution.py:17
  80.3 13.4 %collective-permute-start.11 = (bf16[96,768]{1,0:T(8,128)(2,1)S(1)}, bf16[96,768]{1,0:T(8,128)(2,1)S(1)}, u32[]{:S(2)}, u32[]{:S(2)}) collective-permute-start(bf16[96,768]{1,0:T(8,128)(2,1)S(1)} %get-tuple-element.105), channel_id=1, source_target_pairs={{0,1},{1,0},{2,3},{3,2},{4,5},{5,4},{6,7},{7,6},{8,9},{9,8},{10,11... | collective-permute-start | bytes 442376 | tf_op jit(solution)/shard_map/ppermute | solution.py:17
  93.9 5.6 %collective-permute-start.14 = (bf16[96,768]{1,0:T(8,128)(2,1)S(1)}, bf16[96,768]{1,0:T(8,128)(2,1)S(1)}, u32[]{:S(2)}, u32[]{:S(2)}) collective-permute-start(bf16[96,768]{1,0:T(8,128)(2,1)S(1)} %add_convert_fusion.1), channel_id=1, source_target_pairs={{0,8},{4,12},{8,0},{12,4},{1,9},{5,13},{9,1},{13,5},{2,10},{6,14},... | collective-permute-start | bytes 442376 | tf_op jit(solution)/shard_map/ppermute | solution.py:17
  99.5 6.5 %collective-permute-start.18 = (bf16[864,768]{1,0:T(8,128)(2,1)S(1)}, bf16[864,768]{1,0:T(8,128)(2,1)S(1)}, u32[]{:S(2)}, u32[]{:S(2)}) collective-permute-start(bf16[864,768]{1,0:T(8,128)(2,1)S(1)} %collective-permute-done.10.refs_0_.refs_12_), channel_id=1, source_target_pairs={{0,4},{4,0},{8,12},{12,8},{1,5},{5,1},{9,13},{13,9},{2,6},{6,2},{1... | collective-permute-start | bytes 3981320 | tf_op jit(solution)/shard_map/ppermute | solution.py:17
  99.6 41.4 %collective-permute-start.26 = (bf16[6,192,768]{2,1,0:T(8,128)(2,1)}, bf16[6,192,768]{2,1,0:T(8,128)(2,1)}, u32[]{:S(2)}, u32[]{:S(2)}) collective-permute-start(bf16[6,192,768]{2,1,0:T(8,128)(2,1)} %slice.103.own), channel_id=1, source_target_pairs={{0,8},{4,12},{8,0},{12,4},{1,9},{5,13},{9,1},{13,5},{2,10},{6,14},... | collective-permute-start | bytes 5308424 | tf_op jit(solution)/shard_map/ppermute | solution.py:17
  101.4 8.6 %collective-permute-start.17 = (bf16[96,768]{1,0:T(8,128)(2,1)S(1)}, bf16[96,768]{1,0:T(8,128)(2,1)S(1)}, u32[]{:S(2)}, u32[]{:S(2)}) collective-permute-start(bf16[96,768]{1,0:T(8,128)(2,1)S(1)} %add_convert_fusion.refs_0_), channel_id=1, source_target_pairs={{0,3},{1,2},{2,1},{3,0},{4,7},{5,6},{6,5},{7,4},{8,11},{9,10},{10,... | collective-permute-start | bytes 442376 | tf_op jit(solution)/shard_map/ppermute | solution.py:17
  105.0 12.8 %collective-permute-start.16 = (bf16[96,768]{1,0:T(8,128)(2,1)S(1)}, bf16[96,768]{1,0:T(8,128)(2,1)S(1)}, u32[]{:S(2)}, u32[]{:S(2)}) collective-permute-start(bf16[96,768]{1,0:T(8,128)(2,1)S(1)} %add_convert_fusion.refs_0_), channel_id=1, source_target_pairs={{0,2},{1,3},{2,0},{3,1},{4,6},{5,7},{6,4},{7,5},{8,10},{9,11},{10,... | collective-permute-start | bytes 442376 | tf_op jit(solution)/shard_map/ppermute | solution.py:17
  105.0 12.8 %collective-permute-start.15 = (bf16[96,768]{1,0:T(8,128)(2,1)S(1)}, bf16[96,768]{1,0:T(8,128)(2,1)S(1)}, u32[]{:S(2)}, u32[]{:S(2)}) collective-permute-start(bf16[96,768]{1,0:T(8,128)(2,1)S(1)} %add_convert_fusion.refs_0_), channel_id=1, source_target_pairs={{0,1},{1,0},{2,3},{3,2},{4,5},{5,4},{6,7},{7,6},{8,9},{9,8},{10,11... | collective-permute-start | bytes 442376 | tf_op jit(solution)/shard_map/ppermute | solution.py:17
  129.0 11.2 %collective-permute-start.25 = (bf16[192,192]{1,0:T(8,128)(2,1)S(1)}, bf16[192,192]{1,0:T(8,128)(2,1)S(1)}, u32[]{:S(2)}, u32[]{:S(2)}) collective-permute-start(bf16[192,192]{1,0:T(8,128)(2,1)S(1)} %get-tuple-element.108), channel_id=1, source_target_pairs={{0,3},{1,2},{2,1},{3,0},{4,7},{5,6},{6,5},{7,4},{8,11},{9,10},{10,... | collective-permute-start | bytes 221192 | tf_op jit(solution)/shard_map/ppermute | solution.py:17
  131.5 8.7 %collective-permute-start.24 = (bf16[192,192]{1,0:T(8,128)(2,1)S(1)}, bf16[192,192]{1,0:T(8,128)(2,1)S(1)}, u32[]{:S(2)}, u32[]{:S(2)}) collective-permute-start(bf16[192,192]{1,0:T(8,128)(2,1)S(1)} %get-tuple-element.109), channel_id=1, source_target_pairs={{0,2},{1,3},{2,0},{3,1},{4,6},{5,7},{6,4},{7,5},{8,10},{9,11},{10,... | collective-permute-start | bytes 221192 | tf_op jit(solution)/shard_map/ppermute | solution.py:17
  131.5 8.7 %collective-permute-start.23 = (bf16[192,192]{1,0:T(8,128)(2,1)S(1)}, bf16[192,192]{1,0:T(8,128)(2,1)S(1)}, u32[]{:S(2)}, u32[]{:S(2)}) collective-permute-start(bf16[192,192]{1,0:T(8,128)(2,1)S(1)} %get-tuple-element.110), channel_id=1, source_target_pairs={{0,1},{1,0},{2,3},{3,2},{4,5},{5,4},{6,7},{7,6},{8,9},{9,8},{10,11... | collective-permute-start | bytes 221192 | tf_op jit(solution)/shard_map/ppermute | solution.py:17
  141.0 3.9 %collective-permute-start.27 = (bf16[6,192,768]{2,1,0:T(8,128)(2,1)}, bf16[6,192,768]{2,1,0:T(8,128)(2,1)S(1)}, u32[]{:S(2)}, u32[]{:S(2)}) collective-permute-start(bf16[6,192,768]{2,1,0:T(8,128)(2,1)} %collective-permute-done.26.refs_0_), channel_id=1, source_target_pairs={{0,4},{4,0},{8,12},{12,8},{1,5},{5,1},{9,13},{13,9},{2,6},{6,2},{1... | collective-permute-start | bytes 5308424 | tf_op jit(solution)/shard_map/ppermute | solution.py:17
  (14 other events, 158.6 us)
